TPU v7x, 32 devices: a whole 2x2x4 slice. The times are simulated.
32 devices in a mesh: groups: 2 (over y), aux: 4 (over z), atoms: 4 (over x, core).
Axes of the slice: x: 2, y: 2, z: 4, core: 2. Of those that a mesh axis runs over, the one named last changes fastest.
Arguments:
- three_center: bfloat16 [2048, 4, 3, 128], P('atoms', 'aux'), may hold values from -0.3125 to 0.3125
- virt_density: bfloat16 [4096, 2048], P(('groups', 'atoms')), parts along dimension 0, may hold values from -6 to 6
- occ_density: bfloat16 [4096, 2048], P('groups', 'atoms'), parts along dimension 0, as said below
- partner_list: int32 [16, 3], replicated, may hold values from 0 to 15, as said below
- partner_count: int32 [16], replicated, may hold values from 1 to 3, 30 in all
Outputs:
- polarizability: float32 [8, 4], P(('groups', 'aux'), 'atoms'), parts along dimension 0
There are 2 independent parts, one for each index of `groups`. A program takes and returns all parts, laid end to end along the dimension named above; an argument that names none is the same for every part. Nothing has to cross between parts.
Inputs may be any that keep to these rules, and one draw needn't show every extreme that they name: occ_density is symmetric. `partner_list`: each row lists 3 different blocks, the first being the row's own block.
All inputs are finite; a program needn't handle non-finite values.
Results may differ from a plain program's by a relative error of at most 0.005.
Values may be sent and summed in bfloat16 or wider, within the bound.
No kernel may reach another device: no remote copies, remote signals or barrier semaphores. Data moves between devices by JAX's collectives and lax.ppermute only.
A program may use at most 64 MiB of HBM per device.

v0:
```python
import jax
import jax.numpy as jnp
from jax import lax
from jax.sharding import PartitionSpec as P

BS = 128
KN = 3


def on_device(three_center, virt_density, occ_density, partner_list, partner_count):
    block_total = partner_list.shape[0]
    basis_total = virt_density.shape[1]
    local_rows = three_center.shape[0]
    aux_local = three_center.shape[1]
    blocks_here = local_rows // BS
    first_block = lax.axis_index("atoms") * blocks_here
    own_list = lax.dynamic_slice_in_dim(partner_list, first_block, blocks_here, 0)
    own_count = lax.dynamic_slice_in_dim(partner_count, first_block, blocks_here, 0)
    usable = (jnp.arange(KN)[None, :] < own_count[:, None]).astype(jnp.bfloat16)
    masked = (
        three_center.reshape(blocks_here, BS, aux_local, KN, BS) * usable[:, None, None, :, None]
    )
    full_virt = lax.all_gather(virt_density, "atoms", axis=0, tiled=True)
    picked = jnp.take(full_virt.reshape(block_total, BS, basis_total), own_list, axis=0)
    product = jnp.einsum("brpkn,bknc->brpc", masked, picked, preferred_element_type=jnp.float32)
    product = product.astype(jnp.bfloat16).reshape(local_rows, aux_local, basis_total)
    shard_rows = lax.all_gather(product, "atoms", axis=0, tiled=True)
    count_rows = shard_rows.shape[0]
    occ_part = occ_density
    occ_part = occ_part.reshape(count_rows, blocks_here, BS)
    columns = jnp.take(shard_rows.reshape(count_rows, aux_local, block_total, BS), own_list, axis=2)
    left_side = jnp.einsum(
        "mbr,mpbks->brpks", occ_part, columns, preferred_element_type=jnp.float32
    )
    left_side = left_side.reshape(local_rows, aux_local, KN * BS)
    left_side = left_side.astype(jnp.bfloat16)
    masked_flat = masked.reshape(local_rows, aux_local, KN * BS)
    moved_left, moved_centers = (
        lax.all_to_all(left_side, "aux", split_axis=0, concat_axis=1, tiled=True),
        lax.all_to_all(masked_flat, "aux", split_axis=0, concat_axis=1, tiled=True),
    )
    partial_chi = jnp.einsum(
        "mpe,mqe->pq", moved_left, moved_centers, preferred_element_type=jnp.float32
    )
    partial_chi = partial_chi * jnp.float32(-(basis_total ** (-0.5)))
    row_share = lax.psum_scatter(partial_chi, "aux", scatter_dimension=0, tiled=True)
    polarizability = lax.psum_scatter(row_share, "atoms", scatter_dimension=1, tiled=True)
    return polarizability


def solution(mesh):
    in_specs = (
        P("atoms", "aux", None, None),
        P(("groups", "atoms"), None),
        P("groups", "atoms"),
        P(),
        P(),
    )
    out_specs = P(("groups", "aux"), "atoms")
    return jax.shard_map(
        on_device, mesh=mesh, in_specs=in_specs, out_specs=out_specs, check_vma=False
    )
```

profile of v0, /device:TPU:0, one launch (start us, length us, event | category | flops | bytes accessed | tf_op | source)
XLA Modules:
  0.0 226.7 jit_solution(16192089454439238048)
XLA Ops:
  6.5 0.7 all-gather.3.cloned.1.call-update
  7.3 0.0 all-gather.5.cloned.1.call-start
  7.3 0.8 compare_and_fusion
  8.1 0.1 copy.34
  8.2 0.1 reshape.101
  8.2 0.1 copy.31
  8.4 0.7 dynamic_slice.7
  9.1 1.2 copy.32
  10.4 0.2 broadcast_multiply_fusion
  10.6 59.3 %all-gather.3.cloned.1.call-done = bf16[2048,2048]{1,0:T(8,128)(2,1)} async-done(((bf16[512,2048]{1,0:T(8,128)(2,1)}), bf16[2048,2048]{1,0:T(8,128)(2,1)}) %all-gather.3.cloned.1.call-update) | async-done | bytes 8388624 | tf_op jit(solution)/shard_map/all_gather | solution.py:23
  69.9 7.6 %gather_fusion = bf16[12,128,2048]{2,1,0:T(8,128)(2,1)} fusion(bf16[16,128,2048]{2,1,0:T(8,128)(2,1)} %bitcast.46, s32[1024]{0:T(1024)S(1)} %pad_clamp_fusion), kind=kCustom, calls=%fused_computation | custom fusion | bytes 12582960 | tf_op jit(solution)/shard_map/jit(_take)/gather | solution.py:24
  77.5 5.5 %bitcast_convert_fusion = bf16[4,128,2048]{2,1,0:T(8,128)(2,1)} fusion(bf16[4,3,128,2048]{3,2,1,0:T(8,128)(2,1)} %bitcast.45, pred[4,3]{1,0:T(4,128)(4,1)S(1)} %copy.31, bf16[4,128,3,128]{1,0,3,2:T(4,128)(2,1)S(1)} %broadcast_multiply_fusion), kind=kOutput, calls=%fused_computation.9 | convolution fusion | flops 809500672 | bytes 8781836 | tf_op jit(solution)/shard_map/brpkn,bknc->brpc/dot_general | solution.py:25
  83.0 4.0 %copy.36 = bf16[512,1,2048]{0,2,1:T(8,128)(2,1)} copy(bf16[512,1,2048]{2,0,1:T(8,128)(2,1)} %bitcast.48) | data formatting | bytes 4194304 | tf_op jit(solution)/shard_map/reshape | solution.py:26
  87.1 0.0 all-gather.5.cloned.1.call-update
  87.1 0.2 copy.43
  87.3 0.2 mul.29
  87.5 0.2 mul.31
  87.7 0.1 bitcast_multiply_fusion
  87.7 0.5 broadcast.74
  88.2 0.9 reduce
  89.2 0.2 copy.65
  89.4 0.8 reshape.133
  90.2 4.6 %all-to-all-start.1 = ((bf16[4,2,24576]{2,1,0:T(2,128)(2,1)}), bf16[4,2,24576]{2,1,0:T(2,128)(2,1)S(1)}, u32[]{:S(2)}, u32[]{:S(2)}) async-start(bf16[4,2,24576]{2,1,0:T(2,128)(2,1)} %reshape.133), calls=%async_computation.1 | async-start | bytes 786432 | tf_op jit(solution)/shard_map/all_to_all | solution.py:40
  94.8 2.1 reshape.97
  96.9 48.7 %all-gather.5.cloned.1.call-done = bf16[2048,1,2048]{0,2,1:T(8,128)(2,1)} async-done(((bf16[512,1,2048]{0,2,1:T(8,128)(2,1)}), bf16[2048,1,2048]{0,2,1:T(8,128)(2,1)}) %all-gather.5.cloned.1.call-update) | async-done | bytes 8388624 | tf_op jit(solution)/shard_map/all_gather | solution.py:27
  145.6 12.3 %copy.37 = bf16[2048,16,128]{2,0,1:T(8,128)(2,1)} copy(bf16[2048,16,128]{0,2,1:T(8,128)(2,1)} %bitcast.44) | data formatting | bytes 16777216 | tf_op jit(solution)/shard_map/reshape | solution.py:31
  157.9 7.5 %gather_fusion.1 = bf16[12,2048,128]{2,1,0:T(8,128)(2,1)} fusion(bf16[2048,16,128]{2,0,1:T(8,128)(2,1)} %copy.37, s32[1024]{0:T(1024)S(1)} %pad_clamp_fusion), kind=kCustom, calls=%fused_computation.1 | custom fusion | bytes 12582960 | tf_op jit(solution)/shard_map/jit(_take)/gather | solution.py:31
  165.4 8.8 %copy.38 = bf16[4,3,2048,128]{2,3,1,0:T(8,128)(2,1)} copy(bf16[4,3,2048,128]{3,2,1,0:T(8,128)(2,1)} %bitcast.43) | data formatting | bytes 12582912 | tf_op jit(solution)/shard_map/jit(_take)/gather | solution.py:31
  174.3 4.6 %fusion.17 = bf16[4,128,3,128]{1,3,2,0:T(8,128)(2,1)S(1)} fusion(bf16[2048,4,128,1]{2,1,0,3:T(4,128)(2,1)S(1)} %bitcast.47, bf16[4,3,2048,128]{2,3,1,0:T(8,128)(2,1)} %copy.38, pred[4,3]{1,0:T(4,128)(4,1)S(1)} %copy.31), kind=kOutput, calls=%fused_computation.14 | convolution fusion | flops 808648704 | bytes 8781836 | tf_op jit(solution)/shard_map/mbr,mpbks->brpks/dot_general | solution.py:32
  178.9 0.3 copy.50
  179.2 0.4 reshape.126
  179.7 3.0 %reduce.1 = bf16[512,384]{1,0:T(8,128)(2,1)S(1)} reduce(bf16[512,1,384]{2,1,0:T(2,128)(2,1)S(1)} %reshape.126, bf16[]{:T(256)} %broadcast.74), dimensions={1}, to_apply=%reshape.126.reduce_sub_computation | reduce | bytes 786434 | tf_op jit(solution)/shard_map/convert_element_type | solution.py:36
  182.7 0.8 reshape.135
  183.6 4.6 %all-to-all-start = ((bf16[4,2,24576]{2,1,0:T(2,128)(2,1)}), bf16[4,2,24576]{2,1,0:T(2,128)(2,1)S(1)}, u32[]{:S(2)}, u32[]{:S(2)}) async-start(bf16[4,2,24576]{2,1,0:T(2,128)(2,1)} %reshape.135), calls=%async_computation | async-start | bytes 786432 | tf_op jit(solution)/shard_map/all_to_all | solution.py:39
  188.2 0.6 dynamic-slice
  188.7 0.4 reshape.134
  189.2 0.1 copy.56
  189.2 0.2 copy.52
  189.5 10.8 %all-to-all-done = bf16[4,2,24576]{2,1,0:T(2,128)(2,1)S(1)} async-done(((bf16[4,2,24576]{2,1,0:T(2,128)(2,1)}), bf16[4,2,24576]{2,1,0:T(2,128)(2,1)S(1)}, u32[]{:S(2)}, u32[]{:S(2)}) %all-to-all-start) | async-done | bytes 393248 | tf_op jit(solution)/shard_map/all_to_all | solution.py:39
  200.3 0.4 reshape.136
  200.7 0.1 copy.55
  200.7 0.2 copy.51
  201.0 0.7 fusion.22
  201.7 9.8 %all-reduce = f32[4,4]{1,0:T(4,128)S(1)} all-reduce(f32[4,4]{1,0:T(4,128)S(1)} %fusion.22), channel_id=2, replica_groups=mesh['groups'=2,'aux'=4,'atoms'=4] {'aux'}, use_global_device_ids=true, to_apply=%region_0.1.clone | all-reduce | flops 16 | bytes 128
  211.5 0.6 constant_dynamic-slice_fusion.1
  212.1 0.6 dynamic-slice.2
  212.7 6.0 %all-reduce.1 = f32[1,4]{1,0:T(1,128)S(1)} all-reduce(f32[1,4]{1,0:T(1,128)S(1)} %constant_dynamic-slice_fusion.1), channel_id=3, replica_groups=mesh['groups'=2,'aux'=4,'atoms'=4] {'atoms'}, use_global_device_ids=true, to_apply=%region_1.2.clone | all-reduce | flops 4 | bytes 32
  218.7 1.2 constant_dynamic-slice_fusion
  (14 shorter events, 0.0 us)
Async XLA Ops:
  6.5 63.4 %all-gather.3.cloned.1.call-start = ((), (), s32[]{:S(2)}) async-start(), calls=%async_computation.2 | async-start | bytes 10485760 | tf_op jit(solution)/shard_map/all_gather | solution.py:23
  7.3 138.3 %all-gather.5.cloned.1.call-start = ((), (), s32[]{:S(2)}) async-start(), calls=%async_computation.3 | async-start | bytes 10485760 | tf_op jit(solution)/shard_map/all_gather | solution.py:27
  77.5 9.6 %copy-start.2 = (bf16[512,1,3,128]{3,0,2,1:T(8,128)(2,1)S(1)}, bf16[512,1,3,128]{3,0,2,1:T(8,128)(2,1)}, u32[]{:S(2)}) copy-start(bf16[512,1,3,128]{3,0,2,1:T(8,128)(2,1)} %param.5) | copy-start | bytes 1179652
  83.0 11.8 %copy-start = (bf16[2048,512]{1,0:T(8,128)(2,1)S(1)}, bf16[2048,512]{1,0:T(8,128)(2,1)}, u32[]{:S(2)}) copy-start(bf16[2048,512]{1,0:T(8,128)(2,1)} %param.7) | copy-start | bytes 6291460
  90.2 93.3 %all-to-all-start.1 = ((bf16[4,2,24576]{2,1,0:T(2,128)(2,1)}), bf16[4,2,24576]{2,1,0:T(2,128)(2,1)S(1)}, u32[]{:S(2)}, u32[]{:S(2)}) async-start(bf16[4,2,24576]{2,1,0:T(2,128)(2,1)} %reshape.133), calls=%async_computation.1 | async-start | bytes 786432 | tf_op jit(solution)/shard_map/all_to_all | solution.py:40
  165.4 8.8 %copy-start.1 = (bf16[2048,4,128]{2,1,0:T(4,128)(2,1)S(1)}, bf16[2048,4,128]{2,1,0:T(4,128)(2,1)}, u32[]{:S(2)}) copy-start(bf16[2048,4,128]{2,1,0:T(4,128)(2,1)} %reshape.97) | copy-start | bytes 6291460
  174.3 13.9 %copy-start.4 = (u32[32]{0:T(128)S(1)}, u32[32]{0:T(128)}, u32[]{:S(2)}) copy-start(u32[32]{0:T(128)} %constant.41) | copy-start | bytes 388
  178.9 33.2 %copy-start.3 = (u32[32]{0:T(128)S(1)}, u32[32]{0:T(128)}, u32[]{:S(2)}) copy-start(u32[32]{0:T(128)} %constant.45) | copy-start | bytes 388
  183.6 16.7 %all-to-all-start = ((bf16[4,2,24576]{2,1,0:T(2,128)(2,1)}), bf16[4,2,24576]{2,1,0:T(2,128)(2,1)S(1)}, u32[]{:S(2)}, u32[]{:S(2)}) async-start(bf16[4,2,24576]{2,1,0:T(2,128)(2,1)} %reshape.135), calls=%async_computation | async-start | bytes 786432 | tf_op jit(solution)/shard_map/all_to_all | solution.py:39
Sparse Core Ops, SparseCore 0:
  8.9 60.9 all-gather.2
  87.2 58.3 all-gather.4
where the time goes:
time: 228 us; the launch traced here: 227 us
  waiting for transfers between devices  120 us (53%)
  local copies, waits for them, and re-layouts  52.7 us (23%)
  blocking collectives  15.8 us (7%)
  between operations  13.6 us (6%)
  matrix products  10.8 us (5%)
  starting transfers between devices  9.24 us (4%)
  other arithmetic  5.04 us (2%)
    all_gather x1, waiting for transfers between devices, on_device(): full_virt = lax.all_gather(virt_density, 'atoms', axis=0, tiled=True)  59.3 us
    all_gather x1, waiting for transfers between devices, on_device(): shard_rows = lax.all_gather(product, 'atoms', axis=0, tiled=True)  48.7 us
    gather x2, local copies, waits for them, and re-layouts, on_device(): jnp.take(shard_rows.reshape(count_rows, aux_local, block_total, BS), own_...  16.4 us
    unnamed x2, blocking collectives  15.8 us
    reshape x1, local copies, waits for them, and re-layouts, on_device(): shard_rows.reshape(count_rows, aux_local, block_total, BS)  12.3 us
    all_to_all x1, waiting for transfers between devices, on_device(): lax.all_to_all(left_side, 'aux', split_axis=0, concat_axis=1, tiled=True)  10.8 us
    gather x1, local copies, waits for them, and re-layouts, on_device(): jnp.take(full_virt.reshape(block_total, BS, basis_total), own_list, axis=0)  7.59 us
    unnamed x22, local copies, waits for them, and re-layouts  6.05 us
  transfers between devices with their start and end apart: 4, of which 3 were waited for; matrix products, arithmetic and copies ran while one was open for 21% of the time, Pallas kernels for 0%

commit v1 on v0

v1 whole, which is shorter than its diff:
```python
import functools

import jax
import jax.numpy as jnp
from jax import lax
from jax.experimental import pallas as pl
from jax.experimental.pallas import tpu as pltpu
from jax.sharding import PartitionSpec as P

BS = 128
KN = 3
MIB = 1 << 20


def swap(x, axes, sizes, move):
    perm = []
    total = 1
    for size in sizes:
        total *= size
    for source in range(total):
        coords, rest = [], source
        for size in reversed(sizes):
            coords.append(rest % size)
            rest //= size
        target = 0
        for size, at in zip(sizes, move(*reversed(coords))):
            target = target * size + at
        perm.append((source, target))
    return lax.ppermute(x, axes, perm)


def contract(n_centers, blocks_here, where, plist, pcount, *refs):
    n_refs = 4 + 8 + 1 + n_centers
    v_refs = refs[0:4]
    m_refs = refs[4:12]
    occ_ref = refs[12]
    c_refs = refs[13:n_refs]
    out_ref = refs[n_refs]
    vbuf, mbuf, obuf, cbuf, prod, acc, vsem, msem, osem, csem = refs[n_refs + 1 :]
    rows = v_refs[0].shape[0]
    pairs = vbuf.shape[0]
    n_blocks = plist.shape[0]
    own = where[0]
    parity = where[1]
    plane = where[2]
    aux_at = where[3]

    def shard_of(i):
        return own ^ i

    def needed(pair):
        hit = jnp.int32(0)
        for b in range(blocks_here):
            block = own * blocks_here + b
            for k in range(KN):
                p = plist[block, k]
                use = (k < pcount[block]) & ((p & 1) == parity) & ((p >> 2) == pair)
                hit = hit | use.astype(jnp.int32)
        return hit > 0

    def v_copy(i, pair):
        return pltpu.make_async_copy(
            v_refs[i].at[:, pl.ds(pl.multiple_of(pair * 2 * BS, 2 * BS), 2 * BS)],
            vbuf.at[pair, pl.ds(pl.multiple_of(shard_of(i) * rows, rows), rows)],
            vsem.at[pair, i],
        )

    def m_copies():
        out = []
        for i in range(8):
            if i in (0, 1, 4, 5):
                slot, shard = i // 4, shard_of(i % 2)
            else:
                slot, shard = (plane if i < 4 else 1 - plane), shard_of(2 + i % 2)
            out.append(
                pltpu.make_async_copy(
                    m_refs[i],
                    mbuf.at[slot, pl.ds(pl.multiple_of(shard * rows, rows), rows)],
                    msem.at[i],
                )
            )
        return out

    def c_copies():
        if n_centers == 1:
            return [pltpu.make_async_copy(c_refs[0], cbuf, csem.at[0])]
        slots = [aux_at, aux_at ^ 1, aux_at ^ (2 | plane), aux_at ^ (3 ^ plane)]
        return [pltpu.make_async_copy(c_refs[i], cbuf.at[slots[i]], csem.at[i]) for i in range(4)]

    for copy in m_copies():
        copy.start()
    for pair in range(pairs):

        @pl.when(needed(pair))
        def _():
            for i in range(4):
                v_copy(i, pair).start()

    o_copy = pltpu.make_async_copy(occ_ref, obuf, osem)
    o_copy.start()
    for copy in c_copies():
        copy.start()
    acc[...] = jnp.zeros_like(acc)
    for copy in m_copies():
        copy.wait()

    n_q = cbuf.shape[0]
    o_copy.wait()
    for copy in c_copies():
        copy.wait()

    def one_pair(pair, carry):
        @pl.when(needed(pair))
        def _():
            for i in range(4):
                v_copy(i, pair).wait()

            def one_block(block, carry):
                row = pl.multiple_of(block * BS, BS)

                def emit(depth):
                    left = jnp.concatenate(
                        [mbuf[s, pl.ds(row, BS), : depth * BS] for s in range(2)], axis=0
                    )
                    right = jnp.concatenate(
                        [
                            vbuf[pair, pl.ds(pl.multiple_of(plist[block, k] * BS, BS), BS), :]
                            for k in range(depth)
                        ],
                        axis=0,
                    )
                    res = jnp.dot(left, right, preferred_element_type=jnp.float32).astype(
                        jnp.bfloat16
                    )
                    for s in range(2):
                        for c in range(2):
                            prod[c, pl.ds(row, BS), s * BS : (s + 1) * BS] = res[
                                s * BS : (s + 1) * BS, c * BS : (c + 1) * BS
                            ]

                for depth in range(1, KN + 1):
                    pl.when(pcount[block] == depth)(functools.partial(emit, depth))
                return carry

            lax.fori_loop(0, n_blocks, one_block, 0)

            for b in range(blocks_here):
                block = own * blocks_here + b
                for k in range(KN):
                    p = plist[block, k]

                    @pl.when((k < pcount[block]) & ((p & 1) == parity) & ((p >> 2) == pair))
                    def _(b=b, k=k, p=p):
                        half = (p >> 1) & 1
                        tile = jnp.dot(
                            obuf[b * BS : (b + 1) * BS, :],
                            prod[half],
                            preferred_element_type=jnp.float32,
                        )
                        tile = tile.astype(jnp.bfloat16).astype(jnp.float32)

                        def add(q):
                            center = cbuf[q, b * BS : (b + 1) * BS, k * BS : (k + 1) * BS]
                            center = center.astype(jnp.float32)
                            for s in range(2):
                                term = tile[:, s * BS : (s + 1) * BS] * center
                                acc[s, q] += term.reshape(BS // 8, 8, BS).sum(axis=0)

                        if n_q <= 8:
                            for q in range(n_q):
                                add(q)
                        else:
                            lax.fori_loop(0, n_q, lambda q, c: (add(q), c)[1], 0)

        return carry

    lax.fori_loop(0, pairs, one_pair, 0)
    for s in range(2):
        out_ref[s] = acc[s].sum(axis=1)


def on_device(sizes, three_center, virt_density, occ_density, partner_list, partner_count):
    groups, aux, atoms = sizes
    rows = three_center.shape[0]
    basis_total = virt_density.shape[1]
    blocks_here = rows // BS
    group_at = lax.axis_index("groups")
    aux_at = lax.axis_index("aux")
    atom_at = lax.axis_index("atoms")
    parity = aux_at & 1

    centers = three_center.reshape(rows, KN * BS)
    striped = virt_density.reshape(rows, basis_total // (2 * BS), 2, BS)
    mine = lax.dynamic_index_in_dim(striped, parity, 2, keepdims=False)
    mine = mine.reshape(rows, basis_total // 2)

    core = functools.partial(swap, axes=("atoms",), sizes=(atoms,), move=lambda t: (t ^ 1,))
    across = functools.partial(swap, axes=("atoms",), sizes=(atoms,), move=lambda t: (t ^ 2,))
    plane = functools.partial(swap, axes=("groups",), sizes=(groups,), move=lambda g: (g ^ 1,))
    pair = functools.partial(swap, axes=("aux",), sizes=(aux,), move=lambda a: (a ^ 1,))

    other = pair(centers)
    v_across = across(mine)
    far_a = swap(
        centers, ("groups", "aux", "atoms"), sizes, lambda g, a, t: (g, a ^ g, t ^ 2)
    )
    if aux == 4:
        rest_a = swap(centers, ("groups", "aux"), (groups, aux), lambda g, a: (g, a ^ (2 | g)))
        rest_b = plane(rest_a)
        all_centers = [centers, other, rest_a, rest_b]
    else:
        all_centers = [lax.all_gather(centers, "aux", axis=0)]
    far_b = plane(far_a)
    v_core = core(mine)
    v_both = core(v_across)
    occ_rows = occ_density.T

    m_parts = [centers, core(centers), far_a, core(far_a), other, core(other), far_b, core(far_b)]
    v_parts = [mine, v_core, v_across, v_both]
    where = jnp.stack([atom_at, parity, group_at, aux_at]).astype(jnp.int32)
    n_in = 13 + len(all_centers)
    anywhere = pl.BlockSpec(memory_space=pl.ANY)
    scalars = pl.BlockSpec(memory_space=pltpu.SMEM)
    n_pairs = basis_total // (4 * BS)
    sums = pl.pallas_call(
        functools.partial(contract, len(all_centers), blocks_here),
        out_shape=jax.ShapeDtypeStruct((2, aux, BS), jnp.float32),
        in_specs=[scalars] * 3 + [anywhere] * n_in,
        out_specs=pl.BlockSpec(memory_space=pltpu.VMEM),
        scratch_shapes=[
            pltpu.VMEM((n_pairs, basis_total, 2 * BS), jnp.bfloat16),
            pltpu.VMEM((2, basis_total, KN * BS), jnp.bfloat16),
            pltpu.VMEM((rows, basis_total), jnp.bfloat16),
            pltpu.VMEM((aux, rows, KN * BS), jnp.bfloat16),
            pltpu.VMEM((2, basis_total, 2 * BS), jnp.bfloat16),
            pltpu.VMEM((2, aux, 8, BS), jnp.float32),
            pltpu.SemaphoreType.DMA((n_pairs, 4)),
            pltpu.SemaphoreType.DMA((8,)),
            pltpu.SemaphoreType.DMA,
            pltpu.SemaphoreType.DMA((4,)),
        ],
        compiler_params=pltpu.CompilerParams(vmem_limit_bytes=56 * MIB),
    )(where, partner_list, partner_count, *v_parts, *m_parts, occ_rows, *all_centers)

    total = sums[0] + pair(sums[1])
    total = total + core(total)
    total = total + across(total)
    share = aux // atoms
    row = lax.dynamic_slice_in_dim(total, atom_at * share, share, 0)
    return (row.sum(axis=1) * jnp.float32(-(basis_total ** (-0.5))))[None, :]


def solution(mesh):
    sizes = tuple(mesh.shape[name] for name in ("groups", "aux", "atoms"))
    in_specs = (
        P("atoms", "aux", None, None),
        P(("groups", "atoms"), None),
        P("groups", "atoms"),
        P(),
        P(),
    )
    out_specs = P(("groups", "aux"), "atoms")
    return jax.shard_map(
        functools.partial(on_device, sizes),
        mesh=mesh,
        in_specs=in_specs,
        out_specs=out_specs,
        check_vma=False,
    )
```

time: 228 us -> 98.6 us (0.43)
  waiting for transfers between devices: 120 us -> 42.5 us
  local copies, waits for them, and re-layouts: 52.7 us -> 16.4 us
  Pallas kernels: 0 us -> 18.5 us
  blocking collectives: 15.8 us -> 0 us
  between operations: 13.6 us -> 1.29 us
  matrix products: 10.8 us -> 0 us
  starting transfers between devices: 9.24 us -> 17.8 us
  other arithmetic: 5.04 us -> 1.88 us
    all_gather x2 -> x0, waiting for transfers between devices: 108 us -> none  [the longest x1 59.3 us: on_device(): full_virt = lax.all_gather(virt_density, 'atoms', axis=0, tiled=True)]
    ppermute x0 -> x15, waiting for transfers between devices: none -> 42.5 us  [swap(): return lax.ppermute(x, axes, perm)]
    gather x3 -> x0, local copies, waits for them, and re-layouts: 24 us -> none  [the longest x2 16.4 us: on_device(): jnp.take(shard_rows.reshape(count_rows, aux_local, block_total, BS), own_...]
    pallas_call x0 -> x1, Pallas kernels: none -> 18.5 us  [on_device(): pl.pallas_call(functools.partial(contract, len(all_centers), blocks_here)...]
    ppermute x0 -> x15, starting transfers between devices: none -> 17.8 us  [swap(): return lax.ppermute(x, axes, perm)]
    unnamed x2 -> x0, blocking collectives: 15.8 us -> none
    reshape x4 -> x2, local copies, waits for them, and re-layouts: 19.6 us -> 4.43 us  [the longest x1 3.22 us: on_device(): striped = virt_density.reshape(rows, basis_total // (2 * BS), 2, BS)]
    dot_general x3 -> x0, matrix products: 10.8 us -> none  [the longest x1 5.52 us: on_device(): jnp.einsum('brpkn,bknc->brpc', masked, picked, preferred_element_type=jnp...]
  transfers between devices with their start and end apart: 4 -> 15, of which waited for: 3 -> 6; matrix products, arithmetic and copies ran while one was open for 21% -> 6% of each run, Pallas kernels for 0% -> 0%
where the time goes in v1:
time: 98.6 us; the launch traced here: 98.3 us
  waiting for transfers between devices  42.5 us (43%)
  Pallas kernels  18.5 us (19%)
  starting transfers between devices  17.8 us (18%)
  local copies, waits for them, and re-layouts  16.4 us (17%)
  other arithmetic  1.88 us (2%)
  between operations  1.29 us (1%)
    ppermute x15, waiting for transfers between devices, swap(): return lax.ppermute(x, axes, perm)  42.5 us
    pallas_call x1, Pallas kernels, on_device(): pl.pallas_call(functools.partial(contract, len(all_centers), blocks_here)...  18.5 us
    ppermute x15, starting transfers between devices, swap(): return lax.ppermute(x, axes, perm)  17.8 us
    dynamic_slice x1, local copies, waits for them, and re-layouts, on_device(): mine = lax.dynamic_index_in_dim(striped, parity, 2, keepdims=False)  6.15 us
    unnamed x20, local copies, waits for them, and re-layouts  5.11 us
    reshape x1, local copies, waits for them, and re-layouts, on_device(): striped = virt_density.reshape(rows, basis_total // (2 * BS), 2, BS)  3.22 us
  transfers between devices with their start and end apart: 15, of which 6 were waited for; matrix products, arithmetic and copies ran while one was open for 6% of the time, Pallas kernels for 0%

profile of v1, /device:TPU:0, one launch (start us, length us, event | category | flops | bytes accessed | tf_op | source)
XLA Modules:
  0.0 98.3 jit_solution(17629758959406195039)
XLA Ops:
  0.0 3.2 %reshape.14 = bf16[512,8,2,128]{3,2,1,0:T(2,128)(2,1)S(1)} reshape(bf16[512,2048]{1,0:T(8,128)(2,1)} %param.6) | data formatting | bytes 4194304 | tf_op jit(solution)/shard_map/reshape | solution.py:193
  3.2 0.0 copy-start.6
  3.2 6.2 %dynamic-slice_reduce_fusion = bf16[512,8,128]{2,1,0:T(8,128)(2,1)S(1)} fusion(bf16[512,8,2,128]{3,2,1,0:T(2,128)(2,1)S(1)} %reshape.14, s32[]{:T(128)S(6)} %select_n.7), kind=kLoop, calls=%fused_computation | loop fusion | bytes 2097156 | tf_op jit(solution)/shard_map/jit(dynamic_index_in_dim)/dynamic_slice | solution.py:194
  9.4 0.0 copy-start.7
  9.4 0.0 copy-start.2
  9.4 0.3 copy.23
  9.7 3.0 %collective-permute-start.1 = (bf16[512,1024]{1,0:T(8,128)(2,1)S(1)}, bf16[512,1024]{1,0:T(8,128)(2,1)}, u32[]{:S(2)}, u32[]{:S(2)}) collective-permute-start(bf16[512,1024]{1,0:T(8,128)(2,1)S(1)} %bitcast.18), channel_id=1, source_target_pairs={{0,2},{1,3},{2,0},{3,1},{4,6},{5,7},{6,4},{7,5},{8,10},{9,11},{10,... | collective-permute-start | bytes 3145736 | tf_op jit(solution)/shard_map/ppermute | solution.py:29
  12.7 0.9 copy.11
  13.7 1.2 %copy.18.refs_4_.refs_13_ = bf16[512,384]{1,0:T(8,128)(2,1)S(1)} copy(bf16[512,384]{0,1:T(8,128)(2,1)} %bitcast.22) | data formatting | bytes 786432 | tf_op jit(solution)/shard_map/reshape | solution.py:192
  14.9 2.7 %collective-permute-start.10 = (bf16[512,384]{1,0:T(8,128)(2,1)S(1)}, bf16[512,384]{1,0:T(8,128)(2,1)S(1)}, u32[]{:S(2)}, u32[]{:S(2)}) collective-permute-start(bf16[512,384]{1,0:T(8,128)(2,1)S(1)} %copy.18.refs_4_.refs_13_), channel_id=1, source_target_pairs={{0,8},{4,12},{8,0},{12,4},{16,28},{20,24},{24,20},{28,16},{1,9},{5... | collective-permute-start | bytes 1179656 | tf_op jit(solution)/shard_map/ppermute | solution.py:29
  17.5 1.6 %collective-permute-start.6 = (bf16[512,384]{1,0:T(8,128)(2,1)S(1)}, bf16[512,384]{1,0:T(8,128)(2,1)}, u32[]{:S(2)}, u32[]{:S(2)}) collective-permute-start(bf16[512,384]{1,0:T(8,128)(2,1)S(1)} %copy.18.refs_4_.refs_13_), channel_id=1, source_target_pairs={{0,4},{4,0},{8,12},{12,8},{1,5},{5,1},{9,13},{13,9},{2,6},{6,2},{1... | collective-permute-start | bytes 1179656 | tf_op jit(solution)/shard_map/ppermute | solution.py:29
  19.1 0.5 collective-permute-start.4
  19.6 0.0 collective-permute-start
  19.6 17.2 %collective-permute-done.1.refs_2_ = bf16[512,1024]{1,0:T(8,128)(2,1)} collective-permute-done((bf16[512,1024]{1,0:T(8,128)(2,1)S(1)}, bf16[512,1024]{1,0:T(8,128)(2,1)}, u32[]{:S(2)}, u32[]{:S(2)}) %collective-permute-start.1) | collective-permute-done | bytes 1048608 | tf_op jit(solution)/shard_map/ppermute | solution.py:29
  36.8 0.0 collective-permute-start.2
  36.8 0.0 collective-permute-done.10.refs_15_
  36.8 0.5 collective-permute-start.3
  37.3 0.0 collective-permute-done.6.refs_8_.refs_14_
  37.3 9.4 %collective-permute-start.11 = (bf16[512,384]{1,0:T(8,128)(2,1)S(1)}, bf16[512,384]{1,0:T(8,128)(2,1)S(1)}, u32[]{:S(2)}, u32[]{:S(2)}) collective-permute-start(bf16[512,384]{1,0:T(8,128)(2,1)S(1)} %collective-permute-done.10.refs_15_), channel_id=1, source_target_pairs={{0,16},{16,0},{1,17},{17,1},{2,18},{18,2},{3,19},{19,3},{4,20},{20... | collective-permute-start | bytes 1179656 | tf_op jit(solution)/shard_map/ppermute | solution.py:29
  46.7 0.0 collective-permute-done.4.refs_6_
  46.7 0.1 collective-permute-start.8
  46.8 0.0 collective-permute-done.3.refs_5_
  46.8 0.0 copy-done.3
  46.8 0.1 collective-permute-start.7
  46.9 9.8 %collective-permute-done.11.refs_16_ = bf16[512,384]{1,0:T(8,128)(2,1)S(1)} collective-permute-done((bf16[512,384]{1,0:T(8,128)(2,1)S(1)}, bf16[512,384]{1,0:T(8,128)(2,1)S(1)}, u32[]{:S(2)}, u32[]{:S(2)}) %collective-permute-start.11) | collective-permute-done | bytes 393248 | tf_op jit(solution)/shard_map/ppermute | solution.py:29
  56.6 0.0 collective-permute-start.5
  56.6 0.7 copy-done.5
  57.4 7.2 %collective-permute-done.8.refs_10_ = bf16[512,384]{1,0:T(8,128)(2,1)} collective-permute-done((bf16[512,384]{1,0:T(8,128)(2,1)}, bf16[512,384]{1,0:T(8,128)(2,1)}, u32[]{:S(2)}, u32[]{:S(2)}) %collective-permute-start.8) | collective-permute-done | bytes 393248 | tf_op jit(solution)/shard_map/ppermute | solution.py:29
  64.6 0.0 collective-permute-start.9
  64.6 0.7 copy.17.plist
  65.3 2.5 %copy.15 = bf16[2048,512]{0,1:T(8,128)(2,1)} copy(bf16[2048,512]{1,0:T(8,128)(2,1)S(1)} %copy-done.2) | data formatting | bytes 4194304 | tf_op args[2]
  67.7 0.0 copy-done.1
  67.7 0.6 pad_add_fusion.where
  68.3 0.0 collective-permute-done.7.refs_9_
  68.3 0.0 collective-permute-done.5.refs_7_
  68.3 0.0 collective-permute-done.refs_1_
  68.3 0.0 collective-permute-done.9.refs_11_
  68.3 0.0 collective-permute-done.2.refs_3_
  68.4 18.5 %shard_map.55 = f32[2,4,128]{2,1,0:T(4,128)} custom-call(s32[4]{0:T(128)} %pad_add_fusion.where, s32[16,3]{1,0:T(8,128)} %copy.17.plist, s32[16]{0:T(128)} %pcount.1, bf16[512,1024]{1,0:T(8,128)(2,1)} %bitcast.20, bf16[512,1024]{1,0:T(8,128)(2,1)} %collective-permute-done.refs_1_, bf16[512,1024]{1,0:T(8,128)(2,1)} %collective-permute-done.1.refs_2_, ...), custom_call_target="tpu_custom_call" | custom-call | tf_op jit(solution)/shard_map/pallas_call | solution.py:225
  86.8 0.7 slice_bitcast_fusion
  87.5 0.0 collective-permute-start.12
  87.5 3.6 %collective-permute-done.12 = f32[4,128]{1,0:T(4,128)S(1)} collective-permute-done((f32[4,128]{1,0:T(4,128)S(1)}, f32[4,128]{1,0:T(4,128)S(1)}, u32[]{:S(2)}, u32[]{:S(2)}) %collective-permute-start.12) | collective-permute-done | bytes 2080 | tf_op jit(solution)/shard_map/ppermute | solution.py:29
  91.1 0.7 fusion
  91.8 0.0 collective-permute-start.13
  91.8 1.2 %collective-permute-done.13 = f32[4,128]{1,0:T(4,128)S(1)} collective-permute-done((f32[4,128]{1,0:T(4,128)S(1)}, f32[4,128]{1,0:T(4,128)S(1)}, u32[]{:S(2)}, u32[]{:S(2)}) %collective-permute-start.13) | collective-permute-done | bytes 2080 | tf_op jit(solution)/shard_map/ppermute | solution.py:29
  92.9 0.0 collective-permute-start.14
  92.9 3.6 %collective-permute-done.14 = f32[4,128]{1,0:T(4,128)S(1)} collective-permute-done((f32[4,128]{1,0:T(4,128)S(1)}, f32[4,128]{1,0:T(4,128)S(1)}, u32[]{:S(2)}, u32[]{:S(2)}) %collective-permute-start.14) | collective-permute-done | bytes 2080 | tf_op jit(solution)/shard_map/ppermute | solution.py:29
  96.5 0.6 dynamic-slice_reduce_fusion.1
  (12 shorter events, 0.0 us)
Async XLA Ops:
  3.2 9.5 %copy-start.6 = (bf16[512,1,3,128]{3,0,2,1:T(8,128)(2,1)S(1)}, bf16[512,1,3,128]{3,0,2,1:T(8,128)(2,1)}, u32[]{:S(2)}) copy-start(bf16[512,1,3,128]{3,0,2,1:T(8,128)(2,1)} %param.5) | copy-start | bytes 1179652
  9.4 55.2 %copy-start.7 = (s32[16,3]{0,1:T(4,128)S(1)}, s32[16,3]{0,1:T(4,128)}, u32[]{:S(2)}) copy-start(s32[16,3]{0,1:T(4,128)} %param.8) | copy-start | bytes 580
  9.4 55.8 %copy-start.2 = (bf16[2048,512]{1,0:T(8,128)(2,1)S(1)}, bf16[2048,512]{1,0:T(8,128)(2,1)}, u32[]{:S(2)}) copy-start(bf16[2048,512]{1,0:T(8,128)(2,1)} %param.7) | copy-start | bytes 6291460
  9.7 58.0 %copy-start = (bf16[64,8,8,128]{3,1,2,0:T(8,128)(2,1)}, bf16[64,8,8,128]{3,1,2,0:T(8,128)(2,1)S(1)}, u32[]{:S(2)}) copy-start(bf16[64,8,8,128]{3,1,2,0:T(8,128)(2,1)S(1)} %copy.23) | copy-start | bytes 3145732
  9.7 27.1 %collective-permute-start.1 = (bf16[512,1024]{1,0:T(8,128)(2,1)S(1)}, bf16[512,1024]{1,0:T(8,128)(2,1)}, u32[]{:S(2)}, u32[]{:S(2)}) collective-permute-start(bf16[512,1024]{1,0:T(8,128)(2,1)S(1)} %bitcast.18), channel_id=1, source_target_pairs={{0,2},{1,3},{2,0},{3,1},{4,6},{5,7},{6,4},{7,5},{8,10},{9,11},{10,... | collective-permute-start | bytes 3145736 | tf_op jit(solution)/shard_map/ppermute | solution.py:29
  14.9 52.9 %copy-start.1 = (bf16[512,384]{1,0:T(8,128)(2,1)}, bf16[512,384]{1,0:T(8,128)(2,1)S(1)}, u32[]{:S(2)}) copy-start(bf16[512,384]{1,0:T(8,128)(2,1)S(1)} %copy.18.refs_4_.refs_13_) | copy-start | bytes 1179652
  14.9 21.9 %collective-permute-start.10 = (bf16[512,384]{1,0:T(8,128)(2,1)S(1)}, bf16[512,384]{1,0:T(8,128)(2,1)S(1)}, u32[]{:S(2)}, u32[]{:S(2)}) collective-permute-start(bf16[512,384]{1,0:T(8,128)(2,1)S(1)} %copy.18.refs_4_.refs_13_), channel_id=1, source_target_pairs={{0,8},{4,12},{8,0},{12,4},{16,28},{20,24},{24,20},{28,16},{1,9},{5... | collective-permute-start | bytes 1179656 | tf_op jit(solution)/shard_map/ppermute | solution.py:29
  17.5 19.8 %collective-permute-start.6 = (bf16[512,384]{1,0:T(8,128)(2,1)S(1)}, bf16[512,384]{1,0:T(8,128)(2,1)}, u32[]{:S(2)}, u32[]{:S(2)}) collective-permute-start(bf16[512,384]{1,0:T(8,128)(2,1)S(1)} %copy.18.refs_4_.refs_13_), channel_id=1, source_target_pairs={{0,4},{4,0},{8,12},{12,8},{1,5},{5,1},{9,13},{13,9},{2,6},{6,2},{1... | collective-permute-start | bytes 1179656 | tf_op jit(solution)/shard_map/ppermute | solution.py:29
  19.1 27.6 %collective-permute-start.4 = (bf16[512,384]{1,0:T(8,128)(2,1)S(1)}, bf16[512,384]{1,0:T(8,128)(2,1)}, u32[]{:S(2)}, u32[]{:S(2)}) collective-permute-start(bf16[512,384]{1,0:T(8,128)(2,1)S(1)} %copy.18.refs_4_.refs_13_), channel_id=1, source_target_pairs={{0,2},{1,3},{2,0},{3,1},{4,6},{5,7},{6,4},{7,5},{8,10},{9,11},{10,... | collective-permute-start | bytes 1179656 | tf_op jit(solution)/shard_map/ppermute | solution.py:29
  19.6 48.7 %collective-permute-start = (bf16[512,1024]{1,0:T(8,128)(2,1)S(1)}, bf16[512,1024]{1,0:T(8,128)(2,1)}, u32[]{:S(2)}, u32[]{:S(2)}) collective-permute-start(bf16[512,1024]{1,0:T(8,128)(2,1)S(1)} %bitcast.19), channel_id=1, source_target_pairs={{0,1},{1,0},{2,3},{3,2},{4,5},{5,4},{6,7},{7,6},{8,9},{9,8},{10,11... | collective-permute-start | bytes 3145736 | tf_op jit(solution)/shard_map/ppermute | solution.py:29
  36.8 31.5 %collective-permute-start.2 = (bf16[512,1024]{1,0:T(8,128)(2,1)}, bf16[512,1024]{1,0:T(8,128)(2,1)}, u32[]{:S(2)}, u32[]{:S(2)}) collective-permute-start(bf16[512,1024]{1,0:T(8,128)(2,1)} %collective-permute-done.1.refs_2_), channel_id=1, source_target_pairs={{0,1},{1,0},{2,3},{3,2},{4,5},{5,4},{6,7},{7,6},{8,9},{9,8},{10,11... | collective-permute-start | bytes 3145736 | tf_op jit(solution)/shard_map/ppermute | solution.py:29
  36.8 10.0 %copy-start.3 = (bf16[512,384]{1,0:T(8,128)(2,1)}, bf16[512,384]{1,0:T(8,128)(2,1)S(1)}, u32[]{:S(2)}) copy-start(bf16[512,384]{1,0:T(8,128)(2,1)S(1)} %collective-permute-done.10.refs_15_) | copy-start | bytes 1179652
  36.8 10.0 %collective-permute-start.3 = (bf16[512,384]{1,0:T(8,128)(2,1)S(1)}, bf16[512,384]{1,0:T(8,128)(2,1)S(1)}, u32[]{:S(2)}, u32[]{:S(2)}) collective-permute-start(bf16[512,384]{1,0:T(8,128)(2,1)S(1)} %copy.18.refs_4_.refs_13_), channel_id=1, source_target_pairs={{0,1},{1,0},{2,3},{3,2},{4,5},{5,4},{6,7},{7,6},{8,9},{9,8},{10,11... | collective-permute-start | bytes 1179656 | tf_op jit(solution)/shard_map/ppermute | solution.py:29
  37.3 19.3 %collective-permute-start.11 = (bf16[512,384]{1,0:T(8,128)(2,1)S(1)}, bf16[512,384]{1,0:T(8,128)(2,1)S(1)}, u32[]{:S(2)}, u32[]{:S(2)}) collective-permute-start(bf16[512,384]{1,0:T(8,128)(2,1)S(1)} %collective-permute-done.10.refs_15_), channel_id=1, source_target_pairs={{0,16},{16,0},{1,17},{17,1},{2,18},{18,2},{3,19},{19,3},{4,20},{20... | collective-permute-start | bytes 1179656 | tf_op jit(solution)/shard_map/ppermute | solution.py:29
  46.7 17.9 %collective-permute-start.8 = (bf16[512,384]{1,0:T(8,128)(2,1)}, bf16[512,384]{1,0:T(8,128)(2,1)}, u32[]{:S(2)}, u32[]{:S(2)}) collective-permute-start(bf16[512,384]{1,0:T(8,128)(2,1)} %collective-permute-done.4.refs_6_), channel_id=1, source_target_pairs={{0,16},{16,0},{1,17},{17,1},{2,18},{18,2},{3,19},{19,3},{4,20},{20... | collective-permute-start | bytes 1179656 | tf_op jit(solution)/shard_map/ppermute | solution.py:29
  46.8 9.8 %copy-start.4 = (bf16[512,384]{1,0:T(8,128)(2,1)}, bf16[512,384]{1,0:T(8,128)(2,1)S(1)}, u32[]{:S(2)}) copy-start(bf16[512,384]{1,0:T(8,128)(2,1)S(1)} %collective-permute-done.3.refs_5_) | copy-start | bytes 1179652
  46.8 21.5 %collective-permute-start.7 = (bf16[512,384]{1,0:T(8,128)(2,1)}, bf16[512,384]{1,0:T(8,128)(2,1)}, u32[]{:S(2)}, u32[]{:S(2)}) collective-permute-start(bf16[512,384]{1,0:T(8,128)(2,1)} %collective-permute-done.6.refs_8_.refs_14_), channel_id=1, source_target_pairs={{0,1},{1,0},{2,3},{3,2},{4,5},{5,4},{6,7},{7,6},{8,9},{9,8},{10,11... | collective-permute-start | bytes 1179656 | tf_op jit(solution)/shard_map/ppermute | solution.py:29
  56.6 0.7 copy-start.5
  56.6 11.7 %collective-permute-start.5 = (bf16[512,384]{1,0:T(8,128)(2,1)}, bf16[512,384]{1,0:T(8,128)(2,1)}, u32[]{:S(2)}, u32[]{:S(2)}) collective-permute-start(bf16[512,384]{1,0:T(8,128)(2,1)} %collective-permute-done.4.refs_6_), channel_id=1, source_target_pairs={{0,1},{1,0},{2,3},{3,2},{4,5},{5,4},{6,7},{7,6},{8,9},{9,8},{10,11... | collective-permute-start | bytes 1179656 | tf_op jit(solution)/shard_map/ppermute | solution.py:29
  64.6 3.8 %collective-permute-start.9 = (bf16[512,384]{1,0:T(8,128)(2,1)}, bf16[512,384]{1,0:T(8,128)(2,1)}, u32[]{:S(2)}, u32[]{:S(2)}) collective-permute-start(bf16[512,384]{1,0:T(8,128)(2,1)} %collective-permute-done.8.refs_10_), channel_id=1, source_target_pairs={{0,1},{1,0},{2,3},{3,2},{4,5},{5,4},{6,7},{7,6},{8,9},{9,8},{10,11... | collective-permute-start | bytes 1179656 | tf_op jit(solution)/shard_map/ppermute | solution.py:29
  87.5 3.6 %collective-permute-start.12 = (f32[4,128]{1,0:T(4,128)S(1)}, f32[4,128]{1,0:T(4,128)S(1)}, u32[]{:S(2)}, u32[]{:S(2)}) collective-permute-start(f32[4,128]{1,0:T(4,128)S(1)} %slice_bitcast_fusion), channel_id=1, source_target_pairs={{0,4},{4,0},{8,12},{12,8},{1,5},{5,1},{9,13},{13,9},{2,6},{6,2},{1... | collective-permute-start | bytes 6152 | tf_op jit(solution)/shard_map/ppermute | solution.py:29
  91.8 1.2 %collective-permute-start.13 = (f32[4,128]{1,0:T(4,128)S(1)}, f32[4,128]{1,0:T(4,128)S(1)}, u32[]{:S(2)}, u32[]{:S(2)}) collective-permute-start(f32[4,128]{1,0:T(4,128)S(1)} %fusion), channel_id=1, source_target_pairs={{0,1},{1,0},{2,3},{3,2},{4,5},{5,4},{6,7},{7,6},{8,9},{9,8},{10,11... | collective-permute-start | bytes 6152 | tf_op jit(solution)/shard_map/ppermute | solution.py:29
  92.9 3.6 %collective-permute-start.14 = (f32[4,128]{1,0:T(4,128)S(1)}, f32[4,128]{1,0:T(4,128)S(1)}, u32[]{:S(2)}, u32[]{:S(2)}) collective-permute-start(f32[4,128]{1,0:T(4,128)S(1)} %add.18), channel_id=1, source_target_pairs={{0,2},{1,3},{2,0},{3,1},{4,6},{5,7},{6,4},{7,5},{8,10},{9,11},{10,... | collective-permute-start | bytes 6152 | tf_op jit(solution)/shard_map/ppermute | solution.py:29

commit v2 on v0

v2 whole, which is shorter than its diff:
```python
import functools

import jax
import jax.numpy as jnp
from jax import lax
from jax.experimental import pallas as pl
from jax.experimental.pallas import tpu as pltpu
from jax.sharding import PartitionSpec as P

BS = 128
KN = 3
MIB = 1 << 20


def swap(x, axes, sizes, move):
    perm = []
    total = 1
    for size in sizes:
        total *= size
    for source in range(total):
        coords, rest = [], source
        for size in reversed(sizes):
            coords.append(rest % size)
            rest //= size
        target = 0
        for size, at in zip(sizes, move(*reversed(coords))):
            target = target * size + at
        perm.append((source, target))
    return lax.ppermute(x, axes, perm)


def select(blocks_half, where, virt_ref, near_ref, far_ref, buf, sem):
    parity, half = where[1], where[0] >> 1

    def copy(i):
        at = half if i < blocks_half else 1 - half
        block = 2 * (at * blocks_half + i % blocks_half) + parity
        columns = pl.ds(pl.multiple_of(block * BS, BS), BS)
        return pltpu.make_async_copy(virt_ref.at[:, columns], buf.at[i], sem.at[i])

    order = list(range(blocks_half, 2 * blocks_half)) + list(range(blocks_half))
    for i in order:
        copy(i).start()
    for i in order:
        copy(i).wait()
        out_ref = near_ref if i < blocks_half else far_ref
        row = i % blocks_half * BS
        out_ref[row : row + BS, :] = buf[i].T


def contract(n_centers, far_half, where, plist, pcount, *refs):
    v_refs, m_refs, occ_ref = refs[0:4], refs[4:12], refs[12]
    c_refs = refs[13 : 13 + n_centers]
    out_ref, vbuf, prod, acc, vsem = refs[13 + n_centers :]
    own, parity, plane, aux_at = where[0], where[1], where[2], where[3]
    half = 1 - (own >> 1) if far_half else own >> 1
    columns, rows = v_refs[0].shape
    blocks_here = rows // BS
    n_q = acc.shape[1]

    def used(b, k):
        block = own * blocks_here + b
        p = plist[block, k]
        return (k < pcount[block]) & ((p & 1) == parity) & ((p >> 3) == half)

    any_used = jnp.int32(0)
    for b in range(blocks_here):
        for k in range(KN):
            any_used = any_used | used(b, k).astype(jnp.int32)
    acc[...] = jnp.zeros_like(acc)

    @pl.when(any_used > 0)
    def _():
        copies = [pltpu.make_async_copy(v_refs[i], vbuf.at[own ^ i], vsem.at[i]) for i in range(4)]
        for copy in copies:
            copy.start()
        for copy in copies:
            copy.wait()

        for i in range(4):
            first = (own ^ i) * blocks_here
            mine, others = m_refs[i], m_refs[4 + i]
            slot = 0 if i < 2 else plane

            def one_block(j, carry, first=first, mine=mine, others=others, slot=slot):
                block = first + j
                row = pl.ds(pl.multiple_of(j * BS, BS), BS)
                column = pl.ds(pl.multiple_of(block * BS, BS), BS)

                def emit(depth):
                    weights = jnp.concatenate(
                        [
                            jnp.concatenate([m[k, row, :] for k in range(depth)], axis=1)
                            for m in (mine, others)
                        ],
                        axis=0,
                    )
                    parts = []
                    for k in range(depth):
                        p = plist[block, k]
                        at = pl.ds(pl.multiple_of(lax.rem(p, blocks_here) * BS, BS), BS)
                        parts.append(vbuf[p // blocks_here, :, at])
                    res = lax.dot_general(
                        jnp.concatenate(parts, axis=1),
                        weights,
                        (((1,), (1,)), ((), ())),
                        preferred_element_type=jnp.float32,
                    ).astype(jnp.bfloat16)
                    prod[slot, :, column] = res[:, :BS]
                    prod[1 - slot, :, column] = res[:, BS:]

                for depth in range(1, KN + 1):
                    pl.when(pcount[block] == depth)(functools.partial(emit, depth))
                return carry

            lax.fori_loop(0, blocks_here, one_block, 0)

        for b in range(blocks_here):
            for k in range(KN):
                p = plist[own * blocks_here + b, k]

                @pl.when(used(b, k))
                def _(b=b, k=k, p=p):
                    at = pl.ds(pl.multiple_of(((p >> 1) & 3) * BS, BS), BS)
                    both = jnp.concatenate([prod[0, at, :], prod[1, at, :]], axis=0)
                    left = jnp.dot(
                        both, occ_ref[:, b * BS : (b + 1) * BS], preferred_element_type=jnp.float32
                    )
                    left = left.astype(jnp.bfloat16).astype(jnp.float32)
                    left = [left[s * BS : (s + 1) * BS, :].T for s in range(2)]

                    def add(q, center):
                        center = center.astype(jnp.float32)
                        for s in range(2):
                            acc[s, q] += (left[s] * center).reshape(BS // 8, 8, BS).sum(axis=0)

                    span = slice(b * BS, (b + 1) * BS)
                    if n_centers == 1:
                        lax.fori_loop(
                            0, n_q, lambda q, c: (add(q, c_refs[0][q, k, span, :]), c)[1], 0
                        )
                    else:
                        steps = [0, 1, 2 | plane, 3 ^ plane]
                        for step, c_ref in zip(steps, c_refs):
                            add(aux_at ^ step, c_ref[k, span, :])

    for s in range(2):
        out_ref[s] = acc[s].sum(axis=1)


def on_device(sizes, three_center, virt_density, occ_density, partner_list, partner_count):
    groups, aux, atoms = sizes
    rows = three_center.shape[0]
    basis_total = virt_density.shape[1]
    group_at = lax.axis_index("groups")
    aux_at = lax.axis_index("aux")
    atom_at = lax.axis_index("atoms")
    where = jnp.stack([atom_at, aux_at & 1, group_at, aux_at]).astype(jnp.int32)
    half_columns = basis_total // 4
    n_blocks = half_columns // BS

    core = functools.partial(swap, axes=("atoms",), sizes=(atoms,), move=lambda t: (t ^ 1,))
    across = functools.partial(swap, axes=("atoms",), sizes=(atoms,), move=lambda t: (t ^ 2,))
    plane = functools.partial(swap, axes=("groups",), sizes=(groups,), move=lambda g: (g ^ 1,))
    pair = functools.partial(swap, axes=("aux",), sizes=(aux,), move=lambda a: (a ^ 1,))

    anywhere = pl.BlockSpec(memory_space=pl.ANY)
    scalars = pl.BlockSpec(memory_space=pltpu.SMEM)
    vmem = pl.BlockSpec(memory_space=pltpu.VMEM)

    centers = three_center[:, 0].transpose(1, 0, 2)
    far_a = swap(
        centers, ("groups", "aux", "atoms"), sizes, lambda g, a, t: (g, a ^ g, t ^ 2)
    )
    near, far = pl.pallas_call(
        functools.partial(select, n_blocks),
        out_shape=[jax.ShapeDtypeStruct((half_columns, rows), jnp.bfloat16)] * 2,
        in_specs=[scalars, anywhere],
        out_specs=[vmem, vmem],
        scratch_shapes=[
            pltpu.VMEM((2 * n_blocks, rows, BS), jnp.bfloat16),
            pltpu.SemaphoreType.DMA((2 * n_blocks,)),
        ],
        compiler_params=pltpu.CompilerParams(vmem_limit_bytes=8 * MIB),
    )(where, virt_density)

    v_a = across(far)
    other = pair(centers)
    if aux == 4:
        rest_a = swap(centers, ("groups", "aux"), (groups, aux), lambda g, a: (g, a ^ (2 | g)))
    v_b = across(near)
    far_b = plane(far_a)
    if aux == 4:
        rest_b = plane(rest_a)
        all_centers = [centers, other, rest_a, rest_b]
    else:
        all_centers = [lax.all_gather(centers, "aux", axis=0)]

    m_parts = [centers, core(centers), far_a, core(far_a), other, core(other), far_b, core(far_b)]

    def run(far_half, v_parts):
        return pl.pallas_call(
            functools.partial(contract, len(all_centers), far_half),
            out_shape=jax.ShapeDtypeStruct((2, aux, BS), jnp.float32),
            in_specs=[scalars] * 3 + [anywhere] * 4 + [vmem] * (9 + len(all_centers)),
            out_specs=vmem,
            scratch_shapes=[
                pltpu.VMEM((4, half_columns, rows), jnp.bfloat16),
                pltpu.VMEM((2, half_columns, basis_total), jnp.bfloat16),
                pltpu.VMEM((2, aux, 8, BS), jnp.float32),
                pltpu.SemaphoreType.DMA((4,)),
            ],
            compiler_params=pltpu.CompilerParams(
                vmem_limit_bytes=(16 if aux == 4 else 40) * MIB
            ),
        )(where, partner_list, partner_count, *v_parts, *m_parts, occ_density, *all_centers)

    sums = run(False, [near, core(near), v_a, core(v_a)])
    sums = sums + run(True, [far, core(far), v_b, core(v_b)])

    sums = sums + core(sums)
    diagonal = swap(sums[1], ("aux", "atoms"), (aux, atoms), lambda a, t: (a ^ 1, t ^ 2))
    total = sums[0] + across(sums[0]) + pair(sums[1]) + diagonal
    share = aux // atoms
    row = lax.dynamic_slice_in_dim(total, atom_at * share, share, 0)
    return (row.sum(axis=1) * jnp.float32(-(basis_total ** (-0.5))))[None, :]


def solution(mesh):
    sizes = tuple(mesh.shape[name] for name in ("groups", "aux", "atoms"))
    in_specs = (
        P("atoms", "aux", None, None),
        P(("groups", "atoms"), None),
        P("groups", "atoms"),
        P(),
        P(),
    )
    out_specs = P(("groups", "aux"), "atoms")
    return jax.shard_map(
        functools.partial(on_device, sizes),
        mesh=mesh,
        in_specs=in_specs,
        out_specs=out_specs,
        check_vma=False,
    )
```

time: 228 us -> 85.6 us (0.38)
  waiting for transfers between devices: 120 us -> 34.3 us
  local copies, waits for them, and re-layouts: 52.7 us -> 11.6 us
  blocking collectives: 15.8 us -> 0 us
  starting transfers between devices: 9.24 us -> 24.7 us
  Pallas kernels: 0 us -> 13.1 us
  between operations: 13.6 us -> 1.27 us
  matrix products: 10.8 us -> 0 us
  other arithmetic: 5.04 us -> 0.7 us
    all_gather x2 -> x0, waiting for transfers between devices: 108 us -> none  [the longest x1 59.3 us: on_device(): full_virt = lax.all_gather(virt_density, 'atoms', axis=0, tiled=True)]
    ppermute x0 -> x19, waiting for transfers between devices: none -> 34.3 us  [swap(): return lax.ppermute(x, axes, perm)]
    ppermute x0 -> x19, starting transfers between devices: none -> 24.7 us  [swap(): return lax.ppermute(x, axes, perm)]
    gather x3 -> x0, local copies, waits for them, and re-layouts: 24 us -> none  [the longest x2 16.4 us: on_device(): jnp.take(shard_rows.reshape(count_rows, aux_local, block_total, BS), own_...]
    reshape x4 -> x0, local copies, waits for them, and re-layouts: 19.6 us -> none  [the longest x1 12.3 us: on_device(): shard_rows.reshape(count_rows, aux_local, block_total, BS)]
    unnamed x2 -> x0, blocking collectives: 15.8 us -> none
    pallas_call x0 -> x3, Pallas kernels: none -> 13.1 us  [the longest x2 10.7 us: run(): pl.pallas_call(functools.partial(contract, len(all_centers), far_half), o...]
    dot_general x3 -> x0, matrix products: 10.8 us -> none  [the longest x1 5.52 us: on_device(): jnp.einsum('brpkn,bknc->brpc', masked, picked, preferred_element_type=jnp...]
  transfers between devices with their start and end apart: 4 -> 19, of which waited for: 3 -> 10; matrix products, arithmetic and copies ran while one was open for 21% -> 0% of each run, Pallas kernels for 0% -> 4%
where the time goes in v2:
time: 85.6 us; the launch traced here: 85.7 us
  waiting for transfers between devices  34.3 us (40%)
  starting transfers between devices  24.7 us (29%)
  Pallas kernels  13.1 us (15%)
  local copies, waits for them, and re-layouts  11.6 us (14%)
  between operations  1.27 us (1%)
    ppermute x19, waiting for transfers between devices, swap(): return lax.ppermute(x, axes, perm)  34.3 us
    ppermute x19, starting transfers between devices, swap(): return lax.ppermute(x, axes, perm)  24.7 us
    unnamed x33, local copies, waits for them, and re-layouts  11.6 us
    pallas_call x2, Pallas kernels, run(): pl.pallas_call(functools.partial(contract, len(all_centers), far_half), o...  10.7 us
    pallas_call x1, Pallas kernels, on_device(): pl.pallas_call(functools.partial(select, n_blocks), out_shape=[jax.ShapeD...  2.42 us
  transfers between devices with their start and end apart: 19, of which 10 were waited for; matrix products, arithmetic and copies ran while one was open for 0% of the time, Pallas kernels for 4%

profile of v2, /device:TPU:0, one launch (start us, length us, event | category | flops | bytes accessed | tf_op | source)
XLA Modules:
  0.0 85.7 jit_solution(8800071392791944929)
XLA Ops:
  0.0 2.9 %collective-permute-start.4 = (bf16[3,512,128]{2,1,0:T(8,128)(2,1)}, bf16[3,512,128]{2,1,0:T(8,128)(2,1)S(1)}, u32[]{:S(2)}, u32[]{:S(2)}) collective-permute-start(bf16[3,512,128]{2,1,0:T(8,128)(2,1)} %bitcast.14), channel_id=1, source_target_pairs={{0,2},{1,3},{2,0},{3,1},{4,6},{5,7},{6,4},{7,5},{8,10},{9,11},{10,... | collective-permute-start | bytes 1179656 | tf_op jit(solution)/shard_map/ppermute | solution.py:29
  2.9 2.6 %collective-permute-start.10 = (bf16[3,512,128]{2,1,0:T(8,128)(2,1)}, bf16[3,512,128]{2,1,0:T(8,128)(2,1)S(1)}, u32[]{:S(2)}, u32[]{:S(2)}) collective-permute-start(bf16[3,512,128]{2,1,0:T(8,128)(2,1)} %bitcast.15), channel_id=1, source_target_pairs={{0,8},{4,12},{8,0},{12,4},{16,28},{20,24},{24,20},{28,16},{1,9},{5... | collective-permute-start | bytes 1179656 | tf_op jit(solution)/shard_map/ppermute | solution.py:29
  5.5 0.1 pad_add_fusion.where
  5.6 1.6 %copy-done.3 = bf16[512,2048]{1,0:T(8,128)(2,1)S(1)} copy-done((bf16[512,2048]{1,0:T(8,128)(2,1)S(1)}, bf16[512,2048]{1,0:T(8,128)(2,1)}, u32[]{:S(2)}) %copy-start.3) | copy-done | bytes 2097176
  7.2 2.4 %shard_map.55 = (bf16[512,512]{1,0:T(8,128)(2,1)}, bf16[512,512]{1,0:T(8,128)(2,1)S(1)}) custom-call(s32[4]{0:T(128)S(1)} %pad_add_fusion.where, bf16[512,2048]{1,0:T(8,128)(2,1)S(1)} %copy-done.3), custom_call_target="tpu_custom_call" | custom-call | tf_op jit(solution)/shard_map/pallas_call | solution.py:175
  9.6 0.6 collective-permute-start.13
  10.2 1.6 %collective-permute-start.6 = (bf16[3,512,128]{2,1,0:T(8,128)(2,1)}, bf16[3,512,128]{2,1,0:T(8,128)(2,1)S(1)}, u32[]{:S(2)}, u32[]{:S(2)}) collective-permute-start(bf16[3,512,128]{2,1,0:T(8,128)(2,1)} %bitcast.16), channel_id=1, source_target_pairs={{0,4},{4,0},{8,12},{12,8},{1,5},{5,1},{9,13},{13,9},{2,6},{6,2},{1... | collective-permute-start | bytes 1179656 | tf_op jit(solution)/shard_map/ppermute | solution.py:29
  11.8 0.0 collective-permute-start.3
  11.8 1.0 %collective-permute-done.4.refs_6_ = bf16[3,512,128]{2,1,0:T(8,128)(2,1)S(1)} collective-permute-done((bf16[3,512,128]{2,1,0:T(8,128)(2,1)}, bf16[3,512,128]{2,1,0:T(8,128)(2,1)S(1)}, u32[]{:S(2)}, u32[]{:S(2)}) %collective-permute-start.4) | collective-permute-done | bytes 393248 | tf_op jit(solution)/shard_map/ppermute | solution.py:29
  12.8 0.0 collective-permute-start.12
  12.8 10.4 %collective-permute-done.10.refs_15_ = bf16[3,512,128]{2,1,0:T(8,128)(2,1)S(1)} collective-permute-done((bf16[3,512,128]{2,1,0:T(8,128)(2,1)}, bf16[3,512,128]{2,1,0:T(8,128)(2,1)S(1)}, u32[]{:S(2)}, u32[]{:S(2)}) %collective-permute-start.10) | collective-permute-done | bytes 393248 | tf_op jit(solution)/shard_map/ppermute | solution.py:29
  23.2 0.5 collective-permute-start.1
  23.7 0.8 copy-done.10
  24.5 3.3 %collective-permute-done.6.refs_8_.refs_14_ = bf16[3,512,128]{2,1,0:T(8,128)(2,1)S(1)} collective-permute-done((bf16[3,512,128]{2,1,0:T(8,128)(2,1)}, bf16[3,512,128]{2,1,0:T(8,128)(2,1)S(1)}, u32[]{:S(2)}, u32[]{:S(2)}) %collective-permute-start.6) | collective-permute-done | bytes 393248 | tf_op jit(solution)/shard_map/ppermute | solution.py:29
  27.8 4.0 %collective-permute-start.8 = (bf16[3,512,128]{2,1,0:T(8,128)(2,1)S(1)}, bf16[3,512,128]{2,1,0:T(8,128)(2,1)}, u32[]{:S(2)}, u32[]{:S(2)}) collective-permute-start(bf16[3,512,128]{2,1,0:T(8,128)(2,1)S(1)} %collective-permute-done.4.refs_6_), channel_id=1, source_target_pairs={{0,16},{16,0},{1,17},{17,1},{2,18},{18,2},{3,19},{19,3},{4,20},{20... | collective-permute-start | bytes 1179656 | tf_op jit(solution)/shard_map/ppermute | solution.py:29
  31.8 0.0 collective-permute-done.3.refs_5_
  31.8 0.8 copy-done.4
  32.6 0.0 collective-permute-start.5
  32.6 0.0 collective-permute-done.13.refs_2_
  32.6 0.0 collective-permute-start.11
  32.6 0.8 copy-done.12
  33.4 0.5 collective-permute-start.14
  33.9 2.1 %collective-permute-done.1.refs_2_ = bf16[512,512]{1,0:T(8,128)(2,1)} collective-permute-done((bf16[512,512]{1,0:T(8,128)(2,1)S(1)}, bf16[512,512]{1,0:T(8,128)(2,1)}, u32[]{:S(2)}, u32[]{:S(2)}) %collective-permute-start.1) | collective-permute-done | bytes 524320 | tf_op jit(solution)/shard_map/ppermute | solution.py:29
  36.0 6.0 %collective-permute-done.8.refs_10_ = bf16[3,512,128]{2,1,0:T(8,128)(2,1)} collective-permute-done((bf16[3,512,128]{2,1,0:T(8,128)(2,1)S(1)}, bf16[3,512,128]{2,1,0:T(8,128)(2,1)}, u32[]{:S(2)}, u32[]{:S(2)}) %collective-permute-start.8) | collective-permute-done | bytes 393248 | tf_op jit(solution)/shard_map/ppermute | solution.py:29
  42.0 0.7 copy-done.6
  42.7 0.5 collective-permute-start.7
  43.2 5.3 %collective-permute-done.11.refs_16_ = bf16[3,512,128]{2,1,0:T(8,128)(2,1)S(1)} collective-permute-done((bf16[3,512,128]{2,1,0:T(8,128)(2,1)S(1)}, bf16[3,512,128]{2,1,0:T(8,128)(2,1)S(1)}, u32[]{:S(2)}, u32[]{:S(2)}) %collective-permute-start.11) | collective-permute-done | bytes 393248 | tf_op jit(solution)/shard_map/ppermute | solution.py:29
  48.5 0.8 copy-done.8
  49.2 0.1 copy.6.plist
  49.3 0.0 collective-permute-done.7.refs_9_
  49.3 0.0 collective-permute-done.14.refs_3_
  49.3 2.0 %collective-permute-done.9.refs_11_ = bf16[3,512,128]{2,1,0:T(8,128)(2,1)} collective-permute-done((bf16[3,512,128]{2,1,0:T(8,128)(2,1)}, bf16[3,512,128]{2,1,0:T(8,128)(2,1)}, u32[]{:S(2)}, u32[]{:S(2)}) %collective-permute-start.9) | collective-permute-done | bytes 393248 | tf_op jit(solution)/shard_map/ppermute | solution.py:29
  51.3 1.0 %copy-done.1 = bf16[512,1,3,128]{3,0,2,1:T(8,128)(2,1)S(1)} copy-done((bf16[512,1,3,128]{3,0,2,1:T(8,128)(2,1)S(1)}, bf16[512,1,3,128]{3,0,2,1:T(8,128)(2,1)}, u32[]{:S(2)}) %copy-start.1) | copy-done | bytes 393240
  52.3 1.0 %copy-done.5 = bf16[3,512,128]{2,1,0:T(8,128)(2,1)S(1)} copy-done((bf16[3,512,128]{2,1,0:T(8,128)(2,1)S(1)}, bf16[3,512,128]{2,1,0:T(8,128)(2,1)}, u32[]{:S(2)}) %copy-start.5) | copy-done | bytes 393240
  53.3 1.0 %copy-done.7 = bf16[3,512,128]{2,1,0:T(8,128)(2,1)S(1)} copy-done((bf16[3,512,128]{2,1,0:T(8,128)(2,1)S(1)}, bf16[3,512,128]{2,1,0:T(8,128)(2,1)}, u32[]{:S(2)}) %copy-start.7) | copy-done | bytes 393240
  54.3 1.0 %copy-done.9 = bf16[3,512,128]{2,1,0:T(8,128)(2,1)S(1)} copy-done((bf16[3,512,128]{2,1,0:T(8,128)(2,1)S(1)}, bf16[3,512,128]{2,1,0:T(8,128)(2,1)}, u32[]{:S(2)}) %copy-start.9) | copy-done | bytes 393240
  55.3 1.0 %copy-done.11 = bf16[512,512]{1,0:T(8,128)(2,1)S(1)} copy-done((bf16[512,512]{1,0:T(8,128)(2,1)S(1)}, bf16[512,512]{1,0:T(8,128)(2,1)}, u32[]{:S(2)}) %copy-start.11) | copy-done | bytes 524312
  56.3 1.0 %copy-done.13 = bf16[512,512]{1,0:T(8,128)(2,1)S(1)} copy-done((bf16[512,512]{1,0:T(8,128)(2,1)S(1)}, bf16[512,512]{1,0:T(8,128)(2,1)}, u32[]{:S(2)}) %copy-start.13) | copy-done | bytes 524312
  57.4 1.4 %shard_map.57 = f32[2,4,128]{2,1,0:T(4,128)S(1)} custom-call(s32[4]{0:T(128)S(1)} %pad_add_fusion.where, s32[16,3]{1,0:T(8,128)S(1)} %copy.6.plist, s32[16]{0:T(128)S(1)} %copy-done.14, bf16[512,512]{1,0:T(8,128)(2,1)S(1)} %copy-done.11, bf16[512,512]{1,0:T(8,128)(2,1)S(1)} %copy-done.13, bf16[512,512]{1,0:T(8,128)(2,1)} %collective-permute-done.13.refs_2_, ...), custom_call_target="tpu_custom_call" | custom-call | tf_op jit(solution)/shard_map/pallas_call | solution.py:202
  58.8 9.3 %shard_map.56 = f32[2,4,128]{2,1,0:T(4,128)S(1)} custom-call(s32[4]{0:T(128)S(1)} %pad_add_fusion.where, s32[16,3]{1,0:T(8,128)S(1)} %copy.6.plist, s32[16]{0:T(128)S(1)} %copy-done.14, bf16[512,512]{1,0:T(8,128)(2,1)} %get-tuple-element.7.refs_0_, bf16[512,512]{1,0:T(8,128)(2,1)} %collective-permute-done.refs_1_, ...), custom_call_target="tpu_custom_call" | custom-call | tf_op jit(solution)/shard_map/pallas_call | solution.py:202
  68.1 1.2 %collective-permute-start.15 = (f32[2,4,128]{2,1,0:T(4,128)S(1)}, f32[2,4,128]{2,1,0:T(4,128)S(1)}, u32[]{:S(2)}, u32[]{:S(2)}) collective-permute-start(f32[2,4,128]{2,1,0:T(4,128)S(1)} %add.18), channel_id=1, source_target_pairs={{0,1},{1,0},{2,3},{3,2},{4,5},{5,4},{6,7},{7,6},{8,9},{9,8},{10,11... | collective-permute-start | bytes 12296 | tf_op jit(solution)/shard_map/ppermute | solution.py:29
  69.4 0.8 collective-permute-done.15
  70.2 6.9 %collective-permute-start.16 = (f32[4,128]{1,0:T(4,128)S(1)}, f32[4,128]{1,0:T(4,128)S(1)}, u32[]{:S(2)}, u32[]{:S(2)}) collective-permute-start(f32[4,128]{1,0:T(4,128)S(1)} %get-tuple-element.9), channel_id=1, source_target_pairs={{0,2},{1,3},{2,0},{3,1},{4,6},{5,7},{6,4},{7,5},{8,10},{9,11},{10,... | collective-permute-start | bytes 6152 | tf_op jit(solution)/shard_map/ppermute | solution.py:29
  77.1 2.4 %collective-permute-start.17 = (f32[4,128]{1,0:T(4,128)S(1)}, f32[4,128]{1,0:T(4,128)S(1)}, u32[]{:S(2)}, u32[]{:S(2)}) collective-permute-start(f32[4,128]{1,0:T(4,128)S(1)} %get-tuple-element.10), channel_id=1, source_target_pairs={{0,4},{4,0},{8,12},{12,8},{1,5},{5,1},{9,13},{13,9},{2,6},{6,2},{1... | collective-permute-start | bytes 6152 | tf_op jit(solution)/shard_map/ppermute | solution.py:29
  79.4 0.9 %collective-permute-start.18 = (f32[4,128]{1,0:T(4,128)S(1)}, f32[4,128]{1,0:T(4,128)S(1)}, u32[]{:S(2)}, u32[]{:S(2)}) collective-permute-start(f32[4,128]{1,0:T(4,128)S(1)} %get-tuple-element.10), channel_id=1, source_target_pairs={{0,6},{1,7},{2,4},{3,5},{4,2},{5,3},{6,0},{7,1},{8,14},{9,15},{10,... | collective-permute-start | bytes 6152 | tf_op jit(solution)/shard_map/ppermute | solution.py:29
  80.4 0.6 collective-permute-done.17
  81.0 2.9 %collective-permute-done.18 = f32[4,128]{1,0:T(4,128)S(1)} collective-permute-done((f32[4,128]{1,0:T(4,128)S(1)}, f32[4,128]{1,0:T(4,128)S(1)}, u32[]{:S(2)}, u32[]{:S(2)}) %collective-permute-start.18) | collective-permute-done | bytes 2080 | tf_op jit(solution)/shard_map/ppermute | solution.py:29
  83.9 0.6 dynamic-slice_reduce_fusion
  (32 shorter events, 0.1 us)
Async XLA Ops:
  0.0 51.3 %copy-start = (bf16[2048,512]{1,0:T(8,128)(2,1)S(1)}, bf16[2048,512]{1,0:T(8,128)(2,1)}, u32[]{:S(2)}) copy-start(bf16[2048,512]{1,0:T(8,128)(2,1)} %refs_12_.3) | copy-start | bytes 6291460
  0.0 12.8 %collective-permute-start.4 = (bf16[3,512,128]{2,1,0:T(8,128)(2,1)}, bf16[3,512,128]{2,1,0:T(8,128)(2,1)S(1)}, u32[]{:S(2)}, u32[]{:S(2)}) collective-permute-start(bf16[3,512,128]{2,1,0:T(8,128)(2,1)} %bitcast.14), channel_id=1, source_target_pairs={{0,2},{1,3},{2,0},{3,1},{4,6},{5,7},{6,4},{7,5},{8,10},{9,11},{10,... | collective-permute-start | bytes 1179656 | tf_op jit(solution)/shard_map/ppermute | solution.py:29
  2.9 20.2 %collective-permute-start.10 = (bf16[3,512,128]{2,1,0:T(8,128)(2,1)}, bf16[3,512,128]{2,1,0:T(8,128)(2,1)S(1)}, u32[]{:S(2)}, u32[]{:S(2)}) collective-permute-start(bf16[3,512,128]{2,1,0:T(8,128)(2,1)} %bitcast.15), channel_id=1, source_target_pairs={{0,8},{4,12},{8,0},{12,4},{16,28},{20,24},{24,20},{28,16},{1,9},{5... | collective-permute-start | bytes 1179656 | tf_op jit(solution)/shard_map/ppermute | solution.py:29
  5.6 1.6 %copy-start.3 = (bf16[512,2048]{1,0:T(8,128)(2,1)S(1)}, bf16[512,2048]{1,0:T(8,128)(2,1)}, u32[]{:S(2)}) copy-start(bf16[512,2048]{1,0:T(8,128)(2,1)} %virt_ref.1) | copy-start | bytes 6291460
  7.2 42.0 %copy-start.15 = (s32[16,3]{0,1:T(4,128)S(1)}, s32[16,3]{0,1:T(4,128)}, u32[]{:S(2)}) copy-start(s32[16,3]{0,1:T(4,128)} %param.8) | copy-start | bytes 580
  7.2 44.1 %copy-start.14 = (s32[16]{0:T(128)S(1)}, s32[16]{0:T(128)}, u32[]{:S(2)}) copy-start(s32[16]{0:T(128)} %pcount.3) | copy-start | bytes 196
  9.6 22.9 %collective-permute-start.13 = (bf16[512,512]{1,0:T(8,128)(2,1)}, bf16[512,512]{1,0:T(8,128)(2,1)}, u32[]{:S(2)}, u32[]{:S(2)}) collective-permute-start(bf16[512,512]{1,0:T(8,128)(2,1)} %get-tuple-element.7.refs_0_), channel_id=1, source_target_pairs={{0,2},{1,3},{2,0},{3,1},{4,6},{5,7},{6,4},{7,5},{8,10},{9,11},{10,... | collective-permute-start | bytes 1572872 | tf_op jit(solution)/shard_map/ppermute | solution.py:29
  10.2 17.5 %collective-permute-start.6 = (bf16[3,512,128]{2,1,0:T(8,128)(2,1)}, bf16[3,512,128]{2,1,0:T(8,128)(2,1)S(1)}, u32[]{:S(2)}, u32[]{:S(2)}) collective-permute-start(bf16[3,512,128]{2,1,0:T(8,128)(2,1)} %bitcast.16), channel_id=1, source_target_pairs={{0,4},{4,0},{8,12},{12,8},{1,5},{5,1},{9,13},{13,9},{2,6},{6,2},{1... | collective-permute-start | bytes 1179656 | tf_op jit(solution)/shard_map/ppermute | solution.py:29
  11.8 20.0 %collective-permute-start.3 = (bf16[3,512,128]{2,1,0:T(8,128)(2,1)}, bf16[3,512,128]{2,1,0:T(8,128)(2,1)S(1)}, u32[]{:S(2)}, u32[]{:S(2)}) collective-permute-start(bf16[3,512,128]{2,1,0:T(8,128)(2,1)} %bitcast.17), channel_id=1, source_target_pairs={{0,1},{1,0},{2,3},{3,2},{4,5},{5,4},{6,7},{7,6},{8,9},{9,8},{10,11... | collective-permute-start | bytes 1179656 | tf_op jit(solution)/shard_map/ppermute | solution.py:29
  12.8 19.8 %collective-permute-start.12 = (bf16[512,512]{1,0:T(8,128)(2,1)S(1)}, bf16[512,512]{1,0:T(8,128)(2,1)S(1)}, u32[]{:S(2)}, u32[]{:S(2)}) collective-permute-start(bf16[512,512]{1,0:T(8,128)(2,1)S(1)} %get-tuple-element.8.refs_0_), channel_id=1, source_target_pairs={{0,1},{1,0},{2,3},{3,2},{4,5},{5,4},{6,7},{7,6},{8,9},{9,8},{10,11... | collective-permute-start | bytes 1572872 | tf_op jit(solution)/shard_map/ppermute | solution.py:29
  23.2 12.8 %collective-permute-start.1 = (bf16[512,512]{1,0:T(8,128)(2,1)S(1)}, bf16[512,512]{1,0:T(8,128)(2,1)}, u32[]{:S(2)}, u32[]{:S(2)}) collective-permute-start(bf16[512,512]{1,0:T(8,128)(2,1)S(1)} %get-tuple-element.8.refs_0_), channel_id=1, source_target_pairs={{0,2},{1,3},{2,0},{3,1},{4,6},{5,7},{6,4},{7,5},{8,10},{9,11},{10,... | collective-permute-start | bytes 1572872 | tf_op jit(solution)/shard_map/ppermute | solution.py:29
  23.7 0.8 copy-start.10
  27.8 14.2 %collective-permute-start.8 = (bf16[3,512,128]{2,1,0:T(8,128)(2,1)S(1)}, bf16[3,512,128]{2,1,0:T(8,128)(2,1)}, u32[]{:S(2)}, u32[]{:S(2)}) collective-permute-start(bf16[3,512,128]{2,1,0:T(8,128)(2,1)S(1)} %collective-permute-done.4.refs_6_), channel_id=1, source_target_pairs={{0,16},{16,0},{1,17},{17,1},{2,18},{18,2},{3,19},{19,3},{4,20},{20... | collective-permute-start | bytes 1179656 | tf_op jit(solution)/shard_map/ppermute | solution.py:29
  31.8 0.8 copy-start.4
  32.6 9.4 %collective-permute-start.5 = (bf16[3,512,128]{2,1,0:T(8,128)(2,1)S(1)}, bf16[3,512,128]{2,1,0:T(8,128)(2,1)S(1)}, u32[]{:S(2)}, u32[]{:S(2)}) collective-permute-start(bf16[3,512,128]{2,1,0:T(8,128)(2,1)S(1)} %collective-permute-done.4.refs_6_), channel_id=1, source_target_pairs={{0,1},{1,0},{2,3},{3,2},{4,5},{5,4},{6,7},{7,6},{8,9},{9,8},{10,11... | collective-permute-start | bytes 1179656 | tf_op jit(solution)/shard_map/ppermute | solution.py:29
  32.6 15.9 %collective-permute-start.11 = (bf16[3,512,128]{2,1,0:T(8,128)(2,1)S(1)}, bf16[3,512,128]{2,1,0:T(8,128)(2,1)S(1)}, u32[]{:S(2)}, u32[]{:S(2)}) collective-permute-start(bf16[3,512,128]{2,1,0:T(8,128)(2,1)S(1)} %collective-permute-done.10.refs_15_), channel_id=1, source_target_pairs={{0,16},{16,0},{1,17},{17,1},{2,18},{18,2},{3,19},{19,3},{4,20},{20... | collective-permute-start | bytes 1179656 | tf_op jit(solution)/shard_map/ppermute | solution.py:29
  32.6 0.8 copy-start.12
  33.4 15.9 %collective-permute-start.14 = (bf16[512,512]{1,0:T(8,128)(2,1)}, bf16[512,512]{1,0:T(8,128)(2,1)}, u32[]{:S(2)}, u32[]{:S(2)}) collective-permute-start(bf16[512,512]{1,0:T(8,128)(2,1)} %collective-permute-done.13.refs_2_), channel_id=1, source_target_pairs={{0,1},{1,0},{2,3},{3,2},{4,5},{5,4},{6,7},{7,6},{8,9},{9,8},{10,11... | collective-permute-start | bytes 1572872 | tf_op jit(solution)/shard_map/ppermute | solution.py:29
  36.0 22.8 %collective-permute-start = (bf16[512,512]{1,0:T(8,128)(2,1)}, bf16[512,512]{1,0:T(8,128)(2,1)}, u32[]{:S(2)}, u32[]{:S(2)}) collective-permute-start(bf16[512,512]{1,0:T(8,128)(2,1)} %get-tuple-element.7.refs_0_), channel_id=1, source_target_pairs={{0,1},{1,0},{2,3},{3,2},{4,5},{5,4},{6,7},{7,6},{8,9},{9,8},{10,11... | collective-permute-start | bytes 1572872 | tf_op jit(solution)/shard_map/ppermute | solution.py:29
  42.0 16.8 %collective-permute-start.2 = (bf16[512,512]{1,0:T(8,128)(2,1)}, bf16[512,512]{1,0:T(8,128)(2,1)}, u32[]{:S(2)}, u32[]{:S(2)}) collective-permute-start(bf16[512,512]{1,0:T(8,128)(2,1)} %collective-permute-done.1.refs_2_), channel_id=1, source_target_pairs={{0,1},{1,0},{2,3},{3,2},{4,5},{5,4},{6,7},{7,6},{8,9},{9,8},{10,11... | collective-permute-start | bytes 1572872 | tf_op jit(solution)/shard_map/ppermute | solution.py:29
  42.0 0.7 copy-start.6
  42.7 6.6 %collective-permute-start.7 = (bf16[3,512,128]{2,1,0:T(8,128)(2,1)S(1)}, bf16[3,512,128]{2,1,0:T(8,128)(2,1)}, u32[]{:S(2)}, u32[]{:S(2)}) collective-permute-start(bf16[3,512,128]{2,1,0:T(8,128)(2,1)S(1)} %collective-permute-done.6.refs_8_.refs_14_), channel_id=1, source_target_pairs={{0,1},{1,0},{2,3},{3,2},{4,5},{5,4},{6,7},{7,6},{8,9},{9,8},{10,11... | collective-permute-start | bytes 1179656 | tf_op jit(solution)/shard_map/ppermute | solution.py:29
  48.5 0.8 copy-start.8
  49.2 2.1 %collective-permute-start.9 = (bf16[3,512,128]{2,1,0:T(8,128)(2,1)}, bf16[3,512,128]{2,1,0:T(8,128)(2,1)}, u32[]{:S(2)}, u32[]{:S(2)}) collective-permute-start(bf16[3,512,128]{2,1,0:T(8,128)(2,1)} %collective-permute-done.8.refs_10_), channel_id=1, source_target_pairs={{0,1},{1,0},{2,3},{3,2},{4,5},{5,4},{6,7},{7,6},{8,9},{9,8},{10,11... | collective-permute-start | bytes 1179656 | tf_op jit(solution)/shard_map/ppermute | solution.py:29
  51.3 1.0 %copy-start.1 = (bf16[512,1,3,128]{3,0,2,1:T(8,128)(2,1)S(1)}, bf16[512,1,3,128]{3,0,2,1:T(8,128)(2,1)}, u32[]{:S(2)}) copy-start(bf16[512,1,3,128]{3,0,2,1:T(8,128)(2,1)} %param.5) | copy-start | bytes 1179652
  52.3 1.0 %copy-start.5 = (bf16[3,512,128]{2,1,0:T(8,128)(2,1)S(1)}, bf16[3,512,128]{2,1,0:T(8,128)(2,1)}, u32[]{:S(2)}) copy-start(bf16[3,512,128]{2,1,0:T(8,128)(2,1)} %copy-done.4) | copy-start | bytes 1179652
  53.3 1.0 %copy-start.7 = (bf16[3,512,128]{2,1,0:T(8,128)(2,1)S(1)}, bf16[3,512,128]{2,1,0:T(8,128)(2,1)}, u32[]{:S(2)}) copy-start(bf16[3,512,128]{2,1,0:T(8,128)(2,1)} %copy-done.6) | copy-start | bytes 1179652
  54.3 1.0 %copy-start.9 = (bf16[3,512,128]{2,1,0:T(8,128)(2,1)S(1)}, bf16[3,512,128]{2,1,0:T(8,128)(2,1)}, u32[]{:S(2)}) copy-start(bf16[3,512,128]{2,1,0:T(8,128)(2,1)} %copy-done.8) | copy-start | bytes 1179652
  55.3 1.0 %copy-start.11 = (bf16[512,512]{1,0:T(8,128)(2,1)S(1)}, bf16[512,512]{1,0:T(8,128)(2,1)}, u32[]{:S(2)}) copy-start(bf16[512,512]{1,0:T(8,128)(2,1)} %copy-done.10) | copy-start | bytes 1572868
  56.3 1.0 %copy-start.13 = (bf16[512,512]{1,0:T(8,128)(2,1)S(1)}, bf16[512,512]{1,0:T(8,128)(2,1)}, u32[]{:S(2)}) copy-start(bf16[512,512]{1,0:T(8,128)(2,1)} %copy-done.12) | copy-start | bytes 1572868
  57.4 1.4 %copy-start.2 = (bf16[512,1,3,128]{3,0,2,1:T(8,128)(2,1)S(1)}, bf16[512,1,3,128]{3,0,2,1:T(8,128)(2,1)}, u32[]{:S(2)}) copy-start(bf16[512,1,3,128]{3,0,2,1:T(8,128)(2,1)} %param.5) | copy-start | bytes 1179652
  68.1 2.1 %collective-permute-start.15 = (f32[2,4,128]{2,1,0:T(4,128)S(1)}, f32[2,4,128]{2,1,0:T(4,128)S(1)}, u32[]{:S(2)}, u32[]{:S(2)}) collective-permute-start(f32[2,4,128]{2,1,0:T(4,128)S(1)} %add.18), channel_id=1, source_target_pairs={{0,1},{1,0},{2,3},{3,2},{4,5},{5,4},{6,7},{7,6},{8,9},{9,8},{10,11... | collective-permute-start | bytes 12296 | tf_op jit(solution)/shard_map/ppermute | solution.py:29
  70.2 10.2 %collective-permute-start.16 = (f32[4,128]{1,0:T(4,128)S(1)}, f32[4,128]{1,0:T(4,128)S(1)}, u32[]{:S(2)}, u32[]{:S(2)}) collective-permute-start(f32[4,128]{1,0:T(4,128)S(1)} %get-tuple-element.9), channel_id=1, source_target_pairs={{0,2},{1,3},{2,0},{3,1},{4,6},{5,7},{6,4},{7,5},{8,10},{9,11},{10,... | collective-permute-start | bytes 6152 | tf_op jit(solution)/shard_map/ppermute | solution.py:29
  77.1 3.9 %collective-permute-start.17 = (f32[4,128]{1,0:T(4,128)S(1)}, f32[4,128]{1,0:T(4,128)S(1)}, u32[]{:S(2)}, u32[]{:S(2)}) collective-permute-start(f32[4,128]{1,0:T(4,128)S(1)} %get-tuple-element.10), channel_id=1, source_target_pairs={{0,4},{4,0},{8,12},{12,8},{1,5},{5,1},{9,13},{13,9},{2,6},{6,2},{1... | collective-permute-start | bytes 6152 | tf_op jit(solution)/shard_map/ppermute | solution.py:29
  79.4 4.5 %collective-permute-start.18 = (f32[4,128]{1,0:T(4,128)S(1)}, f32[4,128]{1,0:T(4,128)S(1)}, u32[]{:S(2)}, u32[]{:S(2)}) collective-permute-start(f32[4,128]{1,0:T(4,128)S(1)} %get-tuple-element.10), channel_id=1, source_target_pairs={{0,6},{1,7},{2,4},{3,5},{4,2},{5,3},{6,0},{7,1},{8,14},{9,15},{10,... | collective-permute-start | bytes 6152 | tf_op jit(solution)/shard_map/ppermute | solution.py:29

commit v3 on v2

v3 whole, which is shorter than its diff:
```python
import functools

import jax
import jax.numpy as jnp
from jax import lax
from jax.experimental import pallas as pl
from jax.experimental.pallas import tpu as pltpu
from jax.sharding import PartitionSpec as P

BS = 128
KN = 3
MIB = 1 << 20


def swap(x, axes, sizes, move):
    perm = []
    total = 1
    for size in sizes:
        total *= size
    for source in range(total):
        coords, rest = [], source
        for size in reversed(sizes):
            coords.append(rest % size)
            rest //= size
        target = 0
        for size, at in zip(sizes, move(*reversed(coords))):
            target = target * size + at
        perm.append((source, target))
    return lax.ppermute(x, axes, perm)


def select(blocks_half, where, virt_ref, near_ref, far_ref, buf, sem):
    parity, half = where[1], where[0] >> 1

    def copy(i):
        at = half if i < blocks_half else 1 - half
        block = 2 * (at * blocks_half + i % blocks_half) + parity
        columns = pl.ds(pl.multiple_of(block * BS, BS), BS)
        return pltpu.make_async_copy(virt_ref.at[:, columns], buf.at[i], sem.at[i])

    order = list(range(blocks_half, 2 * blocks_half)) + list(range(blocks_half))
    for i in order:
        copy(i).start()
    for i in order:
        copy(i).wait()
        out_ref = near_ref if i < blocks_half else far_ref
        row = i % blocks_half * BS
        out_ref[row : row + BS, :] = buf[i].T


def after(x, *others):
    return lax.optimization_barrier((x,) + others)[0]


def left_tiles(far_half, where, plist, pcount, v_refs, m_refs, occ_ref, left_ref, scratch):
    vbuf, mbuf, obuf, prod, listed, place, vsem, msem, osem = scratch
    own, parity = where[0], where[1]
    half = 1 - (own >> 1) if far_half else own >> 1
    basis = mbuf.shape[2]
    rows = basis // 4
    blocks_here = rows // BS
    n_places = vbuf.shape[0]

    def used(b, k):
        block = own * blocks_here + b
        p = plist[block, k]
        return (k < pcount[block]) & ((p & 1) == parity) & ((p >> 3) == half)

    def column(b, k):
        return (plist[own * blocks_here + b, k] >> 1) & 3

    count = jnp.int32(0)
    for c in range(n_places):
        need = jnp.int32(0)
        for b in range(blocks_here):
            for k in range(KN):
                need = need | (used(b, k) & (column(b, k) == c)).astype(jnp.int32)
        place[c] = count

        @pl.when(need > 0)
        def _(c=c, count=count):
            listed[count] = c

        count = count + need

    @pl.when((count & 1) == 1)
    def _():
        listed[count] = listed[count - 1]

    groups = (count + 1) >> 1

    def v_copies(at):
        row = pl.ds(pl.multiple_of(listed[at] * BS, BS), BS)
        return [
            pltpu.make_async_copy(v_refs[i].at[row], vbuf.at[at, own ^ i], vsem.at[at, i])
            for i in range(4)
        ]

    def m_copies():
        out = []
        for i in range(8):
            span = pl.ds(pl.multiple_of((own ^ (i % 4)) * rows, rows), rows)
            out.append(
                pltpu.make_async_copy(m_refs[i], mbuf.at[i // 4, :, span], msem.at[i])
            )
        return out

    o_copy = pltpu.make_async_copy(occ_ref, obuf, osem)

    @pl.when(count > 0)
    def _():
        for copy in v_copies(0) + v_copies(1) + m_copies():
            copy.start()

        @pl.when(groups > 1)
        def _():
            for copy in v_copies(2) + v_copies(3):
                copy.start()

        o_copy.start()
        for copy in m_copies():
            copy.wait()

        def one_group(g, carry):
            for copy in v_copies(2 * g) + v_copies(2 * g + 1):
                copy.wait()

            def four_blocks(i, carry):
                for j in range(4):
                    block = 4 * i + j
                    span = pl.ds(pl.multiple_of(block * BS, BS), BS)
                    weights, parts = [], []
                    for k in range(KN):
                        p = plist[block, k]
                        at = pl.ds(pl.multiple_of((p & 3) * BS, BS), BS)
                        parts.append(
                            jnp.concatenate(
                                [vbuf[2 * g + h, p >> 2, :, at] for h in range(2)], axis=0
                            )
                        )
                        weight = jnp.concatenate([mbuf[s, k, span, :] for s in range(2)], axis=0)
                        if k > 0:
                            weight = jnp.where(k < pcount[block], weight, jnp.zeros_like(weight))
                        weights.append(weight)
                    res = lax.dot_general(
                        jnp.concatenate(parts, axis=1),
                        jnp.concatenate(weights, axis=1),
                        (((1,), (1,)), ((), ())),
                        preferred_element_type=jnp.float32,
                    ).astype(jnp.bfloat16)
                    for s in range(2):
                        for h in range(2):
                            prod[2 * g + h, s * BS : (s + 1) * BS, span] = res[
                                h * BS : (h + 1) * BS, s * BS : (s + 1) * BS
                            ]
                return carry

            lax.fori_loop(0, basis // (4 * BS), four_blocks, 0)
            return carry

        lax.fori_loop(0, groups, one_group, 0)
        o_copy.wait()
        for b in range(blocks_here):
            for k in range(KN):

                @pl.when(used(b, k))
                def _(b=b, k=k):
                    left = jnp.dot(
                        prod[place[column(b, k)]],
                        obuf[:, b * BS : (b + 1) * BS],
                        preferred_element_type=jnp.float32,
                    )
                    left_ref[b * KN + k] = left.astype(jnp.bfloat16)


def first(where, plist, pcount, *refs):
    left_tiles(False, where, plist, pcount, refs[0:4], refs[4:12], refs[12], refs[13], refs[14:])


def second(n_centers, where, plist, pcount, *refs):
    before_ref = refs[13]
    c_refs = refs[14 : 14 + n_centers]
    out_ref, left, cbuf, acc, csem, bsem = refs[14 + n_centers : 20 + n_centers]
    own, parity, plane, aux_at = where[0], where[1], where[2], where[3]
    half = 1 - (own >> 1)
    n_q, _, rows, _ = cbuf.shape
    blocks_here = rows // BS

    if n_centers == 1:
        copies = [pltpu.make_async_copy(c_refs[0], cbuf, csem.at[0])]
    else:
        steps = [0, 1, 2 | plane, 3 ^ plane]
        copies = [
            pltpu.make_async_copy(c_refs[i], cbuf.at[aux_at ^ steps[i]], csem.at[i])
            for i in range(n_centers)
        ]
    slots = [(b, k) for b in range(blocks_here) for k in range(KN)]

    def kept(b, k):
        block = own * blocks_here + b
        p = plist[block, k]
        return (k < pcount[block]) & ((p & 1) == parity) & ((p >> 3) != half)

    def before(b, k):
        i = b * KN + k
        return pltpu.make_async_copy(before_ref.at[i], left.at[i], bsem.at[i])

    for b, k in slots:
        pl.when(kept(b, k))(lambda b=b, k=k: before(b, k).start())
    for copy in copies:
        copy.start()
    acc[...] = jnp.zeros_like(acc)
    left_tiles(
        True, where, plist, pcount, refs[0:4], refs[4:12], refs[12], left, refs[20 + n_centers :]
    )
    for b, k in slots:
        pl.when(kept(b, k))(lambda b=b, k=k: before(b, k).wait())
    for copy in copies:
        copy.wait()

    for b, k in slots:
        block = own * blocks_here + b

        @pl.when((k < pcount[block]) & ((plist[block, k] & 1) == parity))
        def _(b=b, k=k):
            tile = left[b * KN + k].astype(jnp.float32)
            tile = [tile[s * BS : (s + 1) * BS, :].T for s in range(2)]

            def add(q, carry):
                center = cbuf[q, k, b * BS : (b + 1) * BS, :].astype(jnp.float32)
                for s in range(2):
                    acc[s, q] += (tile[s] * center).reshape(BS // 8, 8, BS).sum(axis=0)
                return carry

            lax.fori_loop(0, n_q, add, 0, unroll=n_q <= 8)

    for s in range(2):
        out_ref[s] = acc[s].sum(axis=1)


def on_device(sizes, three_center, virt_density, occ_density, partner_list, partner_count):
    groups, aux, atoms = sizes
    rows = three_center.shape[0]
    basis_total = virt_density.shape[1]
    group_at = lax.axis_index("groups")
    aux_at = lax.axis_index("aux")
    atom_at = lax.axis_index("atoms")
    where = jnp.stack([atom_at, aux_at & 1, group_at, aux_at]).astype(jnp.int32)
    half_columns = basis_total // 4
    n_blocks = half_columns // BS
    n_slots = rows // BS * KN

    core = functools.partial(swap, axes=("atoms",), sizes=(atoms,), move=lambda t: (t ^ 1,))
    across = functools.partial(swap, axes=("atoms",), sizes=(atoms,), move=lambda t: (t ^ 2,))
    plane = functools.partial(swap, axes=("groups",), sizes=(groups,), move=lambda g: (g ^ 1,))
    pair = functools.partial(swap, axes=("aux",), sizes=(aux,), move=lambda a: (a ^ 1,))

    anywhere = pl.BlockSpec(memory_space=pltpu.HBM)
    scalars = pl.BlockSpec(memory_space=pltpu.SMEM)
    vmem = pl.BlockSpec(memory_space=pltpu.VMEM)

    centers = three_center[:, 0].transpose(1, 0, 2)
    far_a = across(centers)
    other = pair(centers)
    near, far = pl.pallas_call(
        functools.partial(select, n_blocks),
        out_shape=[jax.ShapeDtypeStruct((half_columns, rows), jnp.bfloat16)] * 2,
        in_specs=[scalars, anywhere],
        out_specs=[vmem, vmem],
        scratch_shapes=[
            pltpu.VMEM((2 * n_blocks, rows, BS), jnp.bfloat16),
            pltpu.SemaphoreType.DMA((2 * n_blocks,)),
        ],
        compiler_params=pltpu.CompilerParams(vmem_limit_bytes=8 * MIB),
    )(where, virt_density)
    v_a = across(far)
    if aux == 4:
        rest_a = swap(centers, ("groups", "aux"), (groups, aux), lambda g, a: (g, a ^ (2 | g)))
        rest_b = plane(rest_a)
        all_centers = [centers, other, rest_a, rest_b]
        early, late = rest_a, rest_b
    else:
        all_centers = [lax.all_gather(centers, "aux", axis=0)]
        early, late = other, all_centers[0]
    far_b = pair(far_a)
    v_b = across(after(near, far_a))

    m_parts = [centers, core(centers), far_a, core(far_a), other, core(other), far_b, core(after(far_b, early))]

    def scratch():
        return [
            pltpu.VMEM((n_blocks, 4, BS, rows), jnp.bfloat16),
            pltpu.VMEM((2, KN, basis_total, BS), jnp.bfloat16),
            pltpu.VMEM((basis_total, rows), jnp.bfloat16),
            pltpu.VMEM((n_blocks, 2 * BS, basis_total), jnp.bfloat16),
            pltpu.SMEM((n_blocks,), jnp.int32),
            pltpu.SMEM((n_blocks,), jnp.int32),
            pltpu.SemaphoreType.DMA((n_blocks, 4)),
            pltpu.SemaphoreType.DMA((8,)),
            pltpu.SemaphoreType.DMA,
        ]

    tiles = jax.ShapeDtypeStruct((n_slots, 2 * BS, BS), jnp.bfloat16)
    before = pl.pallas_call(
        first,
        out_shape=tiles,
        in_specs=[scalars] * 3 + [anywhere] * 13,
        out_specs=vmem,
        scratch_shapes=scratch(),
        compiler_params=pltpu.CompilerParams(vmem_limit_bytes=20 * MIB),
    )(where, partner_list, partner_count, near, core(near), v_a, core(v_a), *m_parts, occ_density)
    v_b_core = core(after(v_b, before, late))
    sums = pl.pallas_call(
        functools.partial(second, len(all_centers)),
        out_shape=jax.ShapeDtypeStruct((2, aux, BS), jnp.float32),
        in_specs=[scalars] * 3 + [anywhere] * (14 + len(all_centers)),
        out_specs=vmem,
        scratch_shapes=[
            pltpu.VMEM(tiles.shape, tiles.dtype),
            pltpu.VMEM((aux, KN, rows, BS), jnp.bfloat16),
            pltpu.VMEM((2, aux, 8, BS), jnp.float32),
            pltpu.SemaphoreType.DMA((4,)),
            pltpu.SemaphoreType.DMA((n_slots,)),
        ]
        + scratch(),
        compiler_params=pltpu.CompilerParams(vmem_limit_bytes=(20 if aux == 4 else 48) * MIB),
    )(
        where,
        partner_list,
        partner_count,
        far,
        core(far),
        v_b,
        v_b_core,
        *m_parts,
        occ_density,
        before,
        *all_centers,
    )

    sums = sums + core(sums)
    diagonal = swap(sums[1], ("aux", "atoms"), (aux, atoms), lambda a, t: (a ^ 1, t ^ 2))
    total = sums[0] + across(sums[0]) + pair(sums[1]) + diagonal
    share = aux // atoms
    row = lax.dynamic_slice_in_dim(total, atom_at * share, share, 0)
    return (row.sum(axis=1) * jnp.float32(-(basis_total ** (-0.5))))[None, :]


def solution(mesh):
    sizes = tuple(mesh.shape[name] for name in ("groups", "aux", "atoms"))
    in_specs = (
        P("atoms", "aux", None, None),
        P(("groups", "atoms"), None),
        P("groups", "atoms"),
        P(),
        P(),
    )
    out_specs = P(("groups", "aux"), "atoms")
    return jax.shard_map(
        functools.partial(on_device, sizes),
        mesh=mesh,
        in_specs=in_specs,
        out_specs=out_specs,
        check_vma=False,
    )
```

time: 85.6 us -> 72 us (0.84)
  waiting for transfers between devices: 34.3 us -> 23.7 us
  Pallas kernels: 13.1 us -> 19.2 us
  starting transfers between devices: 24.7 us -> 19 us
  local copies, waits for them, and re-layouts: 11.6 us -> 8.04 us
    ppermute x19, waiting for transfers between devices: 34.3 us -> 23.7 us  [swap(): return lax.ppermute(x, axes, perm)]
    pallas_call x2, Pallas kernels: 10.7 us -> 16.7 us  [the longest x1 8.74 us: on_device(): pl.pallas_call(first, out_shape=tiles, in_specs=[scalars] * 3 + [anywhere...]
    ppermute x19, starting transfers between devices: 24.7 us -> 19 us  [swap(): return lax.ppermute(x, axes, perm)]
    unnamed x33 -> x29, local copies, waits for them, and re-layouts: 11.6 us -> 8.04 us
  transfers between devices with their start and end apart: 19 -> 19, of which waited for: 10 -> 9; matrix products, arithmetic and copies ran while one was open for 0% -> 0% of each run, Pallas kernels for 4% -> 16%
where the time goes in v3:
time: 72 us; the launch traced here: 71.9 us
  waiting for transfers between devices  23.7 us (33%)
  Pallas kernels  19.2 us (27%)
  starting transfers between devices  19 us (26%)
  local copies, waits for them, and re-layouts  8.04 us (11%)
  between operations  1.3 us (2%)
    ppermute x19, waiting for transfers between devices, swap(): return lax.ppermute(x, axes, perm)  23.7 us
    ppermute x19, starting transfers between devices, swap(): return lax.ppermute(x, axes, perm)  19 us
    pallas_call x1, Pallas kernels, on_device(): pl.pallas_call(first, out_shape=tiles, in_specs=[scalars] * 3 + [anywhere...  8.74 us
    unnamed x29, local copies, waits for them, and re-layouts  8.04 us
    pallas_call x1, Pallas kernels, on_device(): pl.pallas_call(functools.partial(second, len(all_centers)), out_shape=jax...  8 us
    pallas_call x1, Pallas kernels, on_device(): pl.pallas_call(functools.partial(select, n_blocks), out_shape=[jax.ShapeD...  2.43 us
  transfers between devices with their start and end apart: 19, of which 9 were waited for; matrix products, arithmetic and copies ran while one was open for 0% of the time, Pallas kernels for 16%

profile of v3, /device:TPU:0, one launch (start us, length us, event | category | flops | bytes accessed | tf_op | source)
XLA Modules:
  0.0 71.9 jit_solution(12821672684062087234)
XLA Ops:
  0.0 2.9 %collective-permute-start.1 = (bf16[3,512,128]{2,1,0:T(8,128)(2,1)}, bf16[3,512,128]{2,1,0:T(8,128)(2,1)S(1)}, u32[]{:S(2)}, u32[]{:S(2)}) collective-permute-start(bf16[3,512,128]{2,1,0:T(8,128)(2,1)} %bitcast.14), channel_id=1, source_target_pairs={{0,2},{1,3},{2,0},{3,1},{4,6},{5,7},{6,4},{7,5},{8,10},{9,11},{10,... | collective-permute-start | bytes 1179656 | tf_op jit(solution)/shard_map/ppermute | solution.py:29
  2.9 2.6 %collective-permute-start.11 = (bf16[3,512,128]{2,1,0:T(8,128)(2,1)}, bf16[3,512,128]{2,1,0:T(8,128)(2,1)}, u32[]{:S(2)}, u32[]{:S(2)}) collective-permute-start(bf16[3,512,128]{2,1,0:T(8,128)(2,1)} %bitcast.15), channel_id=1, source_target_pairs={{0,8},{4,12},{8,0},{12,4},{16,28},{20,24},{24,20},{28,16},{1,9},{5... | collective-permute-start | bytes 1179656 | tf_op jit(solution)/shard_map/ppermute | solution.py:29
  5.5 1.6 %collective-permute-start.8 = (bf16[3,512,128]{2,1,0:T(8,128)(2,1)}, bf16[3,512,128]{2,1,0:T(8,128)(2,1)S(1)}, u32[]{:S(2)}, u32[]{:S(2)}) collective-permute-start(bf16[3,512,128]{2,1,0:T(8,128)(2,1)} %bitcast.16), channel_id=1, source_target_pairs={{0,4},{4,0},{8,12},{12,8},{1,5},{5,1},{9,13},{13,9},{2,6},{6,2},{1... | collective-permute-start | bytes 1179656 | tf_op jit(solution)/shard_map/ppermute | solution.py:29
  7.1 0.1 pad_add_fusion.where
  7.2 1.6 %copy-done.3 = bf16[512,2048]{1,0:T(8,128)(2,1)S(1)} copy-done((bf16[512,2048]{1,0:T(8,128)(2,1)S(1)}, bf16[512,2048]{1,0:T(8,128)(2,1)}, u32[]{:S(2)}) %copy-start.3) | copy-done | bytes 2097176
  8.8 2.4 %shard_map.55 = (bf16[512,512]{1,0:T(8,128)(2,1)}, bf16[512,512]{1,0:T(8,128)(2,1)S(1)}) custom-call(s32[4]{0:T(128)S(1)} %pad_add_fusion.where, bf16[512,2048]{1,0:T(8,128)(2,1)S(1)} %copy-done.3), custom_call_target="tpu_custom_call" | custom-call | tf_op jit(solution)/shard_map/pallas_call | solution.py:265
  11.2 0.6 collective-permute-start.4
  11.8 0.0 collective-permute-start.3
  11.8 0.4 collective-permute-done.1.refs_6_
  12.3 2.5 %collective-permute-start.10 = (bf16[3,512,128]{2,1,0:T(8,128)(2,1)S(1)}, bf16[3,512,128]{2,1,0:T(8,128)(2,1)S(1)}, u32[]{:S(2)}, u32[]{:S(2)}) collective-permute-start(bf16[3,512,128]{2,1,0:T(8,128)(2,1)S(1)} %collective-permute-done.1.refs_6_), channel_id=1, source_target_pairs={{0,4},{4,0},{8,12},{12,8},{1,5},{5,1},{9,13},{13,9},{2,6},{6,2},{1... | collective-permute-start | bytes 1179656 | tf_op jit(solution)/shard_map/ppermute | solution.py:29
  14.8 8.5 %collective-permute-done.11.refs_16_ = bf16[3,512,128]{2,1,0:T(8,128)(2,1)} collective-permute-done((bf16[3,512,128]{2,1,0:T(8,128)(2,1)}, bf16[3,512,128]{2,1,0:T(8,128)(2,1)}, u32[]{:S(2)}, u32[]{:S(2)}) %collective-permute-start.11) | collective-permute-done | bytes 393248 | tf_op jit(solution)/shard_map/ppermute | solution.py:29
  23.3 0.0 collective-permute-start.6
  23.3 1.4 %collective-permute-done.8.refs_8_.refs_15_ = bf16[3,512,128]{2,1,0:T(8,128)(2,1)S(1)} collective-permute-done((bf16[3,512,128]{2,1,0:T(8,128)(2,1)}, bf16[3,512,128]{2,1,0:T(8,128)(2,1)S(1)}, u32[]{:S(2)}, u32[]{:S(2)}) %collective-permute-start.8) | collective-permute-done | bytes 393248 | tf_op jit(solution)/shard_map/ppermute | solution.py:29
  24.6 0.0 collective-permute-start.7
  24.6 0.0 collective-permute-done.4.refs_2_
  24.7 0.5 collective-permute-start.5
  25.2 6.6 %collective-permute-done.10.refs_10_ = bf16[3,512,128]{2,1,0:T(8,128)(2,1)S(1)} collective-permute-done((bf16[3,512,128]{2,1,0:T(8,128)(2,1)S(1)}, bf16[3,512,128]{2,1,0:T(8,128)(2,1)S(1)}, u32[]{:S(2)}, u32[]{:S(2)}) %collective-permute-start.10) | collective-permute-done | bytes 393248 | tf_op jit(solution)/shard_map/ppermute | solution.py:29
  31.8 0.5 collective-permute-start.2
  32.3 0.8 %copy-done.4 = bf16[3,512,128]{2,1,0:T(8,128)(2,1)} copy-done((bf16[3,512,128]{2,1,0:T(8,128)(2,1)}, bf16[3,512,128]{2,1,0:T(8,128)(2,1)S(1)}, u32[]{:S(2)}) %copy-start.4) | copy-done | bytes 393240
  33.0 0.0 collective-permute-start.9
  33.1 0.8 %copy-done.8 = bf16[512,512]{1,0:T(8,128)(2,1)} copy-done((bf16[512,512]{1,0:T(8,128)(2,1)}, bf16[512,512]{1,0:T(8,128)(2,1)S(1)}, u32[]{:S(2)}) %copy-start.8) | copy-done | bytes 524312
  33.8 0.5 collective-permute-start.12
  34.4 0.8 %copy-done.6 = bf16[3,512,128]{2,1,0:T(8,128)(2,1)} copy-done((bf16[3,512,128]{2,1,0:T(8,128)(2,1)}, bf16[3,512,128]{2,1,0:T(8,128)(2,1)S(1)}, u32[]{:S(2)}) %copy-start.6) | copy-done | bytes 393240
  35.1 2.4 %collective-permute-start.13 = (bf16[3,512,128]{2,1,0:T(8,128)(2,1)}, bf16[3,512,128]{2,1,0:T(8,128)(2,1)}, u32[]{:S(2)}, u32[]{:S(2)}) collective-permute-start(bf16[3,512,128]{2,1,0:T(8,128)(2,1)} %collective-permute-done.11.refs_16_), channel_id=1, source_target_pairs={{0,16},{16,0},{1,17},{17,1},{2,18},{18,2},{3,19},{19,3},{4,20},{20... | collective-permute-start | bytes 1179656 | tf_op jit(solution)/shard_map/ppermute | solution.py:29
  37.5 0.1 copy.7.plist
  37.6 0.0 collective-permute-done.9.refs_9_
  37.6 0.0 collective-permute-start
  37.6 0.0 collective-permute-done.5.refs_3_
  37.6 0.0 copy-start.1
  37.6 1.0 %copy-done.1 = bf16[512,1,3,128]{3,0,2,1:T(8,128)(2,1)S(1)} copy-done((bf16[512,1,3,128]{3,0,2,1:T(8,128)(2,1)S(1)}, bf16[512,1,3,128]{3,0,2,1:T(8,128)(2,1)}, u32[]{:S(2)}) %copy-start.1) | copy-done | bytes 393240
  38.6 1.0 %copy-done.5 = bf16[3,512,128]{2,1,0:T(8,128)(2,1)S(1)} copy-done((bf16[3,512,128]{2,1,0:T(8,128)(2,1)S(1)}, bf16[3,512,128]{2,1,0:T(8,128)(2,1)}, u32[]{:S(2)}) %copy-start.5) | copy-done | bytes 393240
  39.6 1.0 %copy-done.7 = bf16[3,512,128]{2,1,0:T(8,128)(2,1)S(1)} copy-done((bf16[3,512,128]{2,1,0:T(8,128)(2,1)S(1)}, bf16[3,512,128]{2,1,0:T(8,128)(2,1)}, u32[]{:S(2)}) %copy-start.7) | copy-done | bytes 393240
  40.6 1.0 %copy-done.9 = bf16[512,512]{1,0:T(8,128)(2,1)S(1)} copy-done((bf16[512,512]{1,0:T(8,128)(2,1)S(1)}, bf16[512,512]{1,0:T(8,128)(2,1)}, u32[]{:S(2)}) %copy-start.9) | copy-done | bytes 524312
  41.7 8.7 %shard_map.56.refs_13_ = bf16[12,256,128]{2,1,0:T(8,128)(2,1)S(1)} custom-call(s32[4]{0:T(128)S(1)} %pad_add_fusion.where, s32[16,3]{1,0:T(8,128)S(1)} %copy.7.plist, s32[16]{0:T(128)S(1)} %copy-done.12, bf16[512,512]{1,0:T(8,128)(2,1)} %get-tuple-element.12.refs_0_, bf16[512,512]{1,0:T(8,128)(2,1)S(1)} %copy-done.9, ...), custom_call_target="tpu_custom_call" | custom-call | tf_op jit(solution)/shard_map/pallas_call | solution.py:304
  50.4 0.0 collective-permute-done.13.refs_17_
  50.4 0.0 collective-permute-done.2.refs_2_
  50.4 1.4 %collective-permute-start.14 = (bf16[512,512]{1,0:T(8,128)(2,1)}, bf16[512,512]{1,0:T(8,128)(2,1)S(1)}, u32[]{:S(2)}, u32[]{:S(2)}) collective-permute-start(bf16[512,512]{1,0:T(8,128)(2,1)} %collective-permute-done.2.refs_2_), channel_id=1, source_target_pairs={{0,1},{1,0},{2,3},{3,2},{4,5},{5,4},{6,7},{7,6},{8,9},{9,8},{10,11... | collective-permute-start | bytes 1572872 | tf_op jit(solution)/shard_map/ppermute | solution.py:29
  51.8 1.7 %collective-permute-done.14.refs_3_ = bf16[512,512]{1,0:T(8,128)(2,1)S(1)} collective-permute-done((bf16[512,512]{1,0:T(8,128)(2,1)}, bf16[512,512]{1,0:T(8,128)(2,1)S(1)}, u32[]{:S(2)}, u32[]{:S(2)}) %collective-permute-start.14) | collective-permute-done | bytes 524320 | tf_op jit(solution)/shard_map/ppermute | solution.py:29
  53.6 8.0 %shard_map.57 = f32[2,4,128]{2,1,0:T(4,128)S(1)} custom-call(s32[4]{0:T(128)S(1)} %pad_add_fusion.where, s32[16,3]{1,0:T(8,128)S(1)} %copy.7.plist, s32[16]{0:T(128)S(1)} %copy-done.12, bf16[512,512]{1,0:T(8,128)(2,1)S(1)} %copy-done.11, bf16[512,512]{1,0:T(8,128)(2,1)S(1)} %collective-permute-done.refs_1_, bf16[512,512]{1,0:T(8,128)(2,1)} %collective-permute-done.2.refs_2_, ...), custom_call_target="tpu_custom_call" | custom-call | tf_op jit(solution)/shard_map/pallas_call | solution.py:313
  61.6 0.1 collective-permute-start.15
  61.6 1.2 %collective-permute-done.15 = f32[2,4,128]{2,1,0:T(4,128)S(1)} collective-permute-done((f32[2,4,128]{2,1,0:T(4,128)S(1)}, f32[2,4,128]{2,1,0:T(4,128)S(1)}, u32[]{:S(2)}, u32[]{:S(2)}) %collective-permute-start.15) | collective-permute-done | bytes 4128 | tf_op jit(solution)/shard_map/ppermute | solution.py:29
  62.8 0.8 %collective-permute-start.16 = (f32[4,128]{1,0:T(4,128)S(1)}, f32[4,128]{1,0:T(4,128)S(1)}, u32[]{:S(2)}, u32[]{:S(2)}) collective-permute-start(f32[4,128]{1,0:T(4,128)S(1)} %get-tuple-element.15), channel_id=1, source_target_pairs={{0,2},{1,3},{2,0},{3,1},{4,6},{5,7},{6,4},{7,5},{8,10},{9,11},{10,... | collective-permute-start | bytes 6152 | tf_op jit(solution)/shard_map/ppermute | solution.py:29
  63.6 2.1 %collective-permute-start.17 = (f32[4,128]{1,0:T(4,128)S(1)}, f32[4,128]{1,0:T(4,128)S(1)}, u32[]{:S(2)}, u32[]{:S(2)}) collective-permute-start(f32[4,128]{1,0:T(4,128)S(1)} %get-tuple-element.16), channel_id=1, source_target_pairs={{0,4},{4,0},{8,12},{12,8},{1,5},{5,1},{9,13},{13,9},{2,6},{6,2},{1... | collective-permute-start | bytes 6152 | tf_op jit(solution)/shard_map/ppermute | solution.py:29
  65.6 0.7 collective-permute-start.18
  66.3 0.1 collective-permute-done.16
  66.4 0.8 %collective-permute-done.17 = f32[4,128]{1,0:T(4,128)S(1)} collective-permute-done((f32[4,128]{1,0:T(4,128)S(1)}, f32[4,128]{1,0:T(4,128)S(1)}, u32[]{:S(2)}, u32[]{:S(2)}) %collective-permute-start.17) | collective-permute-done | bytes 2080 | tf_op jit(solution)/shard_map/ppermute | solution.py:29
  67.2 2.9 %collective-permute-done.18 = f32[4,128]{1,0:T(4,128)S(1)} collective-permute-done((f32[4,128]{1,0:T(4,128)S(1)}, f32[4,128]{1,0:T(4,128)S(1)}, u32[]{:S(2)}, u32[]{:S(2)}) %collective-permute-start.18) | collective-permute-done | bytes 2080 | tf_op jit(solution)/shard_map/ppermute | solution.py:29
  70.1 0.6 dynamic-slice_reduce_fusion
  (27 shorter events, 0.1 us)
Async XLA Ops:
  0.0 37.6 %copy-start = (bf16[2048,512]{1,0:T(8,128)(2,1)S(1)}, bf16[2048,512]{1,0:T(8,128)(2,1)}, u32[]{:S(2)}) copy-start(bf16[2048,512]{1,0:T(8,128)(2,1)} %refs_12_.3) | copy-start | bytes 6291460
  0.0 12.3 %collective-permute-start.1 = (bf16[3,512,128]{2,1,0:T(8,128)(2,1)}, bf16[3,512,128]{2,1,0:T(8,128)(2,1)S(1)}, u32[]{:S(2)}, u32[]{:S(2)}) collective-permute-start(bf16[3,512,128]{2,1,0:T(8,128)(2,1)} %bitcast.14), channel_id=1, source_target_pairs={{0,2},{1,3},{2,0},{3,1},{4,6},{5,7},{6,4},{7,5},{8,10},{9,11},{10,... | collective-permute-start | bytes 1179656 | tf_op jit(solution)/shard_map/ppermute | solution.py:29
  2.9 20.3 %collective-permute-start.11 = (bf16[3,512,128]{2,1,0:T(8,128)(2,1)}, bf16[3,512,128]{2,1,0:T(8,128)(2,1)}, u32[]{:S(2)}, u32[]{:S(2)}) collective-permute-start(bf16[3,512,128]{2,1,0:T(8,128)(2,1)} %bitcast.15), channel_id=1, source_target_pairs={{0,8},{4,12},{8,0},{12,4},{16,28},{20,24},{24,20},{28,16},{1,9},{5... | collective-permute-start | bytes 1179656 | tf_op jit(solution)/shard_map/ppermute | solution.py:29
  5.5 19.1 %collective-permute-start.8 = (bf16[3,512,128]{2,1,0:T(8,128)(2,1)}, bf16[3,512,128]{2,1,0:T(8,128)(2,1)S(1)}, u32[]{:S(2)}, u32[]{:S(2)}) collective-permute-start(bf16[3,512,128]{2,1,0:T(8,128)(2,1)} %bitcast.16), channel_id=1, source_target_pairs={{0,4},{4,0},{8,12},{12,8},{1,5},{5,1},{9,13},{13,9},{2,6},{6,2},{1... | collective-permute-start | bytes 1179656 | tf_op jit(solution)/shard_map/ppermute | solution.py:29
  7.2 1.6 %copy-start.3 = (bf16[512,2048]{1,0:T(8,128)(2,1)S(1)}, bf16[512,2048]{1,0:T(8,128)(2,1)}, u32[]{:S(2)}) copy-start(bf16[512,2048]{1,0:T(8,128)(2,1)} %virt_ref.1) | copy-start | bytes 6291460
  8.8 28.7 %copy-start.13 = (s32[16,3]{0,1:T(4,128)S(1)}, s32[16,3]{0,1:T(4,128)}, u32[]{:S(2)}) copy-start(s32[16,3]{0,1:T(4,128)} %param.8) | copy-start | bytes 580
  8.8 28.8 %copy-start.12 = (s32[16]{0:T(128)S(1)}, s32[16]{0:T(128)}, u32[]{:S(2)}) copy-start(s32[16]{0:T(128)} %pcount.3) | copy-start | bytes 196
  11.2 23.1 %copy-start.10 = (bf16[512,512]{1,0:T(8,128)(2,1)}, bf16[512,512]{1,0:T(8,128)(2,1)S(1)}, u32[]{:S(2)}) copy-start(bf16[512,512]{1,0:T(8,128)(2,1)S(1)} %get-tuple-element.10.refs_0_) | copy-start | bytes 1572868
  11.2 13.4 %collective-permute-start.4 = (bf16[512,512]{1,0:T(8,128)(2,1)S(1)}, bf16[512,512]{1,0:T(8,128)(2,1)}, u32[]{:S(2)}, u32[]{:S(2)}) collective-permute-start(bf16[512,512]{1,0:T(8,128)(2,1)S(1)} %get-tuple-element.10.refs_0_), channel_id=1, source_target_pairs={{0,2},{1,3},{2,0},{3,1},{4,6},{5,7},{6,4},{7,5},{8,10},{9,11},{10,... | collective-permute-start | bytes 1572872 | tf_op jit(solution)/shard_map/ppermute | solution.py:29
  11.8 21.2 %collective-permute-start.3 = (bf16[512,512]{1,0:T(8,128)(2,1)}, bf16[512,512]{1,0:T(8,128)(2,1)S(1)}, u32[]{:S(2)}, u32[]{:S(2)}) collective-permute-start(bf16[512,512]{1,0:T(8,128)(2,1)} %get-tuple-element.12.refs_0_), channel_id=1, source_target_pairs={{0,1},{1,0},{2,3},{3,2},{4,5},{5,4},{6,7},{7,6},{8,9},{9,8},{10,11... | collective-permute-start | bytes 1572872 | tf_op jit(solution)/shard_map/ppermute | solution.py:29
  12.3 19.5 %collective-permute-start.10 = (bf16[3,512,128]{2,1,0:T(8,128)(2,1)S(1)}, bf16[3,512,128]{2,1,0:T(8,128)(2,1)S(1)}, u32[]{:S(2)}, u32[]{:S(2)}) collective-permute-start(bf16[3,512,128]{2,1,0:T(8,128)(2,1)S(1)} %collective-permute-done.1.refs_6_), channel_id=1, source_target_pairs={{0,4},{4,0},{8,12},{12,8},{1,5},{5,1},{9,13},{13,9},{2,6},{6,2},{1... | collective-permute-start | bytes 1179656 | tf_op jit(solution)/shard_map/ppermute | solution.py:29
  23.3 9.0 %collective-permute-start.6 = (bf16[3,512,128]{2,1,0:T(8,128)(2,1)}, bf16[3,512,128]{2,1,0:T(8,128)(2,1)S(1)}, u32[]{:S(2)}, u32[]{:S(2)}) collective-permute-start(bf16[3,512,128]{2,1,0:T(8,128)(2,1)} %bitcast.17), channel_id=1, source_target_pairs={{0,1},{1,0},{2,3},{3,2},{4,5},{5,4},{6,7},{7,6},{8,9},{9,8},{10,11... | collective-permute-start | bytes 1179656 | tf_op jit(solution)/shard_map/ppermute | solution.py:29
  24.6 9.7 %collective-permute-start.7 = (bf16[3,512,128]{2,1,0:T(8,128)(2,1)S(1)}, bf16[3,512,128]{2,1,0:T(8,128)(2,1)S(1)}, u32[]{:S(2)}, u32[]{:S(2)}) collective-permute-start(bf16[3,512,128]{2,1,0:T(8,128)(2,1)S(1)} %collective-permute-done.1.refs_6_), channel_id=1, source_target_pairs={{0,1},{1,0},{2,3},{3,2},{4,5},{5,4},{6,7},{7,6},{8,9},{9,8},{10,11... | collective-permute-start | bytes 1179656 | tf_op jit(solution)/shard_map/ppermute | solution.py:29
  24.7 12.9 %collective-permute-start.5 = (bf16[512,512]{1,0:T(8,128)(2,1)}, bf16[512,512]{1,0:T(8,128)(2,1)}, u32[]{:S(2)}, u32[]{:S(2)}) collective-permute-start(bf16[512,512]{1,0:T(8,128)(2,1)} %collective-permute-done.4.refs_2_), channel_id=1, source_target_pairs={{0,1},{1,0},{2,3},{3,2},{4,5},{5,4},{6,7},{7,6},{8,9},{9,8},{10,11... | collective-permute-start | bytes 1572872 | tf_op jit(solution)/shard_map/ppermute | solution.py:29
  31.8 18.6 %collective-permute-start.2 = (bf16[512,512]{1,0:T(8,128)(2,1)}, bf16[512,512]{1,0:T(8,128)(2,1)}, u32[]{:S(2)}, u32[]{:S(2)}) collective-permute-start(bf16[512,512]{1,0:T(8,128)(2,1)} %get-tuple-element.12.refs_0_), channel_id=1, source_target_pairs={{0,2},{1,3},{2,0},{3,1},{4,6},{5,7},{6,4},{7,5},{8,10},{9,11},{10,... | collective-permute-start | bytes 1572872 | tf_op jit(solution)/shard_map/ppermute | solution.py:29
  32.3 0.8 %copy-start.4 = (bf16[3,512,128]{2,1,0:T(8,128)(2,1)}, bf16[3,512,128]{2,1,0:T(8,128)(2,1)S(1)}, u32[]{:S(2)}) copy-start(bf16[3,512,128]{2,1,0:T(8,128)(2,1)S(1)} %collective-permute-done.6.refs_5_) | copy-start | bytes 1179652
  33.0 4.5 %collective-permute-start.9 = (bf16[3,512,128]{2,1,0:T(8,128)(2,1)S(1)}, bf16[3,512,128]{2,1,0:T(8,128)(2,1)}, u32[]{:S(2)}, u32[]{:S(2)}) collective-permute-start(bf16[3,512,128]{2,1,0:T(8,128)(2,1)S(1)} %collective-permute-done.8.refs_8_.refs_15_), channel_id=1, source_target_pairs={{0,1},{1,0},{2,3},{3,2},{4,5},{5,4},{6,7},{7,6},{8,9},{9,8},{10,11... | collective-permute-start | bytes 1179656 | tf_op jit(solution)/shard_map/ppermute | solution.py:29
  33.0 0.8 %copy-start.8 = (bf16[512,512]{1,0:T(8,128)(2,1)}, bf16[512,512]{1,0:T(8,128)(2,1)S(1)}, u32[]{:S(2)}) copy-start(bf16[512,512]{1,0:T(8,128)(2,1)S(1)} %collective-permute-done.3.refs_1_) | copy-start | bytes 1572868
  33.8 3.7 %collective-permute-start.12 = (bf16[3,512,128]{2,1,0:T(8,128)(2,1)S(1)}, bf16[3,512,128]{2,1,0:T(8,128)(2,1)}, u32[]{:S(2)}, u32[]{:S(2)}) collective-permute-start(bf16[3,512,128]{2,1,0:T(8,128)(2,1)S(1)} %collective-permute-done.10.refs_10_), channel_id=1, source_target_pairs={{0,1},{1,0},{2,3},{3,2},{4,5},{5,4},{6,7},{7,6},{8,9},{9,8},{10,11... | collective-permute-start | bytes 1179656 | tf_op jit(solution)/shard_map/ppermute | solution.py:29
  34.4 0.8 %copy-start.6 = (bf16[3,512,128]{2,1,0:T(8,128)(2,1)}, bf16[3,512,128]{2,1,0:T(8,128)(2,1)S(1)}, u32[]{:S(2)}) copy-start(bf16[3,512,128]{2,1,0:T(8,128)(2,1)S(1)} %collective-permute-done.7.refs_7_) | copy-start | bytes 1179652
  35.1 15.3 %collective-permute-start.13 = (bf16[3,512,128]{2,1,0:T(8,128)(2,1)}, bf16[3,512,128]{2,1,0:T(8,128)(2,1)}, u32[]{:S(2)}, u32[]{:S(2)}) collective-permute-start(bf16[3,512,128]{2,1,0:T(8,128)(2,1)} %collective-permute-done.11.refs_16_), channel_id=1, source_target_pairs={{0,16},{16,0},{1,17},{17,1},{2,18},{18,2},{3,19},{19,3},{4,20},{20... | collective-permute-start | bytes 1179656 | tf_op jit(solution)/shard_map/ppermute | solution.py:29
  37.6 14.2 %collective-permute-start = (bf16[512,512]{1,0:T(8,128)(2,1)}, bf16[512,512]{1,0:T(8,128)(2,1)S(1)}, u32[]{:S(2)}, u32[]{:S(2)}) collective-permute-start(bf16[512,512]{1,0:T(8,128)(2,1)} %copy-done.10), channel_id=1, source_target_pairs={{0,1},{1,0},{2,3},{3,2},{4,5},{5,4},{6,7},{7,6},{8,9},{9,8},{10,11... | collective-permute-start | bytes 1572872 | tf_op jit(solution)/shard_map/ppermute | solution.py:29
  37.6 1.0 %copy-start.1 = (bf16[512,1,3,128]{3,0,2,1:T(8,128)(2,1)S(1)}, bf16[512,1,3,128]{3,0,2,1:T(8,128)(2,1)}, u32[]{:S(2)}) copy-start(bf16[512,1,3,128]{3,0,2,1:T(8,128)(2,1)} %param.5) | copy-start | bytes 1179652
  38.6 1.0 %copy-start.5 = (bf16[3,512,128]{2,1,0:T(8,128)(2,1)S(1)}, bf16[3,512,128]{2,1,0:T(8,128)(2,1)}, u32[]{:S(2)}) copy-start(bf16[3,512,128]{2,1,0:T(8,128)(2,1)} %copy-done.4) | copy-start | bytes 1179652
  39.6 1.0 %copy-start.7 = (bf16[3,512,128]{2,1,0:T(8,128)(2,1)S(1)}, bf16[3,512,128]{2,1,0:T(8,128)(2,1)}, u32[]{:S(2)}) copy-start(bf16[3,512,128]{2,1,0:T(8,128)(2,1)} %copy-done.6) | copy-start | bytes 1179652
  40.6 1.0 %copy-start.9 = (bf16[512,512]{1,0:T(8,128)(2,1)S(1)}, bf16[512,512]{1,0:T(8,128)(2,1)}, u32[]{:S(2)}) copy-start(bf16[512,512]{1,0:T(8,128)(2,1)} %copy-done.8) | copy-start | bytes 1572868
  41.7 11.9 %copy-start.2 = (bf16[512,1,3,128]{3,0,2,1:T(8,128)(2,1)S(1)}, bf16[512,1,3,128]{3,0,2,1:T(8,128)(2,1)}, u32[]{:S(2)}) copy-start(bf16[512,1,3,128]{3,0,2,1:T(8,128)(2,1)} %param.5) | copy-start | bytes 1179652
  41.7 11.9 %copy-start.11 = (bf16[512,512]{1,0:T(8,128)(2,1)S(1)}, bf16[512,512]{1,0:T(8,128)(2,1)}, u32[]{:S(2)}) copy-start(bf16[512,512]{1,0:T(8,128)(2,1)} %copy-done.10) | copy-start | bytes 1572868
  50.4 3.1 %collective-permute-start.14 = (bf16[512,512]{1,0:T(8,128)(2,1)}, bf16[512,512]{1,0:T(8,128)(2,1)S(1)}, u32[]{:S(2)}, u32[]{:S(2)}) collective-permute-start(bf16[512,512]{1,0:T(8,128)(2,1)} %collective-permute-done.2.refs_2_), channel_id=1, source_target_pairs={{0,1},{1,0},{2,3},{3,2},{4,5},{5,4},{6,7},{7,6},{8,9},{9,8},{10,11... | collective-permute-start | bytes 1572872 | tf_op jit(solution)/shard_map/ppermute | solution.py:29
  61.6 1.2 %collective-permute-start.15 = (f32[2,4,128]{2,1,0:T(4,128)S(1)}, f32[2,4,128]{2,1,0:T(4,128)S(1)}, u32[]{:S(2)}, u32[]{:S(2)}) collective-permute-start(f32[2,4,128]{2,1,0:T(4,128)S(1)} %shard_map.57), channel_id=1, source_target_pairs={{0,1},{1,0},{2,3},{3,2},{4,5},{5,4},{6,7},{7,6},{8,9},{9,8},{10,11... | collective-permute-start | bytes 12296 | tf_op jit(solution)/shard_map/ppermute | solution.py:29
  62.8 3.6 %collective-permute-start.16 = (f32[4,128]{1,0:T(4,128)S(1)}, f32[4,128]{1,0:T(4,128)S(1)}, u32[]{:S(2)}, u32[]{:S(2)}) collective-permute-start(f32[4,128]{1,0:T(4,128)S(1)} %get-tuple-element.15), channel_id=1, source_target_pairs={{0,2},{1,3},{2,0},{3,1},{4,6},{5,7},{6,4},{7,5},{8,10},{9,11},{10,... | collective-permute-start | bytes 6152 | tf_op jit(solution)/shard_map/ppermute | solution.py:29
  63.6 3.6 %collective-permute-start.17 = (f32[4,128]{1,0:T(4,128)S(1)}, f32[4,128]{1,0:T(4,128)S(1)}, u32[]{:S(2)}, u32[]{:S(2)}) collective-permute-start(f32[4,128]{1,0:T(4,128)S(1)} %get-tuple-element.16), channel_id=1, source_target_pairs={{0,4},{4,0},{8,12},{12,8},{1,5},{5,1},{9,13},{13,9},{2,6},{6,2},{1... | collective-permute-start | bytes 6152 | tf_op jit(solution)/shard_map/ppermute | solution.py:29
  65.6 4.5 %collective-permute-start.18 = (f32[4,128]{1,0:T(4,128)S(1)}, f32[4,128]{1,0:T(4,128)S(1)}, u32[]{:S(2)}, u32[]{:S(2)}) collective-permute-start(f32[4,128]{1,0:T(4,128)S(1)} %get-tuple-element.16), channel_id=1, source_target_pairs={{0,6},{1,7},{2,4},{3,5},{4,2},{5,3},{6,0},{7,1},{8,14},{9,15},{10,... | collective-permute-start | bytes 6152 | tf_op jit(solution)/shard_map/ppermute | solution.py:29

commit v4 on v0

v4 whole, which is shorter than its diff:
```python
import functools

import jax
import jax.numpy as jnp
from jax import lax
from jax.experimental import pallas as pl
from jax.experimental.pallas import tpu as pltpu
from jax.sharding import PartitionSpec as P

BS = 128
KN = 3
MIB = 1 << 20


def swap(x, axes, sizes, move):
    perm = []
    total = 1
    for size in sizes:
        total *= size
    for source in range(total):
        coords, rest = [], source
        for size in reversed(sizes):
            coords.append(rest % size)
            rest //= size
        target = 0
        for size, at in zip(sizes, move(*reversed(coords))):
            target = target * size + at
        perm.append((source, target))
    return lax.ppermute(x, axes, perm)


def select(n_blocks, where, virt_ref, out_ref, buf, sem):
    def copy(i):
        columns = pl.ds(pl.multiple_of((2 * i + where[1]) * BS, BS), BS)
        return pltpu.make_async_copy(virt_ref.at[:, columns], buf.at[i], sem.at[i])

    for i in range(n_blocks):
        copy(i).start()
    for i in range(n_blocks):
        copy(i).wait()
        out_ref[i * BS : (i + 1) * BS, :] = buf[i].T


def after(x, *others):
    return lax.optimization_barrier((x,) + others)[0]


def contract(n_centers, where, plist, pcount, *refs):
    v_refs, m_refs, occ_ref, c_refs = refs[0:4], refs[4:12], refs[12], refs[13 : 13 + n_centers]
    out_ref = refs[13 + n_centers]
    vbuf, mbuf, obuf, cbuf, prod, acc, listed, place, vsem, msem, osem, csem = refs[
        14 + n_centers :
    ]
    own, parity, plane, aux_at = where[0], where[1], where[2], where[3]
    basis = mbuf.shape[2]
    n_q, _, rows, _ = cbuf.shape
    blocks_here = rows // BS
    n_places = vbuf.shape[0]
    slots = [(b, k) for b in range(blocks_here) for k in range(KN)]

    def used(b, k):
        block = own * blocks_here + b
        return (k < pcount[block]) & ((plist[block, k] & 1) == parity)

    def column(b, k):
        return plist[own * blocks_here + b, k] >> 1

    for c in range(n_places):
        place[c] = -1
    count = jnp.int32(0)
    for k in range(KN):
        for b in range(blocks_here):
            c = column(b, k)
            new = used(b, k) & (place[c] < 0)

            @pl.when(new)
            def _(c=c, count=count):
                place[c] = count
                listed[count] = c

            count = count + new.astype(jnp.int32)

    @pl.when((count & 1) == 1)
    def _():
        listed[count] = listed[count - 1]

    groups = (count + 1) >> 1

    def v_copies(at):
        row = pl.ds(pl.multiple_of(listed[at] * BS, BS), BS)
        return [
            pltpu.make_async_copy(v_refs[i].at[row], vbuf.at[at, own ^ i], vsem.at[at, i])
            for i in range(4)
        ]

    def m_copies():
        out = []
        for i in range(8):
            span = pl.ds(pl.multiple_of((own ^ (i % 4)) * rows, rows), rows)
            out.append(pltpu.make_async_copy(m_refs[i], mbuf.at[i // 4, :, span], msem.at[i]))
        return out

    o_copy = pltpu.make_async_copy(occ_ref, obuf, osem)
    if n_centers == 1:
        c_copies = [pltpu.make_async_copy(c_refs[0], cbuf, csem.at[0])]
    else:
        steps = [0, 1, 2 | plane, 3 ^ plane]
        c_copies = [
            pltpu.make_async_copy(c_refs[i], cbuf.at[aux_at ^ steps[i]], csem.at[i])
            for i in range(n_centers)
        ]

    for copy in v_copies(0) + v_copies(1) + m_copies():
        copy.start()
    for g in range(1, n_places // 2):

        @pl.when(g < groups)
        def _(g=g):
            for copy in v_copies(2 * g) + v_copies(2 * g + 1):
                copy.start()

    o_copy.start()
    for copy in c_copies:
        copy.start()
    acc[...] = jnp.zeros_like(acc)
    for copy in m_copies():
        copy.wait()

    def one_group(g, carry):
        for copy in v_copies(2 * g) + v_copies(2 * g + 1):
            copy.wait()

        def four_blocks(i, carry):
            for j in range(4):
                block = 4 * i + j
                span = pl.ds(pl.multiple_of(block * BS, BS), BS)
                weights, parts = [], []
                for k in range(KN):
                    p = plist[block, k]
                    at = pl.ds(pl.multiple_of((p & 3) * BS, BS), BS)
                    parts.append(
                        jnp.concatenate([vbuf[2 * g + h, p >> 2, :, at] for h in range(2)], axis=0)
                    )
                    weight = jnp.concatenate([mbuf[s, k, span, :] for s in range(2)], axis=0)
                    if k > 0:
                        weight = jnp.where(k < pcount[block], weight, jnp.zeros_like(weight))
                    weights.append(weight)
                res = lax.dot_general(
                    jnp.concatenate(parts, axis=1),
                    jnp.concatenate(weights, axis=1),
                    (((1,), (1,)), ((), ())),
                    preferred_element_type=jnp.float32,
                ).astype(jnp.bfloat16)
                for s in range(2):
                    for h in range(2):
                        prod[2 * g + h, s * BS : (s + 1) * BS, span] = res[
                            h * BS : (h + 1) * BS, s * BS : (s + 1) * BS
                        ]
            return carry

        lax.fori_loop(0, basis // (4 * BS), four_blocks, 0)
        return carry

    lax.fori_loop(0, groups, one_group, 0)
    o_copy.wait()
    for copy in c_copies:
        copy.wait()

    for b, k in slots:

        @pl.when(used(b, k))
        def _(b=b, k=k):
            left = jnp.dot(
                prod[place[column(b, k)]],
                obuf[:, b * BS : (b + 1) * BS],
                preferred_element_type=jnp.float32,
            )
            left = left.astype(jnp.bfloat16).astype(jnp.float32)
            left = [left[s * BS : (s + 1) * BS, :].T for s in range(2)]

            def add(q, carry):
                center = cbuf[q, k, b * BS : (b + 1) * BS, :].astype(jnp.float32)
                for s in range(2):
                    acc[s, q] += (left[s] * center).reshape(BS // 8, 8, BS).sum(axis=0)
                return carry

            lax.fori_loop(0, n_q, add, 0, unroll=n_q <= 8)

    for s in range(2):
        out_ref[s] = acc[s].sum(axis=1)


def on_device(sizes, three_center, virt_density, occ_density, partner_list, partner_count):
    groups, aux, atoms = sizes
    rows = three_center.shape[0]
    basis_total = virt_density.shape[1]
    group_at = lax.axis_index("groups")
    aux_at = lax.axis_index("aux")
    atom_at = lax.axis_index("atoms")
    where = jnp.stack([atom_at, aux_at & 1, group_at, aux_at]).astype(jnp.int32)
    columns = basis_total // 2
    n_blocks = columns // BS

    core = functools.partial(swap, axes=("atoms",), sizes=(atoms,), move=lambda t: (t ^ 1,))
    across = functools.partial(swap, axes=("atoms",), sizes=(atoms,), move=lambda t: (t ^ 2,))
    plane = functools.partial(swap, axes=("groups",), sizes=(groups,), move=lambda g: (g ^ 1,))
    pair = functools.partial(swap, axes=("aux",), sizes=(aux,), move=lambda a: (a ^ 1,))

    anywhere = pl.BlockSpec(memory_space=pltpu.HBM)
    scalars = pl.BlockSpec(memory_space=pltpu.SMEM)
    vmem = pl.BlockSpec(memory_space=pltpu.VMEM)

    centers = three_center[:, 0].transpose(1, 0, 2)
    far_a = across(centers)
    other = pair(centers)
    mine = pl.pallas_call(
        functools.partial(select, n_blocks),
        out_shape=jax.ShapeDtypeStruct((columns, rows), jnp.bfloat16),
        in_specs=[scalars, anywhere],
        out_specs=vmem,
        scratch_shapes=[
            pltpu.VMEM((n_blocks, rows, BS), jnp.bfloat16),
            pltpu.SemaphoreType.DMA((n_blocks,)),
        ],
        compiler_params=pltpu.CompilerParams(vmem_limit_bytes=8 * MIB),
    )(where, virt_density)
    v_across = across(mine)
    far_b = pair(after(far_a, other))
    if aux == 4:
        rest_a = swap(centers, ("groups", "aux"), (groups, aux), lambda g, a: (g, a ^ (2 | g)))
        rest_b = plane(rest_a)
        all_centers = [centers, other, rest_a, rest_b]
    else:
        all_centers = [lax.all_gather(centers, "aux", axis=0)]

    m_parts = [centers, core(centers), far_a, core(far_a), other, core(other), far_b]
    m_parts.append(core(far_b))
    v_parts = [mine, core(mine), v_across, core(after(v_across, *m_parts[1:], all_centers[-1]))]

    sums = pl.pallas_call(
        functools.partial(contract, len(all_centers)),
        out_shape=jax.ShapeDtypeStruct((2, aux, BS), jnp.float32),
        in_specs=[scalars] * 3 + [anywhere] * (13 + len(all_centers)),
        out_specs=vmem,
        scratch_shapes=[
            pltpu.VMEM((n_blocks, 4, BS, rows), jnp.bfloat16),
            pltpu.VMEM((2, KN, basis_total, BS), jnp.bfloat16),
            pltpu.VMEM((basis_total, rows), jnp.bfloat16),
            pltpu.VMEM((aux, KN, rows, BS), jnp.bfloat16),
            pltpu.VMEM((n_blocks, 2 * BS, basis_total), jnp.bfloat16),
            pltpu.VMEM((2, aux, 8, BS), jnp.float32),
            pltpu.SMEM((n_blocks,), jnp.int32),
            pltpu.SMEM((n_blocks,), jnp.int32),
            pltpu.SemaphoreType.DMA((n_blocks, 4)),
            pltpu.SemaphoreType.DMA((8,)),
            pltpu.SemaphoreType.DMA,
            pltpu.SemaphoreType.DMA((4,)),
        ],
        compiler_params=pltpu.CompilerParams(vmem_limit_bytes=58 * MIB),
    )(where, partner_list, partner_count, *v_parts, *m_parts, occ_density, *all_centers)

    sums = sums + core(sums)
    diagonal = swap(sums[1], ("aux", "atoms"), (aux, atoms), lambda a, t: (a ^ 1, t ^ 2))
    total = sums[0] + across(sums[0]) + pair(sums[1]) + diagonal
    share = aux // atoms
    row = lax.dynamic_slice_in_dim(total, atom_at * share, share, 0)
    return (row.sum(axis=1) * jnp.float32(-(basis_total ** (-0.5))))[None, :]


def solution(mesh):
    sizes = tuple(mesh.shape[name] for name in ("groups", "aux", "atoms"))
    in_specs = (
        P("atoms", "aux", None, None),
        P(("groups", "atoms"), None),
        P("groups", "atoms"),
        P(),
        P(),
    )
    out_specs = P(("groups", "aux"), "atoms")
    return jax.shard_map(
        functools.partial(on_device, sizes),
        mesh=mesh,
        in_specs=in_specs,
        out_specs=out_specs,
        check_vma=False,
    )
```

time: 228 us -> 68 us (0.30)
  waiting for transfers between devices: 120 us -> 35.7 us
  local copies, waits for them, and re-layouts: 52.7 us -> 3.16 us
  blocking collectives: 15.8 us -> 0 us
  Pallas kernels: 0 us -> 12.5 us
  between operations: 13.6 us -> 1.33 us
  matrix products: 10.8 us -> 0 us
  starting transfers between devices: 9.24 us -> 13.9 us
  other arithmetic: 5.04 us -> 1.36 us
    all_gather x2 -> x0, waiting for transfers between devices: 108 us -> none  [the longest x1 59.3 us: on_device(): full_virt = lax.all_gather(virt_density, 'atoms', axis=0, tiled=True)]
    ppermute x0 -> x16, waiting for transfers between devices: none -> 35.7 us  [swap(): return lax.ppermute(x, axes, perm)]
    gather x3 -> x0, local copies, waits for them, and re-layouts: 24 us -> none  [the longest x2 16.4 us: on_device(): jnp.take(shard_rows.reshape(count_rows, aux_local, block_total, BS), own_...]
    reshape x4 -> x0, local copies, waits for them, and re-layouts: 19.6 us -> none  [the longest x1 12.3 us: on_device(): shard_rows.reshape(count_rows, aux_local, block_total, BS)]
    unnamed x2 -> x0, blocking collectives: 15.8 us -> none
    ppermute x0 -> x16, starting transfers between devices: none -> 13.9 us  [swap(): return lax.ppermute(x, axes, perm)]
    pallas_call x0 -> x2, Pallas kernels: none -> 12.5 us  [the longest x1 10.9 us: on_device(): pl.pallas_call(functools.partial(contract, len(all_centers)), out_shape=j...]
    dot_general x3 -> x0, matrix products: 10.8 us -> none  [the longest x1 5.52 us: on_device(): jnp.einsum('brpkn,bknc->brpc', masked, picked, preferred_element_type=jnp...]
  transfers between devices with their start and end apart: 4 -> 16, of which waited for: 3 -> 9; matrix products, arithmetic and copies ran while one was open for 21% -> 1% of each run, Pallas kernels for 0% -> 2%
where the time goes in v4:
time: 68 us
  waiting for transfers between devices  35.7 us (53%)
  starting transfers between devices  13.9 us (20%)
  Pallas kernels  12.5 us (18%)
  local copies, waits for them, and re-layouts  3.16 us (5%)
  other arithmetic  1.36 us (2%)
  between operations  1.33 us (2%)
    ppermute x16, waiting for transfers between devices, swap(): return lax.ppermute(x, axes, perm)  35.7 us
    ppermute x16, starting transfers between devices, swap(): return lax.ppermute(x, axes, perm)  13.9 us
    pallas_call x1, Pallas kernels, on_device(): pl.pallas_call(functools.partial(contract, len(all_centers)), out_shape=j...  10.9 us
    unnamed x31, local copies, waits for them, and re-layouts  3.15 us
    pallas_call x1, Pallas kernels, on_device(): pl.pallas_call(functools.partial(select, n_blocks), out_shape=jax.ShapeDt...  1.64 us
  transfers between devices with their start and end apart: 16, of which 9 were waited for; matrix products, arithmetic and copies ran while one was open for 1% of the time, Pallas kernels for 2%

profile of v4, /device:TPU:0, one launch (start us, length us, event | category | flops | bytes accessed | tf_op | source)
XLA Modules:
  0.0 68.0 jit_solution(12651368168733954354)
XLA Ops:
  0.0 2.9 %collective-permute-start.3 = (bf16[3,512,128]{2,1,0:T(8,128)(2,1)}, bf16[3,512,128]{2,1,0:T(8,128)(2,1)S(1)}, u32[]{:S(2)}, u32[]{:S(2)}) collective-permute-start(bf16[3,512,128]{2,1,0:T(8,128)(2,1)} %bitcast.14), channel_id=1, source_target_pairs={{0,2},{1,3},{2,0},{3,1},{4,6},{5,7},{6,4},{7,5},{8,10},{9,11},{10,... | collective-permute-start | bytes 1179656 | tf_op jit(solution)/shard_map/ppermute | solution.py:29
  2.9 1.6 %collective-permute-start.5 = (bf16[3,512,128]{2,1,0:T(8,128)(2,1)}, bf16[3,512,128]{2,1,0:T(8,128)(2,1)S(1)}, u32[]{:S(2)}, u32[]{:S(2)}) collective-permute-start(bf16[3,512,128]{2,1,0:T(8,128)(2,1)} %bitcast.15), channel_id=1, source_target_pairs={{0,4},{4,0},{8,12},{12,8},{1,5},{5,1},{9,13},{13,9},{2,6},{6,2},{1... | collective-permute-start | bytes 1179656 | tf_op jit(solution)/shard_map/ppermute | solution.py:29
  4.5 0.1 pad_add_fusion.where
  4.6 1.6 %copy-done.1 = bf16[512,2048]{1,0:T(8,128)(2,1)S(1)} copy-done((bf16[512,2048]{1,0:T(8,128)(2,1)S(1)}, bf16[512,2048]{1,0:T(8,128)(2,1)}, u32[]{:S(2)}) %copy-start.1) | copy-done | bytes 2097176
  6.2 1.6 %shard_map.55.refs_0_ = bf16[1024,512]{1,0:T(8,128)(2,1)S(1)} custom-call(s32[4]{0:T(128)S(1)} %pad_add_fusion.where, bf16[512,2048]{1,0:T(8,128)(2,1)S(1)} %copy-done.1), custom_call_target="tpu_custom_call" | custom-call | tf_op jit(solution)/shard_map/pallas_call | solution.py:216
  7.8 0.0 copy-start
  7.9 0.6 collective-permute-start.1
  8.5 0.0 copy-done.3
  8.5 2.6 %collective-permute-start.9 = (bf16[3,512,128]{2,1,0:T(8,128)(2,1)S(1)}, bf16[3,512,128]{2,1,0:T(8,128)(2,1)S(1)}, u32[]{:S(2)}, u32[]{:S(2)}) collective-permute-start(bf16[3,512,128]{2,1,0:T(8,128)(2,1)S(1)} %bitcast.18), channel_id=1, source_target_pairs={{0,8},{4,12},{8,0},{12,4},{16,28},{20,24},{24,20},{28,16},{1,9},{5... | collective-permute-start | bytes 1179656 | tf_op jit(solution)/shard_map/ppermute | solution.py:29
  11.0 0.0 collective-permute-start.2
  11.0 2.0 %collective-permute-done.3.refs_6_ = bf16[3,512,128]{2,1,0:T(8,128)(2,1)S(1)} collective-permute-done((bf16[3,512,128]{2,1,0:T(8,128)(2,1)}, bf16[3,512,128]{2,1,0:T(8,128)(2,1)S(1)}, u32[]{:S(2)}, u32[]{:S(2)}) %collective-permute-start.3) | collective-permute-done | bytes 393248 | tf_op jit(solution)/shard_map/ppermute | solution.py:29
  13.1 5.5 %collective-permute-done.5.refs_8_.refs_14_ = bf16[3,512,128]{2,1,0:T(8,128)(2,1)S(1)} collective-permute-done((bf16[3,512,128]{2,1,0:T(8,128)(2,1)}, bf16[3,512,128]{2,1,0:T(8,128)(2,1)S(1)}, u32[]{:S(2)}, u32[]{:S(2)}) %collective-permute-start.5) | collective-permute-done | bytes 393248 | tf_op jit(solution)/shard_map/ppermute | solution.py:29
  18.6 0.0 collective-permute-start.7
  18.6 0.0 collective-permute-start.4
  18.6 9.3 %collective-permute-done.9.refs_15_ = bf16[3,512,128]{2,1,0:T(8,128)(2,1)S(1)} collective-permute-done((bf16[3,512,128]{2,1,0:T(8,128)(2,1)S(1)}, bf16[3,512,128]{2,1,0:T(8,128)(2,1)S(1)}, u32[]{:S(2)}, u32[]{:S(2)}) %collective-permute-start.9) | collective-permute-done | bytes 393248 | tf_op jit(solution)/shard_map/ppermute | solution.py:29
  28.0 0.0 collective-permute-start.6
  28.0 0.0 collective-permute-done.2.refs_5_
  28.0 0.1 collective-permute-start.10
  28.0 3.5 %collective-permute-done.7.refs_10_ = bf16[3,512,128]{2,1,0:T(8,128)(2,1)S(1)} collective-permute-done((bf16[3,512,128]{2,1,0:T(8,128)(2,1)S(1)}, bf16[3,512,128]{2,1,0:T(8,128)(2,1)S(1)}, u32[]{:S(2)}, u32[]{:S(2)}) %collective-permute-start.7) | collective-permute-done | bytes 393248 | tf_op jit(solution)/shard_map/ppermute | solution.py:29
  31.5 0.0 collective-permute-start.8
  31.5 0.0 collective-permute-done.4.refs_7_
  31.5 0.5 collective-permute-start
  32.0 0.0 collective-permute-done.6.refs_9_
  32.0 7.5 %collective-permute-done.10.refs_16_ = bf16[3,512,128]{2,1,0:T(8,128)(2,1)S(1)} collective-permute-done((bf16[3,512,128]{2,1,0:T(8,128)(2,1)S(1)}, bf16[3,512,128]{2,1,0:T(8,128)(2,1)S(1)}, u32[]{:S(2)}, u32[]{:S(2)}) %collective-permute-start.10) | collective-permute-done | bytes 393248 | tf_op jit(solution)/shard_map/ppermute | solution.py:29
  39.5 0.0 collective-permute-done.1.refs_2_
  39.5 0.0 copy-start.5
  39.5 0.0 collective-permute-done.8.refs_11_
  39.6 0.8 %copy-done.13 = bf16[3,512,128]{2,1,0:T(8,128)(2,1)} copy-done((bf16[3,512,128]{2,1,0:T(8,128)(2,1)}, bf16[3,512,128]{2,1,0:T(8,128)(2,1)S(1)}, u32[]{:S(2)}) %copy-start.13) | copy-done | bytes 393240
  40.4 0.0 collective-permute-start.11
  40.4 0.0 copy-done.14
  40.4 0.7 copy.6.plist
  41.1 0.0 collective-permute-done.refs_1_
  41.1 2.1 %collective-permute-done.11.refs_3_ = bf16[1024,512]{1,0:T(8,128)(2,1)} collective-permute-done((bf16[1024,512]{1,0:T(8,128)(2,1)S(1)}, bf16[1024,512]{1,0:T(8,128)(2,1)}, u32[]{:S(2)}, u32[]{:S(2)}) %collective-permute-start.11) | collective-permute-done | bytes 1048608 | tf_op jit(solution)/shard_map/ppermute | solution.py:29
  43.2 0.0 copy-done.6
  43.2 0.0 copy-done.4
  43.2 0.0 copy-done.12
  43.2 0.0 copy-done.5
  43.2 10.9 %shard_map.56 = f32[2,4,128]{2,1,0:T(4,128)} custom-call(s32[4]{0:T(128)} %copy-done.2, s32[16,3]{1,0:T(8,128)} %copy.6.plist, s32[16]{0:T(128)} %pcount.1, bf16[1024,512]{1,0:T(8,128)(2,1)} %copy-done, bf16[1024,512]{1,0:T(8,128)(2,1)} %collective-permute-done.refs_1_, bf16[1024,512]{1,0:T(8,128)(2,1)} %copy-done.5, ...), custom_call_target="tpu_custom_call" | custom-call | tf_op jit(solution)/shard_map/pallas_call | solution.py:240
  54.2 0.1 collective-permute-start.12
  54.3 1.3 %collective-permute-done.12 = f32[2,4,128]{2,1,0:T(4,128)S(1)} collective-permute-done((f32[2,4,128]{2,1,0:T(4,128)}, f32[2,4,128]{2,1,0:T(4,128)S(1)}, u32[]{:S(2)}, u32[]{:S(2)}) %collective-permute-start.12) | collective-permute-done | bytes 4128 | tf_op jit(solution)/shard_map/ppermute | solution.py:29
  55.6 0.7 add.15
  56.3 2.0 %collective-permute-start.13 = (f32[4,128]{1,0:T(4,128)S(1)}, f32[4,128]{1,0:T(4,128)S(1)}, u32[]{:S(2)}, u32[]{:S(2)}) collective-permute-start(f32[4,128]{1,0:T(4,128)S(1)} %get-tuple-element.9), channel_id=1, source_target_pairs={{0,2},{1,3},{2,0},{3,1},{4,6},{5,7},{6,4},{7,5},{8,10},{9,11},{10,... | collective-permute-start | bytes 6152 | tf_op jit(solution)/shard_map/ppermute | solution.py:29
  58.3 3.5 %collective-permute-start.14 = (f32[4,128]{1,0:T(4,128)S(1)}, f32[4,128]{1,0:T(4,128)S(1)}, u32[]{:S(2)}, u32[]{:S(2)}) collective-permute-start(f32[4,128]{1,0:T(4,128)S(1)} %get-tuple-element.10), channel_id=1, source_target_pairs={{0,4},{4,0},{8,12},{12,8},{1,5},{5,1},{9,13},{13,9},{2,6},{6,2},{1... | collective-permute-start | bytes 6152 | tf_op jit(solution)/shard_map/ppermute | solution.py:29
  61.8 0.0 collective-permute-start.15
  61.8 0.0 collective-permute-done.13
  61.8 1.6 %collective-permute-done.14 = f32[4,128]{1,0:T(4,128)S(1)} collective-permute-done((f32[4,128]{1,0:T(4,128)S(1)}, f32[4,128]{1,0:T(4,128)S(1)}, u32[]{:S(2)}, u32[]{:S(2)}) %collective-permute-start.14) | collective-permute-done | bytes 2080 | tf_op jit(solution)/shard_map/ppermute | solution.py:29
  63.3 2.9 %collective-permute-done.15 = f32[4,128]{1,0:T(4,128)S(1)} collective-permute-done((f32[4,128]{1,0:T(4,128)S(1)}, f32[4,128]{1,0:T(4,128)S(1)}, u32[]{:S(2)}, u32[]{:S(2)}) %collective-permute-start.15) | collective-permute-done | bytes 2080 | tf_op jit(solution)/shard_map/ppermute | solution.py:29
  66.3 0.6 dynamic-slice_reduce_fusion
  (22 shorter events, 0.0 us)
Async XLA Ops:
  0.0 40.4 %copy-start.14 = (s32[16,3]{0,1:T(4,128)S(1)}, s32[16,3]{0,1:T(4,128)}, u32[]{:S(2)}) copy-start(s32[16,3]{0,1:T(4,128)} %param.8) | copy-start | bytes 580
  0.0 13.1 %collective-permute-start.3 = (bf16[3,512,128]{2,1,0:T(8,128)(2,1)}, bf16[3,512,128]{2,1,0:T(8,128)(2,1)S(1)}, u32[]{:S(2)}, u32[]{:S(2)}) collective-permute-start(bf16[3,512,128]{2,1,0:T(8,128)(2,1)} %bitcast.14), channel_id=1, source_target_pairs={{0,2},{1,3},{2,0},{3,1},{4,6},{5,7},{6,4},{7,5},{8,10},{9,11},{10,... | collective-permute-start | bytes 1179656 | tf_op jit(solution)/shard_map/ppermute | solution.py:29
  2.9 15.7 %collective-permute-start.5 = (bf16[3,512,128]{2,1,0:T(8,128)(2,1)}, bf16[3,512,128]{2,1,0:T(8,128)(2,1)S(1)}, u32[]{:S(2)}, u32[]{:S(2)}) collective-permute-start(bf16[3,512,128]{2,1,0:T(8,128)(2,1)} %bitcast.15), channel_id=1, source_target_pairs={{0,4},{4,0},{8,12},{12,8},{1,5},{5,1},{9,13},{13,9},{2,6},{6,2},{1... | collective-permute-start | bytes 1179656 | tf_op jit(solution)/shard_map/ppermute | solution.py:29
  4.6 1.6 %copy-start.1 = (bf16[512,2048]{1,0:T(8,128)(2,1)S(1)}, bf16[512,2048]{1,0:T(8,128)(2,1)}, u32[]{:S(2)}) copy-start(bf16[512,2048]{1,0:T(8,128)(2,1)} %virt_ref.1) | copy-start | bytes 6291460
  6.2 37.0 %copy-start.2 = (s32[4]{0:T(128)}, s32[4]{0:T(128)S(1)}, u32[]{:S(2)}) copy-start(s32[4]{0:T(128)S(1)} %pad_add_fusion.where) | copy-start | bytes 52
  6.2 2.3 %copy-start.3 = (bf16[512,1,3,128]{3,0,2,1:T(8,128)(2,1)S(1)}, bf16[512,1,3,128]{3,0,2,1:T(8,128)(2,1)}, u32[]{:S(2)}) copy-start(bf16[512,1,3,128]{3,0,2,1:T(8,128)(2,1)} %param.5) | copy-start | bytes 1179652
  7.8 35.4 %copy-start = (bf16[1024,512]{1,0:T(8,128)(2,1)}, bf16[1024,512]{1,0:T(8,128)(2,1)S(1)}, u32[]{:S(2)}) copy-start(bf16[1024,512]{1,0:T(8,128)(2,1)S(1)} %shard_map.55.refs_0_) | copy-start | bytes 3145732
  7.9 31.7 %collective-permute-start.1 = (bf16[1024,512]{1,0:T(8,128)(2,1)S(1)}, bf16[1024,512]{1,0:T(8,128)(2,1)S(1)}, u32[]{:S(2)}, u32[]{:S(2)}) collective-permute-start(bf16[1024,512]{1,0:T(8,128)(2,1)S(1)} %shard_map.55.refs_0_), channel_id=1, source_target_pairs={{0,2},{1,3},{2,0},{3,1},{4,6},{5,7},{6,4},{7,5},{8,10},{9,11},{10,... | collective-permute-start | bytes 3145736 | tf_op jit(solution)/shard_map/ppermute | solution.py:29
  8.5 19.5 %collective-permute-start.9 = (bf16[3,512,128]{2,1,0:T(8,128)(2,1)S(1)}, bf16[3,512,128]{2,1,0:T(8,128)(2,1)S(1)}, u32[]{:S(2)}, u32[]{:S(2)}) collective-permute-start(bf16[3,512,128]{2,1,0:T(8,128)(2,1)S(1)} %bitcast.18), channel_id=1, source_target_pairs={{0,8},{4,12},{8,0},{12,4},{16,28},{20,24},{24,20},{28,16},{1,9},{5... | collective-permute-start | bytes 1179656 | tf_op jit(solution)/shard_map/ppermute | solution.py:29
  11.0 16.9 %collective-permute-start.2 = (bf16[3,512,128]{2,1,0:T(8,128)(2,1)S(1)}, bf16[3,512,128]{2,1,0:T(8,128)(2,1)S(1)}, u32[]{:S(2)}, u32[]{:S(2)}) collective-permute-start(bf16[3,512,128]{2,1,0:T(8,128)(2,1)S(1)} %bitcast.19), channel_id=1, source_target_pairs={{0,1},{1,0},{2,3},{3,2},{4,5},{5,4},{6,7},{7,6},{8,9},{9,8},{10,11... | collective-permute-start | bytes 1179656 | tf_op jit(solution)/shard_map/ppermute | solution.py:29
  13.1 30.1 %copy-start.6 = (bf16[3,512,128]{2,1,0:T(8,128)(2,1)}, bf16[3,512,128]{2,1,0:T(8,128)(2,1)S(1)}, u32[]{:S(2)}) copy-start(bf16[3,512,128]{2,1,0:T(8,128)(2,1)S(1)} %collective-permute-done.3.refs_6_) | copy-start | bytes 1179652
  18.6 24.6 %copy-start.4 = (bf16[3,512,128]{2,1,0:T(8,128)(2,1)}, bf16[3,512,128]{2,1,0:T(8,128)(2,1)S(1)}, u32[]{:S(2)}) copy-start(bf16[3,512,128]{2,1,0:T(8,128)(2,1)S(1)} %collective-permute-done.5.refs_8_.refs_14_) | copy-start | bytes 1179652
  18.6 12.9 %collective-permute-start.7 = (bf16[3,512,128]{2,1,0:T(8,128)(2,1)S(1)}, bf16[3,512,128]{2,1,0:T(8,128)(2,1)S(1)}, u32[]{:S(2)}, u32[]{:S(2)}) collective-permute-start(bf16[3,512,128]{2,1,0:T(8,128)(2,1)S(1)} %collective-permute-done.3.refs_6_), channel_id=1, source_target_pairs={{0,4},{4,0},{8,12},{12,8},{1,5},{5,1},{9,13},{13,9},{2,6},{6,2},{1... | collective-permute-start | bytes 1179656 | tf_op jit(solution)/shard_map/ppermute | solution.py:29
  18.6 12.9 %collective-permute-start.4 = (bf16[3,512,128]{2,1,0:T(8,128)(2,1)S(1)}, bf16[3,512,128]{2,1,0:T(8,128)(2,1)S(1)}, u32[]{:S(2)}, u32[]{:S(2)}) collective-permute-start(bf16[3,512,128]{2,1,0:T(8,128)(2,1)S(1)} %collective-permute-done.3.refs_6_), channel_id=1, source_target_pairs={{0,1},{1,0},{2,3},{3,2},{4,5},{5,4},{6,7},{7,6},{8,9},{9,8},{10,11... | collective-permute-start | bytes 1179656 | tf_op jit(solution)/shard_map/ppermute | solution.py:29
  27.9 11.6 %copy-start.7 = (bf16[3,512,128]{2,1,0:T(8,128)(2,1)}, bf16[3,512,128]{2,1,0:T(8,128)(2,1)S(1)}, u32[]{:S(2)}) copy-start(bf16[3,512,128]{2,1,0:T(8,128)(2,1)S(1)} %collective-permute-done.9.refs_15_) | copy-start | bytes 1179652
  28.0 4.1 %collective-permute-start.6 = (bf16[3,512,128]{2,1,0:T(8,128)(2,1)S(1)}, bf16[3,512,128]{2,1,0:T(8,128)(2,1)S(1)}, u32[]{:S(2)}, u32[]{:S(2)}) collective-permute-start(bf16[3,512,128]{2,1,0:T(8,128)(2,1)S(1)} %collective-permute-done.5.refs_8_.refs_14_), channel_id=1, source_target_pairs={{0,1},{1,0},{2,3},{3,2},{4,5},{5,4},{6,7},{7,6},{8,9},{9,8},{10,11... | collective-permute-start | bytes 1179656 | tf_op jit(solution)/shard_map/ppermute | solution.py:29
  28.0 11.6 %copy-start.8 = (bf16[3,512,128]{2,1,0:T(8,128)(2,1)}, bf16[3,512,128]{2,1,0:T(8,128)(2,1)S(1)}, u32[]{:S(2)}) copy-start(bf16[3,512,128]{2,1,0:T(8,128)(2,1)S(1)} %collective-permute-done.2.refs_5_) | copy-start | bytes 1179652
  28.0 11.5 %collective-permute-start.10 = (bf16[3,512,128]{2,1,0:T(8,128)(2,1)S(1)}, bf16[3,512,128]{2,1,0:T(8,128)(2,1)S(1)}, u32[]{:S(2)}, u32[]{:S(2)}) collective-permute-start(bf16[3,512,128]{2,1,0:T(8,128)(2,1)S(1)} %collective-permute-done.9.refs_15_), channel_id=1, source_target_pairs={{0,16},{16,0},{1,17},{17,1},{2,18},{18,2},{3,19},{19,3},{4,20},{20... | collective-permute-start | bytes 1179656 | tf_op jit(solution)/shard_map/ppermute | solution.py:29
  31.5 8.0 %copy-start.9 = (bf16[3,512,128]{2,1,0:T(8,128)(2,1)}, bf16[3,512,128]{2,1,0:T(8,128)(2,1)S(1)}, u32[]{:S(2)}) copy-start(bf16[3,512,128]{2,1,0:T(8,128)(2,1)S(1)} %collective-permute-done.7.refs_10_) | copy-start | bytes 1179652
  31.5 8.0 %collective-permute-start.8 = (bf16[3,512,128]{2,1,0:T(8,128)(2,1)S(1)}, bf16[3,512,128]{2,1,0:T(8,128)(2,1)S(1)}, u32[]{:S(2)}, u32[]{:S(2)}) collective-permute-start(bf16[3,512,128]{2,1,0:T(8,128)(2,1)S(1)} %collective-permute-done.7.refs_10_), channel_id=1, source_target_pairs={{0,1},{1,0},{2,3},{3,2},{4,5},{5,4},{6,7},{7,6},{8,9},{9,8},{10,11... | collective-permute-start | bytes 1179656 | tf_op jit(solution)/shard_map/ppermute | solution.py:29
  31.5 8.0 %copy-start.10 = (bf16[3,512,128]{2,1,0:T(8,128)(2,1)}, bf16[3,512,128]{2,1,0:T(8,128)(2,1)S(1)}, u32[]{:S(2)}) copy-start(bf16[3,512,128]{2,1,0:T(8,128)(2,1)S(1)} %collective-permute-done.4.refs_7_) | copy-start | bytes 1179652
  31.5 9.6 %collective-permute-start = (bf16[1024,512]{1,0:T(8,128)(2,1)S(1)}, bf16[1024,512]{1,0:T(8,128)(2,1)}, u32[]{:S(2)}, u32[]{:S(2)}) collective-permute-start(bf16[1024,512]{1,0:T(8,128)(2,1)S(1)} %shard_map.55.refs_0_), channel_id=1, source_target_pairs={{0,1},{1,0},{2,3},{3,2},{4,5},{5,4},{6,7},{7,6},{8,9},{9,8},{10,11... | collective-permute-start | bytes 3145736 | tf_op jit(solution)/shard_map/ppermute | solution.py:29
  32.0 7.5 %copy-start.11 = (bf16[3,512,128]{2,1,0:T(8,128)(2,1)}, bf16[3,512,128]{2,1,0:T(8,128)(2,1)S(1)}, u32[]{:S(2)}) copy-start(bf16[3,512,128]{2,1,0:T(8,128)(2,1)S(1)} %collective-permute-done.6.refs_9_) | copy-start | bytes 1179652
  39.5 3.7 %copy-start.12 = (bf16[3,512,128]{2,1,0:T(8,128)(2,1)}, bf16[3,512,128]{2,1,0:T(8,128)(2,1)S(1)}, u32[]{:S(2)}) copy-start(bf16[3,512,128]{2,1,0:T(8,128)(2,1)S(1)} %collective-permute-done.10.refs_16_) | copy-start | bytes 1179652
  39.5 3.7 %copy-start.5 = (bf16[1024,512]{1,0:T(8,128)(2,1)}, bf16[1024,512]{1,0:T(8,128)(2,1)S(1)}, u32[]{:S(2)}) copy-start(bf16[1024,512]{1,0:T(8,128)(2,1)S(1)} %collective-permute-done.1.refs_2_) | copy-start | bytes 3145732
  39.6 0.8 %copy-start.13 = (bf16[3,512,128]{2,1,0:T(8,128)(2,1)}, bf16[3,512,128]{2,1,0:T(8,128)(2,1)S(1)}, u32[]{:S(2)}) copy-start(bf16[3,512,128]{2,1,0:T(8,128)(2,1)S(1)} %collective-permute-done.8.refs_11_) | copy-start | bytes 1179652
  40.4 2.8 %collective-permute-start.11 = (bf16[1024,512]{1,0:T(8,128)(2,1)S(1)}, bf16[1024,512]{1,0:T(8,128)(2,1)}, u32[]{:S(2)}, u32[]{:S(2)}) collective-permute-start(bf16[1024,512]{1,0:T(8,128)(2,1)S(1)} %collective-permute-done.1.refs_2_), channel_id=1, source_target_pairs={{0,1},{1,0},{2,3},{3,2},{4,5},{5,4},{6,7},{7,6},{8,9},{9,8},{10,11... | collective-permute-start | bytes 3145736 | tf_op jit(solution)/shard_map/ppermute | solution.py:29
  54.2 1.4 %collective-permute-start.12 = (f32[2,4,128]{2,1,0:T(4,128)}, f32[2,4,128]{2,1,0:T(4,128)S(1)}, u32[]{:S(2)}, u32[]{:S(2)}) collective-permute-start(f32[2,4,128]{2,1,0:T(4,128)} %shard_map.56), channel_id=1, source_target_pairs={{0,1},{1,0},{2,3},{3,2},{4,5},{5,4},{6,7},{7,6},{8,9},{9,8},{10,11... | collective-permute-start | bytes 12296 | tf_op jit(solution)/shard_map/ppermute | solution.py:29
  56.3 5.5 %collective-permute-start.13 = (f32[4,128]{1,0:T(4,128)S(1)}, f32[4,128]{1,0:T(4,128)S(1)}, u32[]{:S(2)}, u32[]{:S(2)}) collective-permute-start(f32[4,128]{1,0:T(4,128)S(1)} %get-tuple-element.9), channel_id=1, source_target_pairs={{0,2},{1,3},{2,0},{3,1},{4,6},{5,7},{6,4},{7,5},{8,10},{9,11},{10,... | collective-permute-start | bytes 6152 | tf_op jit(solution)/shard_map/ppermute | solution.py:29
  58.3 5.1 %collective-permute-start.14 = (f32[4,128]{1,0:T(4,128)S(1)}, f32[4,128]{1,0:T(4,128)S(1)}, u32[]{:S(2)}, u32[]{:S(2)}) collective-permute-start(f32[4,128]{1,0:T(4,128)S(1)} %get-tuple-element.10), channel_id=1, source_target_pairs={{0,4},{4,0},{8,12},{12,8},{1,5},{5,1},{9,13},{13,9},{2,6},{6,2},{1... | collective-permute-start | bytes 6152 | tf_op jit(solution)/shard_map/ppermute | solution.py:29
  61.8 4.5 %collective-permute-start.15 = (f32[4,128]{1,0:T(4,128)S(1)}, f32[4,128]{1,0:T(4,128)S(1)}, u32[]{:S(2)}, u32[]{:S(2)}) collective-permute-start(f32[4,128]{1,0:T(4,128)S(1)} %get-tuple-element.10), channel_id=1, source_target_pairs={{0,6},{1,7},{2,4},{3,5},{4,2},{5,3},{6,0},{7,1},{8,14},{9,15},{10,... | collective-permute-start | bytes 6152 | tf_op jit(solution)/shard_map/ppermute | solution.py:29

commit v5 on v4

--- a/solution.py
+++ b/solution.py
@@ -45,25 +45,56 @@
     return lax.optimization_barrier((x,) + others)[0]
 
 
+def stage(n_early, where, pcount, *refs):
+    m_refs, occ_ref, c_refs = refs[0:8], refs[8], refs[9 : 9 + n_early]
+    packed_ref, occ_rows_ref, centers_ref, flag_ref, mbuf, obuf, msem, osem, csem = refs[9 + n_early :]
+    own, plane, aux_at = where[0], where[2], where[3]
+    rows = occ_ref.shape[1]
+    blocks_here = rows // BS
+    m_copies = [pltpu.make_async_copy(m_refs[i], mbuf.at[i], msem.at[i]) for i in range(8)]
+    o_copy = pltpu.make_async_copy(occ_ref, obuf, osem)
+    steps = [0, 1, 2 | plane][:n_early]
+    c_copies = [
+        pltpu.make_async_copy(c_refs[i], centers_ref.at[aux_at ^ steps[i]], csem.at[i])
+        for i in range(n_early)
+    ]
+    for copy in m_copies + [o_copy] + c_copies:
+        copy.start()
+    for i in range(8):
+        m_copies[i].wait()
+        at = i // 4 * BS
+        for j in range(blocks_here):
+            block = (own ^ (i % 4)) * blocks_here + j
+            for k in range(KN):
+                tile = mbuf[i, k, j * BS : (j + 1) * BS, :]
+                if k > 0:
+                    tile = jnp.where(k < pcount[block], tile, jnp.zeros_like(tile))
+                packed_ref[block, at : at + BS, k * BS : (k + 1) * BS] = tile
+    o_copy.wait()
+    for b in range(blocks_here):
+        occ_rows_ref[b * BS : (b + 1) * BS, :] = obuf[:, b * BS : (b + 1) * BS].T
+    for copy in c_copies:
+        copy.wait()
+    flag_ref[...] = jnp.zeros_like(flag_ref)
+
+
 def contract(n_centers, where, plist, pcount, *refs):
-    v_refs, m_refs, occ_ref, c_refs = refs[0:4], refs[4:12], refs[12], refs[13 : 13 + n_centers]
-    out_ref = refs[13 + n_centers]
-    vbuf, mbuf, obuf, cbuf, prod, acc, listed, place, vsem, msem, osem, csem = refs[
-        14 + n_centers :
-    ]
+    v_refs, packed_ref, occ_ref, centers_ref = refs[0:4], refs[4], refs[5], refs[6]
+    last_ref, out_ref = refs[7], refs[9]
+    vbuf, prod, acc, listed, place, vsem = refs[-6:]
     own, parity, plane, aux_at = where[0], where[1], where[2], where[3]
-    basis = mbuf.shape[2]
-    n_q, _, rows, _ = cbuf.shape
+    n_q = acc.shape[1]
+    rows = v_refs[0].shape[1]
     blocks_here = rows // BS
     n_places = vbuf.shape[0]
     slots = [(b, k) for b in range(blocks_here) for k in range(KN)]
 
     def used(b, k):
         block = own * blocks_here + b
-        return (k < pcount[block]) & ((plist[block, k] & 1) == parity)
+        return (k < pcount[block]) & ((plist[k, block] & 1) == parity)
 
     def column(b, k):
-        return plist[own * blocks_here + b, k] >> 1
+        return plist[k, own * blocks_here + b] >> 1
 
     for c in range(n_places):
         place[c] = -1
@@ -93,24 +124,7 @@
             for i in range(4)
         ]
 
-    def m_copies():
-        out = []
-        for i in range(8):
-            span = pl.ds(pl.multiple_of((own ^ (i % 4)) * rows, rows), rows)
-            out.append(pltpu.make_async_copy(m_refs[i], mbuf.at[i // 4, :, span], msem.at[i]))
-        return out
-
-    o_copy = pltpu.make_async_copy(occ_ref, obuf, osem)
-    if n_centers == 1:
-        c_copies = [pltpu.make_async_copy(c_refs[0], cbuf, csem.at[0])]
-    else:
-        steps = [0, 1, 2 | plane, 3 ^ plane]
-        c_copies = [
-            pltpu.make_async_copy(c_refs[i], cbuf.at[aux_at ^ steps[i]], csem.at[i])
-            for i in range(n_centers)
-        ]
-
-    for copy in v_copies(0) + v_copies(1) + m_copies():
+    for copy in v_copies(0) + v_copies(1):
         copy.start()
     for g in range(1, n_places // 2):
 
@@ -119,12 +133,7 @@
             for copy in v_copies(2 * g) + v_copies(2 * g + 1):
                 copy.start()
 
-    o_copy.start()
-    for copy in c_copies:
-        copy.start()
     acc[...] = jnp.zeros_like(acc)
-    for copy in m_copies():
-        copy.wait()
 
     def one_group(g, carry):
         for copy in v_copies(2 * g) + v_copies(2 * g + 1):
@@ -133,24 +142,20 @@
         def four_blocks(i, carry):
             for j in range(4):
                 block = 4 * i + j
-                span = pl.ds(pl.multiple_of(block * BS, BS), BS)
-                weights, parts = [], []
+                parts = []
                 for k in range(KN):
-                    p = plist[block, k]
+                    p = plist[k, block]
                     at = pl.ds(pl.multiple_of((p & 3) * BS, BS), BS)
                     parts.append(
                         jnp.concatenate([vbuf[2 * g + h, p >> 2, :, at] for h in range(2)], axis=0)
                     )
-                    weight = jnp.concatenate([mbuf[s, k, span, :] for s in range(2)], axis=0)
-                    if k > 0:
-                        weight = jnp.where(k < pcount[block], weight, jnp.zeros_like(weight))
-                    weights.append(weight)
                 res = lax.dot_general(
                     jnp.concatenate(parts, axis=1),
-                    jnp.concatenate(weights, axis=1),
+                    packed_ref[block],
                     (((1,), (1,)), ((), ())),
                     preferred_element_type=jnp.float32,
                 ).astype(jnp.bfloat16)
+                span = pl.ds(pl.multiple_of(block * BS, BS), BS)
                 for s in range(2):
                     for h in range(2):
                         prod[2 * g + h, s * BS : (s + 1) * BS, span] = res[
@@ -158,33 +163,36 @@
                         ]
             return carry
 
-        lax.fori_loop(0, basis // (4 * BS), four_blocks, 0)
+        lax.fori_loop(0, packed_ref.shape[0] // 4, four_blocks, 0)
         return carry
 
     lax.fori_loop(0, groups, one_group, 0)
-    o_copy.wait()
-    for copy in c_copies:
-        copy.wait()
 
     for b, k in slots:
 
         @pl.when(used(b, k))
         def _(b=b, k=k):
-            left = jnp.dot(
+            left = lax.dot_general(
+                occ_ref[b * BS : (b + 1) * BS, :],
                 prod[place[column(b, k)]],
-                obuf[:, b * BS : (b + 1) * BS],
+                (((1,), (1,)), ((), ())),
                 preferred_element_type=jnp.float32,
             )
             left = left.astype(jnp.bfloat16).astype(jnp.float32)
-            left = [left[s * BS : (s + 1) * BS, :].T for s in range(2)]
-
-            def add(q, carry):
-                center = cbuf[q, k, b * BS : (b + 1) * BS, :].astype(jnp.float32)
+
+            def add(q, center):
+                center = center.astype(jnp.float32)
                 for s in range(2):
-                    acc[s, q] += (left[s] * center).reshape(BS // 8, 8, BS).sum(axis=0)
-                return carry
-
-            lax.fori_loop(0, n_q, add, 0, unroll=n_q <= 8)
+                    term = left[:, s * BS : (s + 1) * BS] * center
+                    acc[s, q] += term.reshape(BS // 8, 8, BS).sum(axis=0)
+
+            span = slice(b * BS, (b + 1) * BS)
+            if n_centers == 1:
+                lax.fori_loop(0, n_q, lambda q, x: (add(q, last_ref[q, k, span, :]), x)[1], 0)
+            else:
+                for step in (0, 1, 2 | plane):
+                    add(aux_at ^ step, centers_ref[aux_at ^ step, k, span, :])
+                add(aux_at ^ 3 ^ plane, last_ref[k, span, :])
 
     for s in range(2):
         out_ref[s] = acc[s].sum(axis=1)
@@ -235,29 +243,44 @@
 
     m_parts = [centers, core(centers), far_a, core(far_a), other, core(other), far_b]
     m_parts.append(core(far_b))
-    v_parts = [mine, core(mine), v_across, core(after(v_across, *m_parts[1:], all_centers[-1]))]
-
+    n_early = 3 if aux == 4 else 0
+    packed, occ_rows, staged, flag = pl.pallas_call(
+        functools.partial(stage, n_early),
+        out_shape=[
+            jax.ShapeDtypeStruct((basis_total // BS, 2 * BS, KN * BS), jnp.bfloat16),
+            jax.ShapeDtypeStruct((rows, basis_total), jnp.bfloat16),
+            jax.ShapeDtypeStruct((aux if n_early else 1, KN, rows, BS), jnp.bfloat16),
+            jax.ShapeDtypeStruct((8, BS), jnp.float32),
+        ],
+        in_specs=[scalars] * 2 + [anywhere] * (9 + n_early),
+        out_specs=[vmem] * 4,
+        scratch_shapes=[
+            pltpu.VMEM((8, KN, rows, BS), jnp.bfloat16),
+            pltpu.VMEM((basis_total, rows), jnp.bfloat16),
+            pltpu.SemaphoreType.DMA((8,)),
+            pltpu.SemaphoreType.DMA,
+            pltpu.SemaphoreType.DMA((4,)),
+        ],
+        compiler_params=pltpu.CompilerParams(vmem_limit_bytes=(20 if aux == 4 else 24) * MIB),
+    )(where, partner_count, *m_parts, occ_density, *all_centers[:n_early])
+    late = all_centers[n_early:]
+    moved, flag, *_ = lax.optimization_barrier((v_across, flag, *late))
+    v_parts = [mine, core(mine), v_across, core(moved)]
     sums = pl.pallas_call(
         functools.partial(contract, len(all_centers)),
         out_shape=jax.ShapeDtypeStruct((2, aux, BS), jnp.float32),
-        in_specs=[scalars] * 3 + [anywhere] * (13 + len(all_centers)),
+        in_specs=[scalars] * 3 + [anywhere] * 4 + [vmem] * (3 + len(late)) + [anywhere],
         out_specs=vmem,
         scratch_shapes=[
             pltpu.VMEM((n_blocks, 4, BS, rows), jnp.bfloat16),
-            pltpu.VMEM((2, KN, basis_total, BS), jnp.bfloat16),
-            pltpu.VMEM((basis_total, rows), jnp.bfloat16),
-            pltpu.VMEM((aux, KN, rows, BS), jnp.bfloat16),
             pltpu.VMEM((n_blocks, 2 * BS, basis_total), jnp.bfloat16),
             pltpu.VMEM((2, aux, 8, BS), jnp.float32),
             pltpu.SMEM((n_blocks,), jnp.int32),
             pltpu.SMEM((n_blocks,), jnp.int32),
             pltpu.SemaphoreType.DMA((n_blocks, 4)),
-            pltpu.SemaphoreType.DMA((8,)),
-            pltpu.SemaphoreType.DMA,
-            pltpu.SemaphoreType.DMA((4,)),
         ],
-        compiler_params=pltpu.CompilerParams(vmem_limit_bytes=58 * MIB),
-    )(where, partner_list, partner_count, *v_parts, *m_parts, occ_density, *all_centers)
+        compiler_params=pltpu.CompilerParams(vmem_limit_bytes=(20 if aux == 4 else 48) * MIB),
+    )(where, partner_list.T, partner_count, *v_parts, packed, occ_rows, staged, *late, flag)
 
     sums = sums + core(sums)
     diagonal = swap(sums[1], ("aux", "atoms"), (aux, atoms), lambda a, t: (a ^ 1, t ^ 2))

time: 68 us -> 68.5 us (level)
  starting transfers between devices: 13.9 us -> 21.2 us
  waiting for transfers between devices: 35.7 us -> 32.7 us
  local copies, waits for them, and re-layouts: 3.16 us -> 1.61 us
  Pallas kernels: 12.5 us -> 11.4 us
    ppermute x16, starting transfers between devices: 13.9 us -> 21.2 us  [swap(): return lax.ppermute(x, axes, perm)]
    pallas_call x1, Pallas kernels: 10.9 us -> 5.62 us  [on_device(): pl.pallas_call(functools.partial(contract, len(all_centers)), out_shape=j...]
    pallas_call x0 -> x1, Pallas kernels: none -> 4.14 us  [on_device(): pl.pallas_call(functools.partial(stage, n_early), out_shape=[jax.ShapeDty...]
    ppermute x16, waiting for transfers between devices: 35.7 us -> 32.7 us  [swap(): return lax.ppermute(x, axes, perm)]
    unnamed x31 -> x10, local copies, waits for them, and re-layouts: 3.15 us -> 1.61 us
  transfers between devices with their start and end apart: 16 -> 16, of which waited for: 9 -> 9; matrix products, arithmetic and copies ran while one was open for 1% -> 0% of each run, Pallas kernels for 2% -> 8%
where the time goes in v5:
time: 68.5 us; the launch traced here: 68.9 us
  waiting for transfers between devices  32.7 us (48%)
  starting transfers between devices  21.2 us (31%)
  Pallas kernels  11.4 us (17%)
  local copies, waits for them, and re-layouts  1.61 us (2%)
  between operations  1.23 us (2%)
  other arithmetic  0.69 us (1%)
    ppermute x16, waiting for transfers between devices, swap(): return lax.ppermute(x, axes, perm)  32.7 us
    ppermute x16, starting transfers between devices, swap(): return lax.ppermute(x, axes, perm)  21.2 us
    pallas_call x1, Pallas kernels, on_device(): pl.pallas_call(functools.partial(contract, len(all_centers)), out_shape=j...  5.62 us
    pallas_call x1, Pallas kernels, on_device(): pl.pallas_call(functools.partial(stage, n_early), out_shape=[jax.ShapeDty...  4.14 us
    pallas_call x1, Pallas kernels, on_device(): pl.pallas_call(functools.partial(select, n_blocks), out_shape=jax.ShapeDt...  1.64 us
    unnamed x10, local copies, waits for them, and re-layouts  1.61 us
  transfers between devices with their start and end apart: 16, of which 9 were waited for; matrix products, arithmetic and copies ran while one was open for 0% of the time, Pallas kernels for 8%

profile of v5, /device:TPU:0, one launch (start us, length us, event | category | flops | bytes accessed | tf_op | source)
XLA Modules:
  0.0 68.9 jit_solution(3363720352585598425)
XLA Ops:
  0.0 0.0 copy-start.4
  0.0 2.9 %collective-permute-start.3 = (bf16[3,512,128]{2,1,0:T(8,128)(2,1)}, bf16[3,512,128]{2,1,0:T(8,128)(2,1)S(1)}, u32[]{:S(2)}, u32[]{:S(2)}) collective-permute-start(bf16[3,512,128]{2,1,0:T(8,128)(2,1)} %bitcast.15), channel_id=1, source_target_pairs={{0,2},{1,3},{2,0},{3,1},{4,6},{5,7},{6,4},{7,5},{8,10},{9,11},{10,... | collective-permute-start | bytes 1179656 | tf_op jit(solution)/shard_map/ppermute | solution.py:29
  2.9 1.6 %collective-permute-start.5 = (bf16[3,512,128]{2,1,0:T(8,128)(2,1)}, bf16[3,512,128]{2,1,0:T(8,128)(2,1)S(1)}, u32[]{:S(2)}, u32[]{:S(2)}) collective-permute-start(bf16[3,512,128]{2,1,0:T(8,128)(2,1)} %bitcast.16), channel_id=1, source_target_pairs={{0,4},{4,0},{8,12},{12,8},{1,5},{5,1},{9,13},{13,9},{2,6},{6,2},{1... | collective-permute-start | bytes 1179656 | tf_op jit(solution)/shard_map/ppermute | solution.py:29
  4.5 0.1 pad_add_fusion.where
  4.6 0.0 copy-start
  4.6 1.6 %copy-done = bf16[512,2048]{1,0:T(8,128)(2,1)S(1)} copy-done((bf16[512,2048]{1,0:T(8,128)(2,1)S(1)}, bf16[512,2048]{1,0:T(8,128)(2,1)}, u32[]{:S(2)}) %copy-start) | copy-done | bytes 2097176
  6.2 0.0 copy-start.2
  6.2 0.0 copy-start.1
  6.2 1.6 %shard_map.55.refs_0_ = bf16[1024,512]{1,0:T(8,128)(2,1)S(1)} custom-call(s32[4]{0:T(128)S(1)} %pad_add_fusion.where, bf16[512,2048]{1,0:T(8,128)(2,1)S(1)} %copy-done), custom_call_target="tpu_custom_call" | custom-call | tf_op jit(solution)/shard_map/pallas_call | solution.py:224
  7.8 0.0 copy-start.3
  7.9 0.6 collective-permute-start.1
  8.5 0.0 copy-done.2
  8.5 2.6 %collective-permute-start.9 = (bf16[3,512,128]{2,1,0:T(8,128)(2,1)S(1)}, bf16[3,512,128]{2,1,0:T(8,128)(2,1)S(1)}, u32[]{:S(2)}, u32[]{:S(2)}) collective-permute-start(bf16[3,512,128]{2,1,0:T(8,128)(2,1)S(1)} %bitcast.17), channel_id=1, source_target_pairs={{0,8},{4,12},{8,0},{12,4},{16,28},{20,24},{24,20},{28,16},{1,9},{5... | collective-permute-start | bytes 1179656 | tf_op jit(solution)/shard_map/ppermute | solution.py:29
  11.0 2.0 %collective-permute-done.3.refs_2_ = bf16[3,512,128]{2,1,0:T(8,128)(2,1)S(1)} collective-permute-done((bf16[3,512,128]{2,1,0:T(8,128)(2,1)}, bf16[3,512,128]{2,1,0:T(8,128)(2,1)S(1)}, u32[]{:S(2)}, u32[]{:S(2)}) %collective-permute-start.3) | collective-permute-done | bytes 393248 | tf_op jit(solution)/shard_map/ppermute | solution.py:29
  13.1 5.5 %collective-permute-done.5.refs_4_.refs_10_ = bf16[3,512,128]{2,1,0:T(8,128)(2,1)S(1)} collective-permute-done((bf16[3,512,128]{2,1,0:T(8,128)(2,1)}, bf16[3,512,128]{2,1,0:T(8,128)(2,1)S(1)}, u32[]{:S(2)}, u32[]{:S(2)}) %collective-permute-start.5) | collective-permute-done | bytes 393248 | tf_op jit(solution)/shard_map/ppermute | solution.py:29
  18.6 0.0 collective-permute-start.7
  18.6 0.0 collective-permute-start.2
  18.6 0.5 collective-permute-start.4
  19.1 8.9 %collective-permute-done.9.refs_11_ = bf16[3,512,128]{2,1,0:T(8,128)(2,1)S(1)} collective-permute-done((bf16[3,512,128]{2,1,0:T(8,128)(2,1)S(1)}, bf16[3,512,128]{2,1,0:T(8,128)(2,1)S(1)}, u32[]{:S(2)}, u32[]{:S(2)}) %collective-permute-start.9) | collective-permute-done | bytes 393248 | tf_op jit(solution)/shard_map/ppermute | solution.py:29
  28.0 0.0 collective-permute-start.6
  28.0 3.6 %collective-permute-done.7.refs_6_ = bf16[3,512,128]{2,1,0:T(8,128)(2,1)S(1)} collective-permute-done((bf16[3,512,128]{2,1,0:T(8,128)(2,1)S(1)}, bf16[3,512,128]{2,1,0:T(8,128)(2,1)S(1)}, u32[]{:S(2)}, u32[]{:S(2)}) %collective-permute-start.7) | collective-permute-done | bytes 393248 | tf_op jit(solution)/shard_map/ppermute | solution.py:29
  31.5 0.0 collective-permute-start.8
  31.5 0.0 collective-permute-done.2.refs_1_
  31.5 1.5 %collective-permute-start.10 = (bf16[3,512,128]{2,1,0:T(8,128)(2,1)S(1)}, bf16[3,512,128]{2,1,0:T(8,128)(2,1)S(1)}, u32[]{:S(2)}, u32[]{:S(2)}) collective-permute-start(bf16[3,512,128]{2,1,0:T(8,128)(2,1)S(1)} %collective-permute-done.9.refs_11_), channel_id=1, source_target_pairs={{0,16},{16,0},{1,17},{17,1},{2,18},{18,2},{3,19},{19,3},{4,20},{20... | collective-permute-start | bytes 1179656 | tf_op jit(solution)/shard_map/ppermute | solution.py:29
  33.0 0.0 collective-permute-done.4.refs_3_
  33.0 0.2 collective-permute-start
  33.2 0.0 collective-permute-done.6.refs_5_
  33.2 0.0 collective-permute-done.8.refs_7_
  33.2 0.0 copy-done.4
  33.2 0.0 copy-done.1
  33.3 4.1 %shard_map.56 = (bf16[16,256,384]{2,1,0:T(8,128)(2,1)S(1)}, bf16[512,2048]{1,0:T(8,128)(2,1)S(1)}, bf16[4,3,512,128]{3,2,1,0:T(8,128)(2,1)S(1)}, f32[8,128]{1,0:T(8,128)S(1)}) custom-call(s32[4]{0:T(128)S(1)} %pad_add_fusion.where, s32[16]{0:T(128)S(1)} %copy-done.4, bf16[3,512,128]{2,1,0:T(8,128)(2,1)S(1)} %bitcast.19, ...), custom_call_target="tpu_custom_call" | custom-call | tf_op jit(solution)/shard_map/pallas_call | solution.py:247
  37.4 5.6 %collective-permute-done.10.refs_7_ = bf16[3,512,128]{2,1,0:T(8,128)(2,1)S(1)} collective-permute-done((bf16[3,512,128]{2,1,0:T(8,128)(2,1)S(1)}, bf16[3,512,128]{2,1,0:T(8,128)(2,1)S(1)}, u32[]{:S(2)}, u32[]{:S(2)}) %collective-permute-start.10) | collective-permute-done | bytes 393248 | tf_op jit(solution)/shard_map/ppermute | solution.py:29
  43.0 0.0 collective-permute-done.1.refs_2_
  43.0 0.0 collective-permute-start.11
  43.1 0.0 collective-permute-done.refs_1_
  43.1 2.7 %collective-permute-done.11.refs_3_ = bf16[1024,512]{1,0:T(8,128)(2,1)S(1)} collective-permute-done((bf16[1024,512]{1,0:T(8,128)(2,1)S(1)}, bf16[1024,512]{1,0:T(8,128)(2,1)S(1)}, u32[]{:S(2)}, u32[]{:S(2)}) %collective-permute-start.11) | collective-permute-done | bytes 1048608 | tf_op jit(solution)/shard_map/ppermute | solution.py:29
  45.7 0.0 copy-done.3
  45.7 5.6 %shard_map.57 = f32[2,4,128]{2,1,0:T(4,128)S(1)} custom-call(s32[4]{0:T(128)S(1)} %pad_add_fusion.where, s32[3,16]{1,0:T(4,128)S(1)} %bitcast.21, s32[16]{0:T(128)S(1)} %copy-done.4, bf16[1024,512]{1,0:T(8,128)(2,1)S(1)} %shard_map.55.refs_0_, bf16[1024,512]{1,0:T(8,128)(2,1)S(1)} %collective-permute-done.refs_1_, ...), custom_call_target="tpu_custom_call" | custom-call | tf_op jit(solution)/shard_map/pallas_call | solution.py:269
  51.3 4.2 %collective-permute-start.12 = (f32[2,4,128]{2,1,0:T(4,128)S(1)}, f32[2,4,128]{2,1,0:T(4,128)S(1)}, u32[]{:S(2)}, u32[]{:S(2)}) collective-permute-start(f32[2,4,128]{2,1,0:T(4,128)S(1)} %shard_map.57), channel_id=1, source_target_pairs={{0,1},{1,0},{2,3},{3,2},{4,5},{5,4},{6,7},{7,6},{8,9},{9,8},{10,11... | collective-permute-start | bytes 12296 | tf_op jit(solution)/shard_map/ppermute | solution.py:29
  55.5 0.8 %collective-permute-done.12 = f32[2,4,128]{2,1,0:T(4,128)S(1)} collective-permute-done((f32[2,4,128]{2,1,0:T(4,128)S(1)}, f32[2,4,128]{2,1,0:T(4,128)S(1)}, u32[]{:S(2)}, u32[]{:S(2)}) %collective-permute-start.12) | collective-permute-done | bytes 4128 | tf_op jit(solution)/shard_map/ppermute | solution.py:29
  56.4 5.6 %collective-permute-start.13 = (f32[4,128]{1,0:T(4,128)S(1)}, f32[4,128]{1,0:T(4,128)S(1)}, u32[]{:S(2)}, u32[]{:S(2)}) collective-permute-start(f32[4,128]{1,0:T(4,128)S(1)} %get-tuple-element.19), channel_id=1, source_target_pairs={{0,2},{1,3},{2,0},{3,1},{4,6},{5,7},{6,4},{7,5},{8,10},{9,11},{10,... | collective-permute-start | bytes 6152 | tf_op jit(solution)/shard_map/ppermute | solution.py:29
  61.9 0.7 %collective-permute-start.14 = (f32[4,128]{1,0:T(4,128)S(1)}, f32[4,128]{1,0:T(4,128)S(1)}, u32[]{:S(2)}, u32[]{:S(2)}) collective-permute-start(f32[4,128]{1,0:T(4,128)S(1)} %get-tuple-element.20), channel_id=1, source_target_pairs={{0,4},{4,0},{8,12},{12,8},{1,5},{5,1},{9,13},{13,9},{2,6},{6,2},{1... | collective-permute-start | bytes 6152 | tf_op jit(solution)/shard_map/ppermute | solution.py:29
  62.6 0.8 %collective-permute-start.15 = (f32[4,128]{1,0:T(4,128)S(1)}, f32[4,128]{1,0:T(4,128)S(1)}, u32[]{:S(2)}, u32[]{:S(2)}) collective-permute-start(f32[4,128]{1,0:T(4,128)S(1)} %get-tuple-element.20), channel_id=1, source_target_pairs={{0,6},{1,7},{2,4},{3,5},{4,2},{5,3},{6,0},{7,1},{8,14},{9,15},{10,... | collective-permute-start | bytes 6152 | tf_op jit(solution)/shard_map/ppermute | solution.py:29
  63.5 0.0 collective-permute-done.13
  63.5 2.0 %collective-permute-done.14 = f32[4,128]{1,0:T(4,128)S(1)} collective-permute-done((f32[4,128]{1,0:T(4,128)S(1)}, f32[4,128]{1,0:T(4,128)S(1)}, u32[]{:S(2)}, u32[]{:S(2)}) %collective-permute-start.14) | collective-permute-done | bytes 2080 | tf_op jit(solution)/shard_map/ppermute | solution.py:29
  65.5 1.6 %collective-permute-done.15 = f32[4,128]{1,0:T(4,128)S(1)} collective-permute-done((f32[4,128]{1,0:T(4,128)S(1)}, f32[4,128]{1,0:T(4,128)S(1)}, u32[]{:S(2)}, u32[]{:S(2)}) %collective-permute-start.15) | collective-permute-done | bytes 2080 | tf_op jit(solution)/shard_map/ppermute | solution.py:29
  67.1 0.6 dynamic-slice_reduce_fusion
  (3 shorter events, 0.0 us)
Async XLA Ops:
  0.0 33.2 %copy-start.4 = (s32[16]{0:T(128)S(1)}, s32[16]{0:T(128)}, u32[]{:S(2)}) copy-start(s32[16]{0:T(128)} %pcount.3) | copy-start | bytes 196
  0.0 13.1 %collective-permute-start.3 = (bf16[3,512,128]{2,1,0:T(8,128)(2,1)}, bf16[3,512,128]{2,1,0:T(8,128)(2,1)S(1)}, u32[]{:S(2)}, u32[]{:S(2)}) collective-permute-start(bf16[3,512,128]{2,1,0:T(8,128)(2,1)} %bitcast.15), channel_id=1, source_target_pairs={{0,2},{1,3},{2,0},{3,1},{4,6},{5,7},{6,4},{7,5},{8,10},{9,11},{10,... | collective-permute-start | bytes 1179656 | tf_op jit(solution)/shard_map/ppermute | solution.py:29
  2.9 15.6 %collective-permute-start.5 = (bf16[3,512,128]{2,1,0:T(8,128)(2,1)}, bf16[3,512,128]{2,1,0:T(8,128)(2,1)S(1)}, u32[]{:S(2)}, u32[]{:S(2)}) collective-permute-start(bf16[3,512,128]{2,1,0:T(8,128)(2,1)} %bitcast.16), channel_id=1, source_target_pairs={{0,4},{4,0},{8,12},{12,8},{1,5},{5,1},{9,13},{13,9},{2,6},{6,2},{1... | collective-permute-start | bytes 1179656 | tf_op jit(solution)/shard_map/ppermute | solution.py:29
  4.6 1.6 %copy-start = (bf16[512,2048]{1,0:T(8,128)(2,1)S(1)}, bf16[512,2048]{1,0:T(8,128)(2,1)}, u32[]{:S(2)}) copy-start(bf16[512,2048]{1,0:T(8,128)(2,1)} %virt_ref.1) | copy-start | bytes 6291460
  6.2 2.3 %copy-start.2 = (bf16[512,1,3,128]{3,0,2,1:T(8,128)(2,1)S(1)}, bf16[512,1,3,128]{3,0,2,1:T(8,128)(2,1)}, u32[]{:S(2)}) copy-start(bf16[512,1,3,128]{3,0,2,1:T(8,128)(2,1)} %param.5) | copy-start | bytes 1179652
  6.2 27.1 %copy-start.1 = (bf16[2048,512]{1,0:T(8,128)(2,1)S(1)}, bf16[2048,512]{1,0:T(8,128)(2,1)}, u32[]{:S(2)}) copy-start(bf16[2048,512]{1,0:T(8,128)(2,1)} %refs_8_.1) | copy-start | bytes 6291460
  7.8 37.9 %copy-start.3 = (s32[16,3]{0,1:T(4,128)S(1)}, s32[16,3]{0,1:T(4,128)}, u32[]{:S(2)}) copy-start(s32[16,3]{0,1:T(4,128)} %param.8) | copy-start | bytes 580
  7.9 35.2 %collective-permute-start.1 = (bf16[1024,512]{1,0:T(8,128)(2,1)S(1)}, bf16[1024,512]{1,0:T(8,128)(2,1)S(1)}, u32[]{:S(2)}, u32[]{:S(2)}) collective-permute-start(bf16[1024,512]{1,0:T(8,128)(2,1)S(1)} %shard_map.55.refs_0_), channel_id=1, source_target_pairs={{0,2},{1,3},{2,0},{3,1},{4,6},{5,7},{6,4},{7,5},{8,10},{9,11},{10,... | collective-permute-start | bytes 3145736 | tf_op jit(solution)/shard_map/ppermute | solution.py:29
  8.5 19.5 %collective-permute-start.9 = (bf16[3,512,128]{2,1,0:T(8,128)(2,1)S(1)}, bf16[3,512,128]{2,1,0:T(8,128)(2,1)S(1)}, u32[]{:S(2)}, u32[]{:S(2)}) collective-permute-start(bf16[3,512,128]{2,1,0:T(8,128)(2,1)S(1)} %bitcast.17), channel_id=1, source_target_pairs={{0,8},{4,12},{8,0},{12,4},{16,28},{20,24},{24,20},{28,16},{1,9},{5... | collective-permute-start | bytes 1179656 | tf_op jit(solution)/shard_map/ppermute | solution.py:29
  18.6 12.9 %collective-permute-start.7 = (bf16[3,512,128]{2,1,0:T(8,128)(2,1)S(1)}, bf16[3,512,128]{2,1,0:T(8,128)(2,1)S(1)}, u32[]{:S(2)}, u32[]{:S(2)}) collective-permute-start(bf16[3,512,128]{2,1,0:T(8,128)(2,1)S(1)} %collective-permute-done.3.refs_2_), channel_id=1, source_target_pairs={{0,4},{4,0},{8,12},{12,8},{1,5},{5,1},{9,13},{13,9},{2,6},{6,2},{1... | collective-permute-start | bytes 1179656 | tf_op jit(solution)/shard_map/ppermute | solution.py:29
  18.6 12.9 %collective-permute-start.2 = (bf16[3,512,128]{2,1,0:T(8,128)(2,1)S(1)}, bf16[3,512,128]{2,1,0:T(8,128)(2,1)S(1)}, u32[]{:S(2)}, u32[]{:S(2)}) collective-permute-start(bf16[3,512,128]{2,1,0:T(8,128)(2,1)S(1)} %bitcast.18), channel_id=1, source_target_pairs={{0,1},{1,0},{2,3},{3,2},{4,5},{5,4},{6,7},{7,6},{8,9},{9,8},{10,11... | collective-permute-start | bytes 1179656 | tf_op jit(solution)/shard_map/ppermute | solution.py:29
  18.6 14.4 %collective-permute-start.4 = (bf16[3,512,128]{2,1,0:T(8,128)(2,1)S(1)}, bf16[3,512,128]{2,1,0:T(8,128)(2,1)S(1)}, u32[]{:S(2)}, u32[]{:S(2)}) collective-permute-start(bf16[3,512,128]{2,1,0:T(8,128)(2,1)S(1)} %collective-permute-done.3.refs_2_), channel_id=1, source_target_pairs={{0,1},{1,0},{2,3},{3,2},{4,5},{5,4},{6,7},{7,6},{8,9},{9,8},{10,11... | collective-permute-start | bytes 1179656 | tf_op jit(solution)/shard_map/ppermute | solution.py:29
  28.0 5.3 %collective-permute-start.6 = (bf16[3,512,128]{2,1,0:T(8,128)(2,1)S(1)}, bf16[3,512,128]{2,1,0:T(8,128)(2,1)S(1)}, u32[]{:S(2)}, u32[]{:S(2)}) collective-permute-start(bf16[3,512,128]{2,1,0:T(8,128)(2,1)S(1)} %collective-permute-done.5.refs_4_.refs_10_), channel_id=1, source_target_pairs={{0,1},{1,0},{2,3},{3,2},{4,5},{5,4},{6,7},{7,6},{8,9},{9,8},{10,11... | collective-permute-start | bytes 1179656 | tf_op jit(solution)/shard_map/ppermute | solution.py:29
  31.5 1.7 %collective-permute-start.8 = (bf16[3,512,128]{2,1,0:T(8,128)(2,1)S(1)}, bf16[3,512,128]{2,1,0:T(8,128)(2,1)S(1)}, u32[]{:S(2)}, u32[]{:S(2)}) collective-permute-start(bf16[3,512,128]{2,1,0:T(8,128)(2,1)S(1)} %collective-permute-done.7.refs_6_), channel_id=1, source_target_pairs={{0,1},{1,0},{2,3},{3,2},{4,5},{5,4},{6,7},{7,6},{8,9},{9,8},{10,11... | collective-permute-start | bytes 1179656 | tf_op jit(solution)/shard_map/ppermute | solution.py:29
  31.5 11.5 %collective-permute-start.10 = (bf16[3,512,128]{2,1,0:T(8,128)(2,1)S(1)}, bf16[3,512,128]{2,1,0:T(8,128)(2,1)S(1)}, u32[]{:S(2)}, u32[]{:S(2)}) collective-permute-start(bf16[3,512,128]{2,1,0:T(8,128)(2,1)S(1)} %collective-permute-done.9.refs_11_), channel_id=1, source_target_pairs={{0,16},{16,0},{1,17},{17,1},{2,18},{18,2},{3,19},{19,3},{4,20},{20... | collective-permute-start | bytes 1179656 | tf_op jit(solution)/shard_map/ppermute | solution.py:29
  33.0 10.0 %collective-permute-start = (bf16[1024,512]{1,0:T(8,128)(2,1)S(1)}, bf16[1024,512]{1,0:T(8,128)(2,1)S(1)}, u32[]{:S(2)}, u32[]{:S(2)}) collective-permute-start(bf16[1024,512]{1,0:T(8,128)(2,1)S(1)} %shard_map.55.refs_0_), channel_id=1, source_target_pairs={{0,1},{1,0},{2,3},{3,2},{4,5},{5,4},{6,7},{7,6},{8,9},{9,8},{10,11... | collective-permute-start | bytes 3145736 | tf_op jit(solution)/shard_map/ppermute | solution.py:29
  43.0 2.7 %collective-permute-start.11 = (bf16[1024,512]{1,0:T(8,128)(2,1)S(1)}, bf16[1024,512]{1,0:T(8,128)(2,1)S(1)}, u32[]{:S(2)}, u32[]{:S(2)}) collective-permute-start(bf16[1024,512]{1,0:T(8,128)(2,1)S(1)} %collective-permute-done.1.refs_2_), channel_id=1, source_target_pairs={{0,1},{1,0},{2,3},{3,2},{4,5},{5,4},{6,7},{7,6},{8,9},{9,8},{10,11... | collective-permute-start | bytes 3145736 | tf_op jit(solution)/shard_map/ppermute | solution.py:29
  51.3 5.0 %collective-permute-start.12 = (f32[2,4,128]{2,1,0:T(4,128)S(1)}, f32[2,4,128]{2,1,0:T(4,128)S(1)}, u32[]{:S(2)}, u32[]{:S(2)}) collective-permute-start(f32[2,4,128]{2,1,0:T(4,128)S(1)} %shard_map.57), channel_id=1, source_target_pairs={{0,1},{1,0},{2,3},{3,2},{4,5},{5,4},{6,7},{7,6},{8,9},{9,8},{10,11... | collective-permute-start | bytes 12296 | tf_op jit(solution)/shard_map/ppermute | solution.py:29
  56.4 7.1 %collective-permute-start.13 = (f32[4,128]{1,0:T(4,128)S(1)}, f32[4,128]{1,0:T(4,128)S(1)}, u32[]{:S(2)}, u32[]{:S(2)}) collective-permute-start(f32[4,128]{1,0:T(4,128)S(1)} %get-tuple-element.19), channel_id=1, source_target_pairs={{0,2},{1,3},{2,0},{3,1},{4,6},{5,7},{6,4},{7,5},{8,10},{9,11},{10,... | collective-permute-start | bytes 6152 | tf_op jit(solution)/shard_map/ppermute | solution.py:29
  61.9 3.6 %collective-permute-start.14 = (f32[4,128]{1,0:T(4,128)S(1)}, f32[4,128]{1,0:T(4,128)S(1)}, u32[]{:S(2)}, u32[]{:S(2)}) collective-permute-start(f32[4,128]{1,0:T(4,128)S(1)} %get-tuple-element.20), channel_id=1, source_target_pairs={{0,4},{4,0},{8,12},{12,8},{1,5},{5,1},{9,13},{13,9},{2,6},{6,2},{1... | collective-permute-start | bytes 6152 | tf_op jit(solution)/shard_map/ppermute | solution.py:29
  62.6 4.5 %collective-permute-start.15 = (f32[4,128]{1,0:T(4,128)S(1)}, f32[4,128]{1,0:T(4,128)S(1)}, u32[]{:S(2)}, u32[]{:S(2)}) collective-permute-start(f32[4,128]{1,0:T(4,128)S(1)} %get-tuple-element.20), channel_id=1, source_target_pairs={{0,6},{1,7},{2,4},{3,5},{4,2},{5,3},{6,0},{7,1},{8,14},{9,15},{10,... | collective-permute-start | bytes 6152 | tf_op jit(solution)/shard_map/ppermute | solution.py:29

commit v6 on v4

v6 whole, which is shorter than its diff:
```python
import functools

import jax
import jax.numpy as jnp
from jax import lax
from jax.experimental import pallas as pl
from jax.experimental.pallas import tpu as pltpu
from jax.sharding import PartitionSpec as P

BS = 128
KN = 3
MIB = 1 << 20


def swap(x, axes, sizes, move):
    perm = []
    total = 1
    for size in sizes:
        total *= size
    for source in range(total):
        coords, rest = [], source
        for size in reversed(sizes):
            coords.append(rest % size)
            rest //= size
        target = 0
        for size, at in zip(sizes, move(*reversed(coords))):
            target = target * size + at
        perm.append((source, target))
    return lax.ppermute(x, axes, perm)


def select(n_blocks, where, virt_ref, out_ref, buf, sem):
    def copy(i):
        columns = pl.ds(pl.multiple_of((2 * i + where[1]) * BS, BS), BS)
        return pltpu.make_async_copy(virt_ref.at[:, columns], buf.at[i], sem.at[i])

    for i in range(n_blocks):
        copy(i).start()
    for i in range(n_blocks):
        copy(i).wait()
        out_ref[i * BS : (i + 1) * BS, :] = buf[i].T


def after(x, *others):
    return lax.optimization_barrier((x,) + others)[0]


def contract(n_centers, where, plist, pcount, *refs):
    v_refs, m_refs, occ_ref, c_refs = refs[0:4], refs[4:12], refs[12], refs[13 : 13 + n_centers]
    out_ref, prod, acc, listed, place = refs[13 + n_centers :]
    own, parity, plane, aux_at = where[0], where[1], where[2], where[3]
    n_q = acc.shape[1]
    rows = v_refs[0].shape[1]
    blocks_here = rows // BS
    n_places = prod.shape[0]

    def used(b, k):
        block = own * blocks_here + b
        return (k < pcount[block]) & ((plist[k, block] & 1) == parity)

    def column(b, k):
        return plist[k, own * blocks_here + b] >> 1

    for c in range(n_places):
        place[c] = -1
    count = jnp.int32(blocks_here // 2)
    for i in range(blocks_here // 2):
        c = own * (blocks_here // 2) + i
        place[c] = i
        listed[i] = c
    for k in range(1, KN):
        for b in range(blocks_here):
            c = column(b, k)
            new = used(b, k) & (place[c] < 0)

            @pl.when(new)
            def _(c=c, count=count):
                place[c] = count
                listed[count] = c

            count = count + new.astype(jnp.int32)

    @pl.when((count & 1) == 1)
    def _():
        listed[count] = listed[count - 1]

    acc[...] = jnp.zeros_like(acc)

    def one_group(g, carry):
        spans = [pl.ds(pl.multiple_of(listed[2 * g + h] * BS, BS), BS) for h in range(2)]
        for i in range(4):
            for j in range(blocks_here):
                block = (own ^ i) * blocks_here + j
                span = slice(j * BS, (j + 1) * BS)
                parts = [jnp.concatenate([v_refs[i][r, span] for r in spans], axis=0)]
                weights = [jnp.concatenate([m_refs[4 * s + i][0, span, :] for s in range(2)])]
                for k in range(1, KN):
                    p = plist[k, block]
                    shard = (p // blocks_here) ^ own
                    at = pl.ds(pl.multiple_of(lax.rem(p, blocks_here) * BS, BS), BS)
                    part = jnp.concatenate([v_refs[0][r, at] for r in spans], axis=0)
                    for q in range(1, 4):
                        other = jnp.concatenate([v_refs[q][r, at] for r in spans], axis=0)
                        part = jnp.where(shard == q, other, part)
                    parts.append(part)
                    weight = jnp.concatenate([m_refs[4 * s + i][k, span, :] for s in range(2)])
                    weights.append(jnp.where(k < pcount[block], weight, jnp.zeros_like(weight)))
                res = lax.dot_general(
                    jnp.concatenate(parts, axis=1),
                    jnp.concatenate(weights, axis=1),
                    (((1,), (1,)), ((), ())),
                    preferred_element_type=jnp.float32,
                ).astype(jnp.bfloat16)
                at = pl.ds(pl.multiple_of(block * BS, BS), BS)
                for s in range(2):
                    for h in range(2):
                        prod[2 * g + h, s * BS : (s + 1) * BS, at] = res[
                            h * BS : (h + 1) * BS, s * BS : (s + 1) * BS
                        ]
        return carry

    lax.fori_loop(0, (count + 1) >> 1, one_group, 0)

    def tile(at, span, k):
        left = jnp.dot(prod[at], occ_ref[:, span], preferred_element_type=jnp.float32)
        left = left.astype(jnp.bfloat16).astype(jnp.float32)
        left = [left[s * BS : (s + 1) * BS, :].T for s in range(2)]

        def add(q, center):
            center = center.astype(jnp.float32)
            for s in range(2):
                acc[s, q] += (left[s] * center).reshape(BS // 8, 8, BS).sum(axis=0)

        if n_centers == 1:
            lax.fori_loop(0, n_q, lambda q, x: (add(q, c_refs[0][q, k, span, :]), x)[1], 0)
        else:
            for step, c_ref in zip([0, 1, 2 | plane, 3 ^ plane], c_refs):
                add(aux_at ^ step, c_ref[k, span, :])

    for i in range(blocks_here // 2):
        tile(i, pl.ds(pl.multiple_of((2 * i + parity) * BS, BS), BS), 0)
    for k in range(1, KN):
        for b in range(blocks_here):

            @pl.when(used(b, k))
            def _(b=b, k=k):
                tile(place[column(b, k)], slice(b * BS, (b + 1) * BS), k)

    for s in range(2):
        out_ref[s] = acc[s].sum(axis=1)


def on_device(sizes, three_center, virt_density, occ_density, partner_list, partner_count):
    groups, aux, atoms = sizes
    rows = three_center.shape[0]
    basis_total = virt_density.shape[1]
    group_at = lax.axis_index("groups")
    aux_at = lax.axis_index("aux")
    atom_at = lax.axis_index("atoms")
    where = jnp.stack([atom_at, aux_at & 1, group_at, aux_at]).astype(jnp.int32)
    columns = basis_total // 2
    n_blocks = columns // BS

    core = functools.partial(swap, axes=("atoms",), sizes=(atoms,), move=lambda t: (t ^ 1,))
    across = functools.partial(swap, axes=("atoms",), sizes=(atoms,), move=lambda t: (t ^ 2,))
    plane = functools.partial(swap, axes=("groups",), sizes=(groups,), move=lambda g: (g ^ 1,))
    pair = functools.partial(swap, axes=("aux",), sizes=(aux,), move=lambda a: (a ^ 1,))

    anywhere = pl.BlockSpec(memory_space=pltpu.HBM)
    scalars = pl.BlockSpec(memory_space=pltpu.SMEM)
    vmem = pl.BlockSpec(memory_space=pltpu.VMEM)

    centers = three_center[:, 0].transpose(1, 0, 2)
    far_a = across(centers)
    other = pair(centers)
    mine = pl.pallas_call(
        functools.partial(select, n_blocks),
        out_shape=jax.ShapeDtypeStruct((columns, rows), jnp.bfloat16),
        in_specs=[scalars, anywhere],
        out_specs=vmem,
        scratch_shapes=[
            pltpu.VMEM((n_blocks, rows, BS), jnp.bfloat16),
            pltpu.SemaphoreType.DMA((n_blocks,)),
        ],
        compiler_params=pltpu.CompilerParams(vmem_limit_bytes=8 * MIB),
    )(where, virt_density)
    v_across = across(mine)
    if aux == 4:
        rest_a = swap(centers, ("groups", "aux"), (groups, aux), lambda g, a: (g, a ^ (2 | g)))
        rest_b = plane(rest_a)
        all_centers = [centers, other, rest_a, rest_b]
        far_b = pair(after(far_a, other, rest_a))
    else:
        all_centers = [lax.all_gather(centers, "aux", axis=0)]
        far_b = pair(after(far_a, other))

    m_parts = [centers, core(centers), far_a, core(far_a), other, core(other), far_b]
    m_parts.append(core(far_b))
    v_parts = [mine, core(mine), v_across]
    v_parts.append(core(after(v_across, *m_parts[1:], all_centers[-1])))
    sums = pl.pallas_call(
        functools.partial(contract, len(all_centers)),
        out_shape=jax.ShapeDtypeStruct((2, aux, BS), jnp.float32),
        in_specs=[scalars] * 3 + [vmem] * (13 + len(all_centers)),
        out_specs=vmem,
        scratch_shapes=[
            pltpu.VMEM((n_blocks, 2 * BS, basis_total), jnp.bfloat16),
            pltpu.VMEM((2, aux, 8, BS), jnp.float32),
            pltpu.SMEM((n_blocks,), jnp.int32),
            pltpu.SMEM((n_blocks,), jnp.int32),
        ],
        compiler_params=pltpu.CompilerParams(vmem_limit_bytes=(24 if aux == 4 else 48) * MIB),
    )(where, partner_list.T, partner_count, *v_parts, *m_parts, occ_density, *all_centers)

    sums = sums + core(sums)
    diagonal = swap(sums[1], ("aux", "atoms"), (aux, atoms), lambda a, t: (a ^ 1, t ^ 2))
    total = sums[0] + across(sums[0]) + pair(sums[1]) + diagonal
    share = aux // atoms
    row = lax.dynamic_slice_in_dim(total, atom_at * share, share, 0)
    return (row.sum(axis=1) * jnp.float32(-(basis_total ** (-0.5))))[None, :]


def solution(mesh):
    sizes = tuple(mesh.shape[name] for name in ("groups", "aux", "atoms"))
    in_specs = (
        P("atoms", "aux", None, None),
        P(("groups", "atoms"), None),
        P("groups", "atoms"),
        P(),
        P(),
    )
    out_specs = P(("groups", "aux"), "atoms")
    return jax.shard_map(
        functools.partial(on_device, sizes),
        mesh=mesh,
        in_specs=in_specs,
        out_specs=out_specs,
        check_vma=False,
    )
```

time: 68 us -> 58.4 us (0.86)
  waiting for transfers between devices: 35.7 us -> 28.1 us
  Pallas kernels: 12.5 us -> 5.05 us
  starting transfers between devices: 13.9 us -> 21.3 us
  local copies, waits for them, and re-layouts: 3.16 us -> 1.61 us
    ppermute x16, waiting for transfers between devices: 35.7 us -> 28.1 us  [swap(): return lax.ppermute(x, axes, perm)]
    pallas_call x1, Pallas kernels: 10.9 us -> 3.41 us  [on_device(): pl.pallas_call(functools.partial(contract, len(all_centers)), out_shape=j...]
    ppermute x16, starting transfers between devices: 13.9 us -> 21.3 us  [swap(): return lax.ppermute(x, axes, perm)]
    unnamed x31 -> x10, local copies, waits for them, and re-layouts: 3.15 us -> 1.61 us
  transfers between devices with their start and end apart: 16 -> 16, of which waited for: 9 -> 10; matrix products, arithmetic and copies ran while one was open for 1% -> 0% of each run, Pallas kernels for 2% -> 3%
where the time goes in v6:
time: 58.4 us; the launch traced here: 57.9 us
  waiting for transfers between devices  28.1 us (48%)
  starting transfers between devices  21.3 us (36%)
  Pallas kernels  5.05 us (9%)
  local copies, waits for them, and re-layouts  1.61 us (3%)
  between operations  1.21 us (2%)
  other arithmetic  0.69 us (1%)
    ppermute x16, waiting for transfers between devices, swap(): return lax.ppermute(x, axes, perm)  28.1 us
    ppermute x16, starting transfers between devices, swap(): return lax.ppermute(x, axes, perm)  21.3 us
    pallas_call x1, Pallas kernels, on_device(): pl.pallas_call(functools.partial(contract, len(all_centers)), out_shape=j...  3.41 us
    pallas_call x1, Pallas kernels, on_device(): pl.pallas_call(functools.partial(select, n_blocks), out_shape=jax.ShapeDt...  1.64 us
    unnamed x10, local copies, waits for them, and re-layouts  1.61 us
  transfers between devices with their start and end apart: 16, of which 10 were waited for; matrix products, arithmetic and copies ran while one was open for 0% of the time, Pallas kernels for 3%

profile of v6, /device:TPU:0, one launch (start us, length us, event | category | flops | bytes accessed | tf_op | source)
XLA Modules:
  0.0 57.9 jit_solution(11032626731013330876)
XLA Ops:
  0.0 0.0 copy-start.4
  0.0 0.0 copy-start.3
  0.0 4.0 %collective-permute-start.7 = (bf16[3,512,128]{2,1,0:T(8,128)(2,1)}, bf16[3,512,128]{2,1,0:T(8,128)(2,1)S(1)}, u32[]{:S(2)}, u32[]{:S(2)}) collective-permute-start(bf16[3,512,128]{2,1,0:T(8,128)(2,1)} %bitcast.15), channel_id=1, source_target_pairs={{0,8},{4,12},{8,0},{12,4},{16,28},{20,24},{24,20},{28,16},{1,9},{5... | collective-permute-start | bytes 1179656 | tf_op jit(solution)/shard_map/ppermute | solution.py:29
  4.0 1.6 %collective-permute-start.5 = (bf16[3,512,128]{2,1,0:T(8,128)(2,1)}, bf16[3,512,128]{2,1,0:T(8,128)(2,1)S(1)}, u32[]{:S(2)}, u32[]{:S(2)}) collective-permute-start(bf16[3,512,128]{2,1,0:T(8,128)(2,1)} %bitcast.16), channel_id=1, source_target_pairs={{0,4},{4,0},{8,12},{12,8},{1,5},{5,1},{9,13},{13,9},{2,6},{6,2},{1... | collective-permute-start | bytes 1179656 | tf_op jit(solution)/shard_map/ppermute | solution.py:29
  5.6 1.5 %collective-permute-start.3 = (bf16[3,512,128]{2,1,0:T(8,128)(2,1)}, bf16[3,512,128]{2,1,0:T(8,128)(2,1)S(1)}, u32[]{:S(2)}, u32[]{:S(2)}) collective-permute-start(bf16[3,512,128]{2,1,0:T(8,128)(2,1)} %bitcast.17), channel_id=1, source_target_pairs={{0,2},{1,3},{2,0},{3,1},{4,6},{5,7},{6,4},{7,5},{8,10},{9,11},{10,... | collective-permute-start | bytes 1179656 | tf_op jit(solution)/shard_map/ppermute | solution.py:29
  7.1 0.1 pad_add_fusion.where
  7.2 0.0 copy-start
  7.2 1.6 %copy-done = bf16[512,2048]{1,0:T(8,128)(2,1)S(1)} copy-done((bf16[512,2048]{1,0:T(8,128)(2,1)S(1)}, bf16[512,2048]{1,0:T(8,128)(2,1)}, u32[]{:S(2)}) %copy-start) | copy-done | bytes 2097176
  8.8 0.0 copy-start.2
  8.8 0.0 copy-start.1
  8.8 1.6 %shard_map.55.refs_0_ = bf16[1024,512]{1,0:T(8,128)(2,1)S(1)} custom-call(s32[4]{0:T(128)S(1)} %pad_add_fusion.where, bf16[512,2048]{1,0:T(8,128)(2,1)S(1)} %copy-done), custom_call_target="tpu_custom_call" | custom-call | tf_op jit(solution)/shard_map/pallas_call | solution.py:176
  10.4 0.6 %collective-permute-start.1 = (bf16[1024,512]{1,0:T(8,128)(2,1)S(1)}, bf16[1024,512]{1,0:T(8,128)(2,1)S(1)}, u32[]{:S(2)}, u32[]{:S(2)}) collective-permute-start(bf16[1024,512]{1,0:T(8,128)(2,1)S(1)} %shard_map.55.refs_0_), channel_id=1, source_target_pairs={{0,2},{1,3},{2,0},{3,1},{4,6},{5,7},{6,4},{7,5},{8,10},{9,11},{10,... | collective-permute-start | bytes 3145736 | tf_op jit(solution)/shard_map/ppermute | solution.py:29
  11.0 0.0 copy-done.2
  11.0 0.0 collective-permute-start.2
  11.0 10.9 %collective-permute-done.7.refs_15_ = bf16[3,512,128]{2,1,0:T(8,128)(2,1)S(1)} collective-permute-done((bf16[3,512,128]{2,1,0:T(8,128)(2,1)}, bf16[3,512,128]{2,1,0:T(8,128)(2,1)S(1)}, u32[]{:S(2)}, u32[]{:S(2)}) %collective-permute-start.7) | collective-permute-done | bytes 393248 | tf_op jit(solution)/shard_map/ppermute | solution.py:29
  21.9 0.2 collective-permute-done.5.refs_8_.refs_14_
  22.1 0.0 collective-permute-done.3.refs_6_
  22.1 1.5 %collective-permute-start.8 = (bf16[3,512,128]{2,1,0:T(8,128)(2,1)S(1)}, bf16[3,512,128]{2,1,0:T(8,128)(2,1)S(1)}, u32[]{:S(2)}, u32[]{:S(2)}) collective-permute-start(bf16[3,512,128]{2,1,0:T(8,128)(2,1)S(1)} %collective-permute-done.3.refs_6_), channel_id=1, source_target_pairs={{0,4},{4,0},{8,12},{12,8},{1,5},{5,1},{9,13},{13,9},{2,6},{6,2},{1... | collective-permute-start | bytes 1179656 | tf_op jit(solution)/shard_map/ppermute | solution.py:29
  23.6 2.5 %collective-permute-start.10 = (bf16[3,512,128]{2,1,0:T(8,128)(2,1)S(1)}, bf16[3,512,128]{2,1,0:T(8,128)(2,1)S(1)}, u32[]{:S(2)}, u32[]{:S(2)}) collective-permute-start(bf16[3,512,128]{2,1,0:T(8,128)(2,1)S(1)} %collective-permute-done.7.refs_15_), channel_id=1, source_target_pairs={{0,16},{16,0},{1,17},{17,1},{2,18},{18,2},{3,19},{19,3},{4,20},{20... | collective-permute-start | bytes 1179656 | tf_op jit(solution)/shard_map/ppermute | solution.py:29
  26.1 0.0 collective-permute-start.6
  26.1 0.0 collective-permute-done.2.refs_5_
  26.1 0.5 collective-permute-start.4
  26.6 5.5 %collective-permute-done.8.refs_10_ = bf16[3,512,128]{2,1,0:T(8,128)(2,1)S(1)} collective-permute-done((bf16[3,512,128]{2,1,0:T(8,128)(2,1)S(1)}, bf16[3,512,128]{2,1,0:T(8,128)(2,1)S(1)}, u32[]{:S(2)}, u32[]{:S(2)}) %collective-permute-start.8) | collective-permute-done | bytes 393248 | tf_op jit(solution)/shard_map/ppermute | solution.py:29
  32.1 0.0 collective-permute-start.9
  32.2 2.0 %collective-permute-done.10.refs_16_ = bf16[3,512,128]{2,1,0:T(8,128)(2,1)S(1)} collective-permute-done((bf16[3,512,128]{2,1,0:T(8,128)(2,1)S(1)}, bf16[3,512,128]{2,1,0:T(8,128)(2,1)S(1)}, u32[]{:S(2)}, u32[]{:S(2)}) %collective-permute-start.10) | collective-permute-done | bytes 393248 | tf_op jit(solution)/shard_map/ppermute | solution.py:29
  34.1 0.0 collective-permute-start
  34.1 0.0 collective-permute-done.6.refs_9_
  34.1 0.0 collective-permute-done.4.refs_7_
  34.1 4.5 %collective-permute-done.1.refs_2_ = bf16[1024,512]{1,0:T(8,128)(2,1)S(1)} collective-permute-done((bf16[1024,512]{1,0:T(8,128)(2,1)S(1)}, bf16[1024,512]{1,0:T(8,128)(2,1)S(1)}, u32[]{:S(2)}, u32[]{:S(2)}) %collective-permute-start.1) | collective-permute-done | bytes 1048608 | tf_op jit(solution)/shard_map/ppermute | solution.py:29
  38.6 0.0 collective-permute-done.9.refs_11_
  38.6 0.0 collective-permute-start.11
  38.6 0.0 collective-permute-done.refs_1_
  38.6 2.7 %collective-permute-done.11.refs_3_ = bf16[1024,512]{1,0:T(8,128)(2,1)S(1)} collective-permute-done((bf16[1024,512]{1,0:T(8,128)(2,1)S(1)}, bf16[1024,512]{1,0:T(8,128)(2,1)S(1)}, u32[]{:S(2)}, u32[]{:S(2)}) %collective-permute-start.11) | collective-permute-done | bytes 1048608 | tf_op jit(solution)/shard_map/ppermute | solution.py:29
  41.3 0.0 copy-done.4
  41.3 0.0 copy-done.3
  41.3 0.0 copy-done.1
  41.3 3.4 %shard_map.56 = f32[2,4,128]{2,1,0:T(4,128)S(1)} custom-call(s32[4]{0:T(128)S(1)} %pad_add_fusion.where, s32[3,16]{1,0:T(4,128)S(1)} %bitcast.21, s32[16]{0:T(128)S(1)} %copy-done.4, bf16[1024,512]{1,0:T(8,128)(2,1)S(1)} %shard_map.55.refs_0_, bf16[1024,512]{1,0:T(8,128)(2,1)S(1)} %collective-permute-done.refs_1_, ...), custom_call_target="tpu_custom_call" | custom-call | tf_op jit(solution)/shard_map/pallas_call | solution.py:201
  44.7 5.5 %collective-permute-start.12 = (f32[2,4,128]{2,1,0:T(4,128)S(1)}, f32[2,4,128]{2,1,0:T(4,128)S(1)}, u32[]{:S(2)}, u32[]{:S(2)}) collective-permute-start(f32[2,4,128]{2,1,0:T(4,128)S(1)} %shard_map.56), channel_id=1, source_target_pairs={{0,1},{1,0},{2,3},{3,2},{4,5},{5,4},{6,7},{7,6},{8,9},{9,8},{10,11... | collective-permute-start | bytes 12296 | tf_op jit(solution)/shard_map/ppermute | solution.py:29
  50.2 0.8 %collective-permute-done.12 = f32[2,4,128]{2,1,0:T(4,128)S(1)} collective-permute-done((f32[2,4,128]{2,1,0:T(4,128)S(1)}, f32[2,4,128]{2,1,0:T(4,128)S(1)}, u32[]{:S(2)}, u32[]{:S(2)}) %collective-permute-start.12) | collective-permute-done | bytes 4128 | tf_op jit(solution)/shard_map/ppermute | solution.py:29
  51.0 0.0 collective-permute-start.13
  51.0 1.4 %collective-permute-start.15 = (f32[4,128]{1,0:T(4,128)S(1)}, f32[4,128]{1,0:T(4,128)S(1)}, u32[]{:S(2)}, u32[]{:S(2)}) collective-permute-start(f32[4,128]{1,0:T(4,128)S(1)} %get-tuple-element.10), channel_id=1, source_target_pairs={{0,6},{1,7},{2,4},{3,5},{4,2},{5,3},{6,0},{7,1},{8,14},{9,15},{10,... | collective-permute-start | bytes 6152 | tf_op jit(solution)/shard_map/ppermute | solution.py:29
  52.5 2.1 %collective-permute-start.14 = (f32[4,128]{1,0:T(4,128)S(1)}, f32[4,128]{1,0:T(4,128)S(1)}, u32[]{:S(2)}, u32[]{:S(2)}) collective-permute-start(f32[4,128]{1,0:T(4,128)S(1)} %get-tuple-element.10), channel_id=1, source_target_pairs={{0,4},{4,0},{8,12},{12,8},{1,5},{5,1},{9,13},{13,9},{2,6},{6,2},{1... | collective-permute-start | bytes 6152 | tf_op jit(solution)/shard_map/ppermute | solution.py:29
  54.5 0.1 collective-permute-done.13
  54.6 1.0 %collective-permute-done.15 = f32[4,128]{1,0:T(4,128)S(1)} collective-permute-done((f32[4,128]{1,0:T(4,128)S(1)}, f32[4,128]{1,0:T(4,128)S(1)}, u32[]{:S(2)}, u32[]{:S(2)}) %collective-permute-start.15) | collective-permute-done | bytes 2080 | tf_op jit(solution)/shard_map/ppermute | solution.py:29
  55.6 0.5 collective-permute-done.14
  56.1 0.6 %dynamic-slice_reduce_fusion = f32[]{:T(128)} fusion(f32[4,128]{1,0:T(4,128)S(1)} %add_add_fusion, s32[]{:T(128)S(6)} %select_n.3), kind=kLoop, calls=%fused_computation.4 | loop fusion | flops 127 | bytes 520 | tf_op jit(solution)/shard_map/reduce_sum | solution.py:220
  (3 shorter events, 0.0 us)
Async XLA Ops:
  0.0 41.3 %copy-start.4 = (s32[16]{0:T(128)S(1)}, s32[16]{0:T(128)}, u32[]{:S(2)}) copy-start(s32[16]{0:T(128)} %pcount.1) | copy-start | bytes 196
  0.0 41.3 %copy-start.3 = (s32[16,3]{0,1:T(4,128)S(1)}, s32[16,3]{0,1:T(4,128)}, u32[]{:S(2)}) copy-start(s32[16,3]{0,1:T(4,128)} %param.8) | copy-start | bytes 580
  0.0 21.9 %collective-permute-start.7 = (bf16[3,512,128]{2,1,0:T(8,128)(2,1)}, bf16[3,512,128]{2,1,0:T(8,128)(2,1)S(1)}, u32[]{:S(2)}, u32[]{:S(2)}) collective-permute-start(bf16[3,512,128]{2,1,0:T(8,128)(2,1)} %bitcast.15), channel_id=1, source_target_pairs={{0,8},{4,12},{8,0},{12,4},{16,28},{20,24},{24,20},{28,16},{1,9},{5... | collective-permute-start | bytes 1179656 | tf_op jit(solution)/shard_map/ppermute | solution.py:29
  4.0 18.0 %collective-permute-start.5 = (bf16[3,512,128]{2,1,0:T(8,128)(2,1)}, bf16[3,512,128]{2,1,0:T(8,128)(2,1)S(1)}, u32[]{:S(2)}, u32[]{:S(2)}) collective-permute-start(bf16[3,512,128]{2,1,0:T(8,128)(2,1)} %bitcast.16), channel_id=1, source_target_pairs={{0,4},{4,0},{8,12},{12,8},{1,5},{5,1},{9,13},{13,9},{2,6},{6,2},{1... | collective-permute-start | bytes 1179656 | tf_op jit(solution)/shard_map/ppermute | solution.py:29
  5.6 16.5 %collective-permute-start.3 = (bf16[3,512,128]{2,1,0:T(8,128)(2,1)}, bf16[3,512,128]{2,1,0:T(8,128)(2,1)S(1)}, u32[]{:S(2)}, u32[]{:S(2)}) collective-permute-start(bf16[3,512,128]{2,1,0:T(8,128)(2,1)} %bitcast.17), channel_id=1, source_target_pairs={{0,2},{1,3},{2,0},{3,1},{4,6},{5,7},{6,4},{7,5},{8,10},{9,11},{10,... | collective-permute-start | bytes 1179656 | tf_op jit(solution)/shard_map/ppermute | solution.py:29
  7.2 1.6 %copy-start = (bf16[512,2048]{1,0:T(8,128)(2,1)S(1)}, bf16[512,2048]{1,0:T(8,128)(2,1)}, u32[]{:S(2)}) copy-start(bf16[512,2048]{1,0:T(8,128)(2,1)} %virt_ref.1) | copy-start | bytes 6291460
  8.8 2.3 %copy-start.2 = (bf16[512,1,3,128]{3,0,2,1:T(8,128)(2,1)S(1)}, bf16[512,1,3,128]{3,0,2,1:T(8,128)(2,1)}, u32[]{:S(2)}) copy-start(bf16[512,1,3,128]{3,0,2,1:T(8,128)(2,1)} %param.5) | copy-start | bytes 1179652
  8.8 32.5 %copy-start.1 = (bf16[2048,512]{1,0:T(8,128)(2,1)S(1)}, bf16[2048,512]{1,0:T(8,128)(2,1)}, u32[]{:S(2)}) copy-start(bf16[2048,512]{1,0:T(8,128)(2,1)} %refs_12_.1) | copy-start | bytes 6291460
  10.4 28.2 %collective-permute-start.1 = (bf16[1024,512]{1,0:T(8,128)(2,1)S(1)}, bf16[1024,512]{1,0:T(8,128)(2,1)S(1)}, u32[]{:S(2)}, u32[]{:S(2)}) collective-permute-start(bf16[1024,512]{1,0:T(8,128)(2,1)S(1)} %shard_map.55.refs_0_), channel_id=1, source_target_pairs={{0,2},{1,3},{2,0},{3,1},{4,6},{5,7},{6,4},{7,5},{8,10},{9,11},{10,... | collective-permute-start | bytes 3145736 | tf_op jit(solution)/shard_map/ppermute | solution.py:29
  11.0 15.1 %collective-permute-start.2 = (bf16[3,512,128]{2,1,0:T(8,128)(2,1)S(1)}, bf16[3,512,128]{2,1,0:T(8,128)(2,1)S(1)}, u32[]{:S(2)}, u32[]{:S(2)}) collective-permute-start(bf16[3,512,128]{2,1,0:T(8,128)(2,1)S(1)} %bitcast.18), channel_id=1, source_target_pairs={{0,1},{1,0},{2,3},{3,2},{4,5},{5,4},{6,7},{7,6},{8,9},{9,8},{10,11... | collective-permute-start | bytes 1179656 | tf_op jit(solution)/shard_map/ppermute | solution.py:29
  22.1 10.1 %collective-permute-start.8 = (bf16[3,512,128]{2,1,0:T(8,128)(2,1)S(1)}, bf16[3,512,128]{2,1,0:T(8,128)(2,1)S(1)}, u32[]{:S(2)}, u32[]{:S(2)}) collective-permute-start(bf16[3,512,128]{2,1,0:T(8,128)(2,1)S(1)} %collective-permute-done.3.refs_6_), channel_id=1, source_target_pairs={{0,4},{4,0},{8,12},{12,8},{1,5},{5,1},{9,13},{13,9},{2,6},{6,2},{1... | collective-permute-start | bytes 1179656 | tf_op jit(solution)/shard_map/ppermute | solution.py:29
  23.6 10.5 %collective-permute-start.10 = (bf16[3,512,128]{2,1,0:T(8,128)(2,1)S(1)}, bf16[3,512,128]{2,1,0:T(8,128)(2,1)S(1)}, u32[]{:S(2)}, u32[]{:S(2)}) collective-permute-start(bf16[3,512,128]{2,1,0:T(8,128)(2,1)S(1)} %collective-permute-done.7.refs_15_), channel_id=1, source_target_pairs={{0,16},{16,0},{1,17},{17,1},{2,18},{18,2},{3,19},{19,3},{4,20},{20... | collective-permute-start | bytes 1179656 | tf_op jit(solution)/shard_map/ppermute | solution.py:29
  26.1 8.0 %collective-permute-start.6 = (bf16[3,512,128]{2,1,0:T(8,128)(2,1)S(1)}, bf16[3,512,128]{2,1,0:T(8,128)(2,1)S(1)}, u32[]{:S(2)}, u32[]{:S(2)}) collective-permute-start(bf16[3,512,128]{2,1,0:T(8,128)(2,1)S(1)} %collective-permute-done.5.refs_8_.refs_14_), channel_id=1, source_target_pairs={{0,1},{1,0},{2,3},{3,2},{4,5},{5,4},{6,7},{7,6},{8,9},{9,8},{10,11... | collective-permute-start | bytes 1179656 | tf_op jit(solution)/shard_map/ppermute | solution.py:29
  26.1 8.0 %collective-permute-start.4 = (bf16[3,512,128]{2,1,0:T(8,128)(2,1)S(1)}, bf16[3,512,128]{2,1,0:T(8,128)(2,1)S(1)}, u32[]{:S(2)}, u32[]{:S(2)}) collective-permute-start(bf16[3,512,128]{2,1,0:T(8,128)(2,1)S(1)} %collective-permute-done.3.refs_6_), channel_id=1, source_target_pairs={{0,1},{1,0},{2,3},{3,2},{4,5},{5,4},{6,7},{7,6},{8,9},{9,8},{10,11... | collective-permute-start | bytes 1179656 | tf_op jit(solution)/shard_map/ppermute | solution.py:29
  32.1 6.4 %collective-permute-start.9 = (bf16[3,512,128]{2,1,0:T(8,128)(2,1)S(1)}, bf16[3,512,128]{2,1,0:T(8,128)(2,1)S(1)}, u32[]{:S(2)}, u32[]{:S(2)}) collective-permute-start(bf16[3,512,128]{2,1,0:T(8,128)(2,1)S(1)} %collective-permute-done.8.refs_10_), channel_id=1, source_target_pairs={{0,1},{1,0},{2,3},{3,2},{4,5},{5,4},{6,7},{7,6},{8,9},{9,8},{10,11... | collective-permute-start | bytes 1179656 | tf_op jit(solution)/shard_map/ppermute | solution.py:29
  34.1 4.5 %collective-permute-start = (bf16[1024,512]{1,0:T(8,128)(2,1)S(1)}, bf16[1024,512]{1,0:T(8,128)(2,1)S(1)}, u32[]{:S(2)}, u32[]{:S(2)}) collective-permute-start(bf16[1024,512]{1,0:T(8,128)(2,1)S(1)} %shard_map.55.refs_0_), channel_id=1, source_target_pairs={{0,1},{1,0},{2,3},{3,2},{4,5},{5,4},{6,7},{7,6},{8,9},{9,8},{10,11... | collective-permute-start | bytes 3145736 | tf_op jit(solution)/shard_map/ppermute | solution.py:29
  38.6 2.7 %collective-permute-start.11 = (bf16[1024,512]{1,0:T(8,128)(2,1)S(1)}, bf16[1024,512]{1,0:T(8,128)(2,1)S(1)}, u32[]{:S(2)}, u32[]{:S(2)}) collective-permute-start(bf16[1024,512]{1,0:T(8,128)(2,1)S(1)} %collective-permute-done.1.refs_2_), channel_id=1, source_target_pairs={{0,1},{1,0},{2,3},{3,2},{4,5},{5,4},{6,7},{7,6},{8,9},{9,8},{10,11... | collective-permute-start | bytes 3145736 | tf_op jit(solution)/shard_map/ppermute | solution.py:29
  44.7 6.3 %collective-permute-start.12 = (f32[2,4,128]{2,1,0:T(4,128)S(1)}, f32[2,4,128]{2,1,0:T(4,128)S(1)}, u32[]{:S(2)}, u32[]{:S(2)}) collective-permute-start(f32[2,4,128]{2,1,0:T(4,128)S(1)} %shard_map.56), channel_id=1, source_target_pairs={{0,1},{1,0},{2,3},{3,2},{4,5},{5,4},{6,7},{7,6},{8,9},{9,8},{10,11... | collective-permute-start | bytes 12296 | tf_op jit(solution)/shard_map/ppermute | solution.py:29
  51.0 3.6 %collective-permute-start.13 = (f32[4,128]{1,0:T(4,128)S(1)}, f32[4,128]{1,0:T(4,128)S(1)}, u32[]{:S(2)}, u32[]{:S(2)}) collective-permute-start(f32[4,128]{1,0:T(4,128)S(1)} %get-tuple-element.9), channel_id=1, source_target_pairs={{0,2},{1,3},{2,0},{3,1},{4,6},{5,7},{6,4},{7,5},{8,10},{9,11},{10,... | collective-permute-start | bytes 6152 | tf_op jit(solution)/shard_map/ppermute | solution.py:29
  51.0 4.5 %collective-permute-start.15 = (f32[4,128]{1,0:T(4,128)S(1)}, f32[4,128]{1,0:T(4,128)S(1)}, u32[]{:S(2)}, u32[]{:S(2)}) collective-permute-start(f32[4,128]{1,0:T(4,128)S(1)} %get-tuple-element.10), channel_id=1, source_target_pairs={{0,6},{1,7},{2,4},{3,5},{4,2},{5,3},{6,0},{7,1},{8,14},{9,15},{10,... | collective-permute-start | bytes 6152 | tf_op jit(solution)/shard_map/ppermute | solution.py:29
  52.5 3.6 %collective-permute-start.14 = (f32[4,128]{1,0:T(4,128)S(1)}, f32[4,128]{1,0:T(4,128)S(1)}, u32[]{:S(2)}, u32[]{:S(2)}) collective-permute-start(f32[4,128]{1,0:T(4,128)S(1)} %get-tuple-element.10), channel_id=1, source_target_pairs={{0,4},{4,0},{8,12},{12,8},{1,5},{5,1},{9,13},{13,9},{2,6},{6,2},{1... | collective-permute-start | bytes 6152 | tf_op jit(solution)/shard_map/ppermute | solution.py:29

commit v7 on v6

--- a/solution.py
+++ b/solution.py
@@ -46,8 +46,9 @@
 
 
 def contract(n_centers, where, plist, pcount, *refs):
-    v_refs, m_refs, occ_ref, c_refs = refs[0:4], refs[4:12], refs[12], refs[13 : 13 + n_centers]
-    out_ref, prod, acc, listed, place = refs[13 + n_centers :]
+    v_refs, m_refs, f_refs, occ_ref = refs[0:4], refs[4:8], refs[8:16], refs[16]
+    c_refs = refs[17 : 17 + n_centers]
+    out_ref, prod, acc, listed, place = refs[17 + n_centers :]
     own, parity, plane, aux_at = where[0], where[1], where[2], where[3]
     n_q = acc.shape[1]
     rows = v_refs[0].shape[1]
@@ -86,6 +87,24 @@
 
     acc[...] = jnp.zeros_like(acc)
 
+    def weight_tile(i, k, j):
+        span = slice(j * BS, (j + 1) * BS)
+        tiles = []
+        for s in range(2):
+            if i < 2:
+                tiles.append(m_refs[2 * s + i][k, span, :])
+            else:
+                half, row = divmod(j * BS, rows // 2)
+                at = 4 * s + 2 * (i - 2)
+                tiles.append(
+                    jnp.where(
+                        plane == half,
+                        f_refs[at][k, row : row + BS, :],
+                        f_refs[at + 1][k, row : row + BS, :],
+                    )
+                )
+        return jnp.concatenate(tiles)
+
     def one_group(g, carry):
         spans = [pl.ds(pl.multiple_of(listed[2 * g + h] * BS, BS), BS) for h in range(2)]
         for i in range(4):
@@ -93,7 +112,7 @@
                 block = (own ^ i) * blocks_here + j
                 span = slice(j * BS, (j + 1) * BS)
                 parts = [jnp.concatenate([v_refs[i][r, span] for r in spans], axis=0)]
-                weights = [jnp.concatenate([m_refs[4 * s + i][0, span, :] for s in range(2)])]
+                weights = [weight_tile(i, 0, j)]
                 for k in range(1, KN):
                     p = plist[k, block]
                     shard = (p // blocks_here) ^ own
@@ -103,7 +122,7 @@
                         other = jnp.concatenate([v_refs[q][r, at] for r in spans], axis=0)
                         part = jnp.where(shard == q, other, part)
                     parts.append(part)
-                    weight = jnp.concatenate([m_refs[4 * s + i][k, span, :] for s in range(2)])
+                    weight = weight_tile(i, k, j)
                     weights.append(jnp.where(k < pcount[block], weight, jnp.zeros_like(weight)))
                 res = lax.dot_general(
                     jnp.concatenate(parts, axis=1),
@@ -171,7 +190,9 @@
     vmem = pl.BlockSpec(memory_space=pltpu.VMEM)
 
     centers = three_center[:, 0].transpose(1, 0, 2)
-    far_a = across(centers)
+    half = rows // 2
+    far_half = lax.dynamic_slice_in_dim(centers, group_at * half, half, 1)
+    far_x = across(far_half)
     other = pair(centers)
     mine = pl.pallas_call(
         functools.partial(select, n_blocks),
@@ -183,25 +204,31 @@
             pltpu.SemaphoreType.DMA((n_blocks,)),
         ],
         compiler_params=pltpu.CompilerParams(vmem_limit_bytes=8 * MIB),
-    )(where, virt_density)
+    )(where, after(virt_density, far_half))
     v_across = across(mine)
+    far_y = plane(far_x)
+    early = [other]
     if aux == 4:
         rest_a = swap(centers, ("groups", "aux"), (groups, aux), lambda g, a: (g, a ^ (2 | g)))
         rest_b = plane(rest_a)
         all_centers = [centers, other, rest_a, rest_b]
-        far_b = pair(after(far_a, other, rest_a))
+        early.append(rest_a)
     else:
         all_centers = [lax.all_gather(centers, "aux", axis=0)]
-        far_b = pair(after(far_a, other))
-
-    m_parts = [centers, core(centers), far_a, core(far_a), other, core(other), far_b]
-    m_parts.append(core(far_b))
+    pair_x, pair_y = pair(after(far_x, far_y)), pair(far_y)
+
+    far_x_core = core(after(far_x, far_y, *early))
+    far_y_core = core(after(far_y, far_x_core))
+    centers_core = core(after(centers, far_y_core))
+    other_core = core(other)
+    m_parts = [centers, centers_core, other, other_core, far_x, far_y, far_x_core, far_y_core]
+    m_parts += [pair_x, pair_y, core(pair_x), core(pair_y)]
     v_parts = [mine, core(mine), v_across]
     v_parts.append(core(after(v_across, *m_parts[1:], all_centers[-1])))
     sums = pl.pallas_call(
         functools.partial(contract, len(all_centers)),
         out_shape=jax.ShapeDtypeStruct((2, aux, BS), jnp.float32),
-        in_specs=[scalars] * 3 + [vmem] * (13 + len(all_centers)),
+        in_specs=[scalars] * 3 + [vmem] * (17 + len(all_centers)),
         out_specs=vmem,
         scratch_shapes=[
             pltpu.VMEM((n_blocks, 2 * BS, basis_total), jnp.bfloat16),

time: 58.4 us -> 59.4 us (1.017); the launches traced: 57.9 us -> 58.2 us
  Pallas kernels: 5.05 us -> 9 us
  waiting for transfers between devices: 28.1 us -> 25.6 us
  starting transfers between devices: 21.3 us -> 19.1 us
  local copies, waits for them, and re-layouts: 1.61 us -> 2.62 us
    pallas_call x1, Pallas kernels: 3.41 us -> 7.36 us  [on_device(): pl.pallas_call(functools.partial(contract, len(all_centers)), out_shape=j...]
    ppermute x16 -> x20, waiting for transfers between devices: 28.1 us -> 25.6 us  [swap(): return lax.ppermute(x, axes, perm)]
    ppermute x16 -> x20, starting transfers between devices: 21.3 us -> 19.1 us  [swap(): return lax.ppermute(x, axes, perm)]
    dynamic_slice x0 -> x1, local copies, waits for them, and re-layouts: none -> 1.01 us  [on_device(): far_half = lax.dynamic_slice_in_dim(centers, group_at * half, half, 1)]
  transfers between devices with their start and end apart: 16 -> 20, of which waited for: 10 -> 13; matrix products, arithmetic and copies ran while one was open for 0% -> 0% of each run, Pallas kernels for 3% -> 3%
where the time goes in v7:
time: 59.4 us; the launch traced here: 58.2 us
  waiting for transfers between devices  25.6 us (43%)
  starting transfers between devices  19.1 us (32%)
  Pallas kernels  9 us (15%)
  local copies, waits for them, and re-layouts  2.62 us (4%)
  between operations  1.23 us (2%)
  other arithmetic  0.69 us (1%)
    ppermute x20, waiting for transfers between devices, swap(): return lax.ppermute(x, axes, perm)  25.6 us
    ppermute x20, starting transfers between devices, swap(): return lax.ppermute(x, axes, perm)  19.1 us
    pallas_call x1, Pallas kernels, on_device(): pl.pallas_call(functools.partial(contract, len(all_centers)), out_shape=j...  7.36 us
    pallas_call x1, Pallas kernels, on_device(): pl.pallas_call(functools.partial(select, n_blocks), out_shape=jax.ShapeDt...  1.64 us
    unnamed x10, local copies, waits for them, and re-layouts  1.61 us
  transfers between devices with their start and end apart: 20, of which 13 were waited for; matrix products, arithmetic and copies ran while one was open for 0% of the time, Pallas kernels for 3%

profile of v7, /device:TPU:0, one launch (start us, length us, event | category | flops | bytes accessed | tf_op | source)
XLA Modules:
  0.0 58.2 jit_solution(4045685018860882988)
XLA Ops:
  0.0 1.0 %dynamic-slice_bitcast_fusion = bf16[3,256,128]{2,1,0:T(8,128)(2,1)S(1)} fusion(bf16[512,1,3,128]{3,0,2,1:T(8,128)(2,1)} %param.5, s32[]{:T(128)S(6)} %select_n.6), kind=kLoop, calls=%fused_computation | loop fusion | bytes 393220 | tf_op jit(solution)/shard_map/dynamic_slice | solution.py:194
  1.0 3.0 %collective-permute-start.2 = (bf16[3,256,128]{2,1,0:T(8,128)(2,1)S(1)}, bf16[3,256,128]{2,1,0:T(8,128)(2,1)S(1)}, u32[]{:S(2)}, u32[]{:S(2)}) collective-permute-start(bf16[3,256,128]{2,1,0:T(8,128)(2,1)S(1)} %dynamic-slice_bitcast_fusion), channel_id=1, source_target_pairs={{0,2},{1,3},{2,0},{3,1},{4,6},{5,7},{6,4},{7,5},{8,10},{9,11},{10,... | collective-permute-start | bytes 589832 | tf_op jit(solution)/shard_map/ppermute | solution.py:29
  4.0 2.6 %collective-permute-start.5 = (bf16[3,512,128]{2,1,0:T(8,128)(2,1)}, bf16[3,512,128]{2,1,0:T(8,128)(2,1)S(1)}, u32[]{:S(2)}, u32[]{:S(2)}) collective-permute-start(bf16[3,512,128]{2,1,0:T(8,128)(2,1)} %bitcast.19), channel_id=1, source_target_pairs={{0,8},{4,12},{8,0},{12,4},{16,28},{20,24},{24,20},{28,16},{1,9},{5... | collective-permute-start | bytes 1179656 | tf_op jit(solution)/shard_map/ppermute | solution.py:29
  6.6 1.6 %collective-permute-start.4 = (bf16[3,512,128]{2,1,0:T(8,128)(2,1)}, bf16[3,512,128]{2,1,0:T(8,128)(2,1)S(1)}, u32[]{:S(2)}, u32[]{:S(2)}) collective-permute-start(bf16[3,512,128]{2,1,0:T(8,128)(2,1)} %bitcast.20), channel_id=1, source_target_pairs={{0,4},{4,0},{8,12},{12,8},{1,5},{5,1},{9,13},{13,9},{2,6},{6,2},{1... | collective-permute-start | bytes 1179656 | tf_op jit(solution)/shard_map/ppermute | solution.py:29
  8.2 0.1 pad_add_fusion.where
  8.3 1.6 %copy-done.1 = bf16[512,2048]{1,0:T(8,128)(2,1)S(1)} copy-done((bf16[512,2048]{1,0:T(8,128)(2,1)S(1)}, bf16[512,2048]{1,0:T(8,128)(2,1)}, u32[]{:S(2)}) %copy-start.1) | copy-done | bytes 2097176
  9.9 1.6 %shard_map.55.refs_0_ = bf16[1024,512]{1,0:T(8,128)(2,1)S(1)} custom-call(s32[4]{0:T(128)S(1)} %pad_add_fusion.where, bf16[512,2048]{1,0:T(8,128)(2,1)S(1)} %copy-done.1), custom_call_target="tpu_custom_call" | custom-call | tf_op jit(solution)/shard_map/pallas_call | solution.py:197
  11.5 0.6 %collective-permute-start.1 = (bf16[1024,512]{1,0:T(8,128)(2,1)S(1)}, bf16[1024,512]{1,0:T(8,128)(2,1)S(1)}, u32[]{:S(2)}, u32[]{:S(2)}) collective-permute-start(bf16[1024,512]{1,0:T(8,128)(2,1)S(1)} %shard_map.55.refs_0_), channel_id=1, source_target_pairs={{0,2},{1,3},{2,0},{3,1},{4,6},{5,7},{6,4},{7,5},{8,10},{9,11},{10,... | collective-permute-start | bytes 3145736 | tf_op jit(solution)/shard_map/ppermute | solution.py:29
  12.1 0.0 collective-permute-done.2.refs_8_
  12.1 1.0 %collective-permute-start.3 = (bf16[3,256,128]{2,1,0:T(8,128)(2,1)S(1)}, bf16[3,256,128]{2,1,0:T(8,128)(2,1)S(1)}, u32[]{:S(2)}, u32[]{:S(2)}) collective-permute-start(bf16[3,256,128]{2,1,0:T(8,128)(2,1)S(1)} %collective-permute-done.2.refs_8_), channel_id=1, source_target_pairs={{0,16},{16,0},{1,17},{17,1},{2,18},{18,2},{3,19},{19,3},{4,20},{20... | collective-permute-start | bytes 589832 | tf_op jit(solution)/shard_map/ppermute | solution.py:29
  13.1 4.7 %collective-permute-done.3.refs_9_ = bf16[3,256,128]{2,1,0:T(8,128)(2,1)S(1)} collective-permute-done((bf16[3,256,128]{2,1,0:T(8,128)(2,1)S(1)}, bf16[3,256,128]{2,1,0:T(8,128)(2,1)S(1)}, u32[]{:S(2)}, u32[]{:S(2)}) %collective-permute-start.3) | collective-permute-done | bytes 196640 | tf_op jit(solution)/shard_map/ppermute | solution.py:29
  17.8 6.5 %collective-permute-done.5.refs_19_ = bf16[3,512,128]{2,1,0:T(8,128)(2,1)S(1)} collective-permute-done((bf16[3,512,128]{2,1,0:T(8,128)(2,1)}, bf16[3,512,128]{2,1,0:T(8,128)(2,1)S(1)}, u32[]{:S(2)}, u32[]{:S(2)}) %collective-permute-start.5) | collective-permute-done | bytes 393248 | tf_op jit(solution)/shard_map/ppermute | solution.py:29
  24.2 0.2 collective-permute-done.4.refs_6_.refs_18_
  24.4 0.0 collective-permute-start.6
  24.4 1.4 %collective-permute-start.10 = (bf16[3,256,128]{2,1,0:T(8,128)(2,1)S(1)}, bf16[3,256,128]{2,1,0:T(8,128)(2,1)S(1)}, u32[]{:S(2)}, u32[]{:S(2)}) collective-permute-start(bf16[3,256,128]{2,1,0:T(8,128)(2,1)S(1)} %collective-permute-done.2.refs_8_), channel_id=1, source_target_pairs={{0,4},{4,0},{8,12},{12,8},{1,5},{5,1},{9,13},{13,9},{2,6},{6,2},{1... | collective-permute-start | bytes 589832 | tf_op jit(solution)/shard_map/ppermute | solution.py:29
  25.9 0.0 collective-permute-done.6.refs_10_
  25.9 0.2 collective-permute-start.7
  26.1 1.4 %collective-permute-start.11 = (bf16[3,256,128]{2,1,0:T(8,128)(2,1)S(1)}, bf16[3,256,128]{2,1,0:T(8,128)(2,1)S(1)}, u32[]{:S(2)}, u32[]{:S(2)}) collective-permute-start(bf16[3,256,128]{2,1,0:T(8,128)(2,1)S(1)} %collective-permute-done.3.refs_9_), channel_id=1, source_target_pairs={{0,4},{4,0},{8,12},{12,8},{1,5},{5,1},{9,13},{13,9},{2,6},{6,2},{1... | collective-permute-start | bytes 589832 | tf_op jit(solution)/shard_map/ppermute | solution.py:29
  27.5 2.5 %collective-permute-start.14 = (bf16[3,512,128]{2,1,0:T(8,128)(2,1)S(1)}, bf16[3,512,128]{2,1,0:T(8,128)(2,1)S(1)}, u32[]{:S(2)}, u32[]{:S(2)}) collective-permute-start(bf16[3,512,128]{2,1,0:T(8,128)(2,1)S(1)} %collective-permute-done.5.refs_19_), channel_id=1, source_target_pairs={{0,16},{16,0},{1,17},{17,1},{2,18},{18,2},{3,19},{19,3},{4,20},{20... | collective-permute-start | bytes 1179656 | tf_op jit(solution)/shard_map/ppermute | solution.py:29
  30.0 2.1 %collective-permute-done.10.refs_12_ = bf16[3,256,128]{2,1,0:T(8,128)(2,1)S(1)} collective-permute-done((bf16[3,256,128]{2,1,0:T(8,128)(2,1)S(1)}, bf16[3,256,128]{2,1,0:T(8,128)(2,1)S(1)}, u32[]{:S(2)}, u32[]{:S(2)}) %collective-permute-start.10) | collective-permute-done | bytes 196640 | tf_op jit(solution)/shard_map/ppermute | solution.py:29
  32.1 0.0 collective-permute-start.12
  32.1 0.0 collective-permute-done.7.refs_11_
  32.1 0.5 collective-permute-start.9
  32.6 3.3 %collective-permute-done.11.refs_13_ = bf16[3,256,128]{2,1,0:T(8,128)(2,1)S(1)} collective-permute-done((bf16[3,256,128]{2,1,0:T(8,128)(2,1)S(1)}, bf16[3,256,128]{2,1,0:T(8,128)(2,1)S(1)}, u32[]{:S(2)}, u32[]{:S(2)}) %collective-permute-start.11) | collective-permute-done | bytes 196640 | tf_op jit(solution)/shard_map/ppermute | solution.py:29
  36.0 0.0 copy-done
  36.0 0.0 collective-permute-start.8
  36.0 0.0 collective-permute-done.12.refs_14_
  36.0 0.5 collective-permute-start.13
  36.5 1.5 %collective-permute-done.13.refs_15_ = bf16[3,256,128]{2,1,0:T(8,128)(2,1)S(1)} collective-permute-done((bf16[3,256,128]{2,1,0:T(8,128)(2,1)S(1)}, bf16[3,256,128]{2,1,0:T(8,128)(2,1)S(1)}, u32[]{:S(2)}, u32[]{:S(2)}) %collective-permute-start.13) | collective-permute-done | bytes 196640 | tf_op jit(solution)/shard_map/ppermute | solution.py:29
  38.0 0.1 collective-permute-start
  38.1 1.2 %collective-permute-done.14.refs_20_ = bf16[3,512,128]{2,1,0:T(8,128)(2,1)S(1)} collective-permute-done((bf16[3,512,128]{2,1,0:T(8,128)(2,1)S(1)}, bf16[3,512,128]{2,1,0:T(8,128)(2,1)S(1)}, u32[]{:S(2)}, u32[]{:S(2)}) %collective-permute-start.14) | collective-permute-done | bytes 393248 | tf_op jit(solution)/shard_map/ppermute | solution.py:29
  39.4 0.0 collective-permute-done.9.refs_7_
  39.4 0.0 collective-permute-done.1.refs_2_
  39.4 0.0 collective-permute-done.8.refs_5_
  39.4 0.1 collective-permute-start.15
  39.4 1.2 %collective-permute-done.refs_1_ = bf16[1024,512]{1,0:T(8,128)(2,1)S(1)} collective-permute-done((bf16[1024,512]{1,0:T(8,128)(2,1)S(1)}, bf16[1024,512]{1,0:T(8,128)(2,1)S(1)}, u32[]{:S(2)}, u32[]{:S(2)}) %collective-permute-start) | collective-permute-done | bytes 1048608 | tf_op jit(solution)/shard_map/ppermute | solution.py:29
  40.6 1.5 %collective-permute-done.15.refs_3_ = bf16[1024,512]{1,0:T(8,128)(2,1)S(1)} collective-permute-done((bf16[1024,512]{1,0:T(8,128)(2,1)S(1)}, bf16[1024,512]{1,0:T(8,128)(2,1)S(1)}, u32[]{:S(2)}, u32[]{:S(2)}) %collective-permute-start.15) | collective-permute-done | bytes 1048608 | tf_op jit(solution)/shard_map/ppermute | solution.py:29
  42.1 0.0 copy-done.4
  42.1 7.4 %shard_map.56 = f32[2,4,128]{2,1,0:T(4,128)S(1)} custom-call(s32[4]{0:T(128)S(1)} %pad_add_fusion.where, s32[3,16]{1,0:T(4,128)S(1)} %bitcast.24, s32[16]{0:T(128)S(1)} %copy-done.4, bf16[1024,512]{1,0:T(8,128)(2,1)S(1)} %shard_map.55.refs_0_, bf16[1024,512]{1,0:T(8,128)(2,1)S(1)} %collective-permute-done.refs_1_, ...), custom_call_target="tpu_custom_call" | custom-call | tf_op jit(solution)/shard_map/pallas_call | solution.py:228
  49.5 0.1 collective-permute-start.16
  49.6 1.2 %collective-permute-done.16 = f32[2,4,128]{2,1,0:T(4,128)S(1)} collective-permute-done((f32[2,4,128]{2,1,0:T(4,128)S(1)}, f32[2,4,128]{2,1,0:T(4,128)S(1)}, u32[]{:S(2)}, u32[]{:S(2)}) %collective-permute-start.16) | collective-permute-done | bytes 4128 | tf_op jit(solution)/shard_map/ppermute | solution.py:29
  50.7 0.0 collective-permute-start.17
  50.7 2.1 %collective-permute-start.19 = (f32[4,128]{1,0:T(4,128)S(1)}, f32[4,128]{1,0:T(4,128)S(1)}, u32[]{:S(2)}, u32[]{:S(2)}) collective-permute-start(f32[4,128]{1,0:T(4,128)S(1)} %get-tuple-element.18), channel_id=1, source_target_pairs={{0,6},{1,7},{2,4},{3,5},{4,2},{5,3},{6,0},{7,1},{8,14},{9,15},{10,... | collective-permute-start | bytes 6152 | tf_op jit(solution)/shard_map/ppermute | solution.py:29
  52.9 1.4 %collective-permute-start.18 = (f32[4,128]{1,0:T(4,128)S(1)}, f32[4,128]{1,0:T(4,128)S(1)}, u32[]{:S(2)}, u32[]{:S(2)}) collective-permute-start(f32[4,128]{1,0:T(4,128)S(1)} %get-tuple-element.18), channel_id=1, source_target_pairs={{0,4},{4,0},{8,12},{12,8},{1,5},{5,1},{9,13},{13,9},{2,6},{6,2},{1... | collective-permute-start | bytes 6152 | tf_op jit(solution)/shard_map/ppermute | solution.py:29
  54.2 0.1 collective-permute-done.17
  54.3 1.0 %collective-permute-done.19 = f32[4,128]{1,0:T(4,128)S(1)} collective-permute-done((f32[4,128]{1,0:T(4,128)S(1)}, f32[4,128]{1,0:T(4,128)S(1)}, u32[]{:S(2)}, u32[]{:S(2)}) %collective-permute-start.19) | collective-permute-done | bytes 2080 | tf_op jit(solution)/shard_map/ppermute | solution.py:29
  55.3 1.1 %collective-permute-done.18 = f32[4,128]{1,0:T(4,128)S(1)} collective-permute-done((f32[4,128]{1,0:T(4,128)S(1)}, f32[4,128]{1,0:T(4,128)S(1)}, u32[]{:S(2)}, u32[]{:S(2)}) %collective-permute-start.18) | collective-permute-done | bytes 2080 | tf_op jit(solution)/shard_map/ppermute | solution.py:29
  56.4 0.6 %dynamic-slice_reduce_fusion = f32[]{:T(128)} fusion(f32[4,128]{1,0:T(4,128)S(1)} %add_add_fusion, s32[]{:T(128)S(6)} %select_n.7), kind=kLoop, calls=%fused_computation.5 | loop fusion | flops 127 | bytes 520 | tf_op jit(solution)/shard_map/reduce_sum | solution.py:247
  (10 shorter events, 0.0 us)
Async XLA Ops:
  0.0 36.0 %copy-start = (bf16[512,1,3,128]{3,0,2,1:T(8,128)(2,1)S(1)}, bf16[512,1,3,128]{3,0,2,1:T(8,128)(2,1)}, u32[]{:S(2)}) copy-start(bf16[512,1,3,128]{3,0,2,1:T(8,128)(2,1)} %param.5) | copy-start | bytes 1179652
  0.0 42.1 %copy-start.4 = (s32[16]{0:T(128)S(1)}, s32[16]{0:T(128)}, u32[]{:S(2)}) copy-start(s32[16]{0:T(128)} %pcount.1) | copy-start | bytes 196
  0.0 42.1 %copy-start.3 = (s32[16,3]{0,1:T(4,128)S(1)}, s32[16,3]{0,1:T(4,128)}, u32[]{:S(2)}) copy-start(s32[16,3]{0,1:T(4,128)} %param.8) | copy-start | bytes 580
  1.0 11.1 %collective-permute-start.2 = (bf16[3,256,128]{2,1,0:T(8,128)(2,1)S(1)}, bf16[3,256,128]{2,1,0:T(8,128)(2,1)S(1)}, u32[]{:S(2)}, u32[]{:S(2)}) collective-permute-start(bf16[3,256,128]{2,1,0:T(8,128)(2,1)S(1)} %dynamic-slice_bitcast_fusion), channel_id=1, source_target_pairs={{0,2},{1,3},{2,0},{3,1},{4,6},{5,7},{6,4},{7,5},{8,10},{9,11},{10,... | collective-permute-start | bytes 589832 | tf_op jit(solution)/shard_map/ppermute | solution.py:29
  4.0 20.2 %collective-permute-start.5 = (bf16[3,512,128]{2,1,0:T(8,128)(2,1)}, bf16[3,512,128]{2,1,0:T(8,128)(2,1)S(1)}, u32[]{:S(2)}, u32[]{:S(2)}) collective-permute-start(bf16[3,512,128]{2,1,0:T(8,128)(2,1)} %bitcast.19), channel_id=1, source_target_pairs={{0,8},{4,12},{8,0},{12,4},{16,28},{20,24},{24,20},{28,16},{1,9},{5... | collective-permute-start | bytes 1179656 | tf_op jit(solution)/shard_map/ppermute | solution.py:29
  6.6 17.8 %collective-permute-start.4 = (bf16[3,512,128]{2,1,0:T(8,128)(2,1)}, bf16[3,512,128]{2,1,0:T(8,128)(2,1)S(1)}, u32[]{:S(2)}, u32[]{:S(2)}) collective-permute-start(bf16[3,512,128]{2,1,0:T(8,128)(2,1)} %bitcast.20), channel_id=1, source_target_pairs={{0,4},{4,0},{8,12},{12,8},{1,5},{5,1},{9,13},{13,9},{2,6},{6,2},{1... | collective-permute-start | bytes 1179656 | tf_op jit(solution)/shard_map/ppermute | solution.py:29
  8.3 1.6 %copy-start.1 = (bf16[512,2048]{1,0:T(8,128)(2,1)S(1)}, bf16[512,2048]{1,0:T(8,128)(2,1)}, u32[]{:S(2)}) copy-start(bf16[512,2048]{1,0:T(8,128)(2,1)} %virt_ref) | copy-start | bytes 6291460
  9.9 32.3 %copy-start.2 = (bf16[2048,512]{1,0:T(8,128)(2,1)S(1)}, bf16[2048,512]{1,0:T(8,128)(2,1)}, u32[]{:S(2)}) copy-start(bf16[2048,512]{1,0:T(8,128)(2,1)} %refs_16_.1) | copy-start | bytes 6291460
  11.5 27.8 %collective-permute-start.1 = (bf16[1024,512]{1,0:T(8,128)(2,1)S(1)}, bf16[1024,512]{1,0:T(8,128)(2,1)S(1)}, u32[]{:S(2)}, u32[]{:S(2)}) collective-permute-start(bf16[1024,512]{1,0:T(8,128)(2,1)S(1)} %shard_map.55.refs_0_), channel_id=1, source_target_pairs={{0,2},{1,3},{2,0},{3,1},{4,6},{5,7},{6,4},{7,5},{8,10},{9,11},{10,... | collective-permute-start | bytes 3145736 | tf_op jit(solution)/shard_map/ppermute | solution.py:29
  12.1 5.7 %collective-permute-start.3 = (bf16[3,256,128]{2,1,0:T(8,128)(2,1)S(1)}, bf16[3,256,128]{2,1,0:T(8,128)(2,1)S(1)}, u32[]{:S(2)}, u32[]{:S(2)}) collective-permute-start(bf16[3,256,128]{2,1,0:T(8,128)(2,1)S(1)} %collective-permute-done.2.refs_8_), channel_id=1, source_target_pairs={{0,16},{16,0},{1,17},{17,1},{2,18},{18,2},{3,19},{19,3},{4,20},{20... | collective-permute-start | bytes 589832 | tf_op jit(solution)/shard_map/ppermute | solution.py:29
  24.4 1.4 %collective-permute-start.6 = (bf16[3,256,128]{2,1,0:T(8,128)(2,1)S(1)}, bf16[3,256,128]{2,1,0:T(8,128)(2,1)S(1)}, u32[]{:S(2)}, u32[]{:S(2)}) collective-permute-start(bf16[3,256,128]{2,1,0:T(8,128)(2,1)S(1)} %collective-permute-done.2.refs_8_), channel_id=1, source_target_pairs={{0,1},{1,0},{2,3},{3,2},{4,5},{5,4},{6,7},{7,6},{8,9},{9,8},{10,11... | collective-permute-start | bytes 589832 | tf_op jit(solution)/shard_map/ppermute | solution.py:29
  24.4 7.7 %collective-permute-start.10 = (bf16[3,256,128]{2,1,0:T(8,128)(2,1)S(1)}, bf16[3,256,128]{2,1,0:T(8,128)(2,1)S(1)}, u32[]{:S(2)}, u32[]{:S(2)}) collective-permute-start(bf16[3,256,128]{2,1,0:T(8,128)(2,1)S(1)} %collective-permute-done.2.refs_8_), channel_id=1, source_target_pairs={{0,4},{4,0},{8,12},{12,8},{1,5},{5,1},{9,13},{13,9},{2,6},{6,2},{1... | collective-permute-start | bytes 589832 | tf_op jit(solution)/shard_map/ppermute | solution.py:29
  25.9 6.3 %collective-permute-start.7 = (bf16[3,256,128]{2,1,0:T(8,128)(2,1)S(1)}, bf16[3,256,128]{2,1,0:T(8,128)(2,1)S(1)}, u32[]{:S(2)}, u32[]{:S(2)}) collective-permute-start(bf16[3,256,128]{2,1,0:T(8,128)(2,1)S(1)} %collective-permute-done.3.refs_9_), channel_id=1, source_target_pairs={{0,1},{1,0},{2,3},{3,2},{4,5},{5,4},{6,7},{7,6},{8,9},{9,8},{10,11... | collective-permute-start | bytes 589832 | tf_op jit(solution)/shard_map/ppermute | solution.py:29
  26.1 9.9 %collective-permute-start.11 = (bf16[3,256,128]{2,1,0:T(8,128)(2,1)S(1)}, bf16[3,256,128]{2,1,0:T(8,128)(2,1)S(1)}, u32[]{:S(2)}, u32[]{:S(2)}) collective-permute-start(bf16[3,256,128]{2,1,0:T(8,128)(2,1)S(1)} %collective-permute-done.3.refs_9_), channel_id=1, source_target_pairs={{0,4},{4,0},{8,12},{12,8},{1,5},{5,1},{9,13},{13,9},{2,6},{6,2},{1... | collective-permute-start | bytes 589832 | tf_op jit(solution)/shard_map/ppermute | solution.py:29
  27.5 11.9 %collective-permute-start.14 = (bf16[3,512,128]{2,1,0:T(8,128)(2,1)S(1)}, bf16[3,512,128]{2,1,0:T(8,128)(2,1)S(1)}, u32[]{:S(2)}, u32[]{:S(2)}) collective-permute-start(bf16[3,512,128]{2,1,0:T(8,128)(2,1)S(1)} %collective-permute-done.5.refs_19_), channel_id=1, source_target_pairs={{0,16},{16,0},{1,17},{17,1},{2,18},{18,2},{3,19},{19,3},{4,20},{20... | collective-permute-start | bytes 1179656 | tf_op jit(solution)/shard_map/ppermute | solution.py:29
  32.1 3.8 %collective-permute-start.12 = (bf16[3,256,128]{2,1,0:T(8,128)(2,1)S(1)}, bf16[3,256,128]{2,1,0:T(8,128)(2,1)S(1)}, u32[]{:S(2)}, u32[]{:S(2)}) collective-permute-start(bf16[3,256,128]{2,1,0:T(8,128)(2,1)S(1)} %collective-permute-done.10.refs_12_), channel_id=1, source_target_pairs={{0,1},{1,0},{2,3},{3,2},{4,5},{5,4},{6,7},{7,6},{8,9},{9,8},{10,11... | collective-permute-start | bytes 589832 | tf_op jit(solution)/shard_map/ppermute | solution.py:29
  32.1 7.2 %collective-permute-start.9 = (bf16[3,512,128]{2,1,0:T(8,128)(2,1)S(1)}, bf16[3,512,128]{2,1,0:T(8,128)(2,1)S(1)}, u32[]{:S(2)}, u32[]{:S(2)}) collective-permute-start(bf16[3,512,128]{2,1,0:T(8,128)(2,1)S(1)} %collective-permute-done.4.refs_6_.refs_18_), channel_id=1, source_target_pairs={{0,1},{1,0},{2,3},{3,2},{4,5},{5,4},{6,7},{7,6},{8,9},{9,8},{10,11... | collective-permute-start | bytes 1179656 | tf_op jit(solution)/shard_map/ppermute | solution.py:29
  36.0 3.4 %collective-permute-start.8 = (bf16[3,512,128]{2,1,0:T(8,128)(2,1)S(1)}, bf16[3,512,128]{2,1,0:T(8,128)(2,1)S(1)}, u32[]{:S(2)}, u32[]{:S(2)}) collective-permute-start(bf16[3,512,128]{2,1,0:T(8,128)(2,1)S(1)} %bitcast.21), channel_id=1, source_target_pairs={{0,1},{1,0},{2,3},{3,2},{4,5},{5,4},{6,7},{7,6},{8,9},{9,8},{10,11... | collective-permute-start | bytes 1179656 | tf_op jit(solution)/shard_map/ppermute | solution.py:29
  36.0 2.0 %collective-permute-start.13 = (bf16[3,256,128]{2,1,0:T(8,128)(2,1)S(1)}, bf16[3,256,128]{2,1,0:T(8,128)(2,1)S(1)}, u32[]{:S(2)}, u32[]{:S(2)}) collective-permute-start(bf16[3,256,128]{2,1,0:T(8,128)(2,1)S(1)} %collective-permute-done.11.refs_13_), channel_id=1, source_target_pairs={{0,1},{1,0},{2,3},{3,2},{4,5},{5,4},{6,7},{7,6},{8,9},{9,8},{10,11... | collective-permute-start | bytes 589832 | tf_op jit(solution)/shard_map/ppermute | solution.py:29
  38.0 2.7 %collective-permute-start = (bf16[1024,512]{1,0:T(8,128)(2,1)S(1)}, bf16[1024,512]{1,0:T(8,128)(2,1)S(1)}, u32[]{:S(2)}, u32[]{:S(2)}) collective-permute-start(bf16[1024,512]{1,0:T(8,128)(2,1)S(1)} %shard_map.55.refs_0_), channel_id=1, source_target_pairs={{0,1},{1,0},{2,3},{3,2},{4,5},{5,4},{6,7},{7,6},{8,9},{9,8},{10,11... | collective-permute-start | bytes 3145736 | tf_op jit(solution)/shard_map/ppermute | solution.py:29
  39.4 2.8 %collective-permute-start.15 = (bf16[1024,512]{1,0:T(8,128)(2,1)S(1)}, bf16[1024,512]{1,0:T(8,128)(2,1)S(1)}, u32[]{:S(2)}, u32[]{:S(2)}) collective-permute-start(bf16[1024,512]{1,0:T(8,128)(2,1)S(1)} %collective-permute-done.1.refs_2_), channel_id=1, source_target_pairs={{0,1},{1,0},{2,3},{3,2},{4,5},{5,4},{6,7},{7,6},{8,9},{9,8},{10,11... | collective-permute-start | bytes 3145736 | tf_op jit(solution)/shard_map/ppermute | solution.py:29
  49.5 1.2 %collective-permute-start.16 = (f32[2,4,128]{2,1,0:T(4,128)S(1)}, f32[2,4,128]{2,1,0:T(4,128)S(1)}, u32[]{:S(2)}, u32[]{:S(2)}) collective-permute-start(f32[2,4,128]{2,1,0:T(4,128)S(1)} %shard_map.56), channel_id=1, source_target_pairs={{0,1},{1,0},{2,3},{3,2},{4,5},{5,4},{6,7},{7,6},{8,9},{9,8},{10,11... | collective-permute-start | bytes 12296 | tf_op jit(solution)/shard_map/ppermute | solution.py:29
  50.7 3.6 %collective-permute-start.17 = (f32[4,128]{1,0:T(4,128)S(1)}, f32[4,128]{1,0:T(4,128)S(1)}, u32[]{:S(2)}, u32[]{:S(2)}) collective-permute-start(f32[4,128]{1,0:T(4,128)S(1)} %get-tuple-element.17), channel_id=1, source_target_pairs={{0,2},{1,3},{2,0},{3,1},{4,6},{5,7},{6,4},{7,5},{8,10},{9,11},{10,... | collective-permute-start | bytes 6152 | tf_op jit(solution)/shard_map/ppermute | solution.py:29
  50.7 4.5 %collective-permute-start.19 = (f32[4,128]{1,0:T(4,128)S(1)}, f32[4,128]{1,0:T(4,128)S(1)}, u32[]{:S(2)}, u32[]{:S(2)}) collective-permute-start(f32[4,128]{1,0:T(4,128)S(1)} %get-tuple-element.18), channel_id=1, source_target_pairs={{0,6},{1,7},{2,4},{3,5},{4,2},{5,3},{6,0},{7,1},{8,14},{9,15},{10,... | collective-permute-start | bytes 6152 | tf_op jit(solution)/shard_map/ppermute | solution.py:29
  52.9 3.6 %collective-permute-start.18 = (f32[4,128]{1,0:T(4,128)S(1)}, f32[4,128]{1,0:T(4,128)S(1)}, u32[]{:S(2)}, u32[]{:S(2)}) collective-permute-start(f32[4,128]{1,0:T(4,128)S(1)} %get-tuple-element.18), channel_id=1, source_target_pairs={{0,4},{4,0},{8,12},{12,8},{1,5},{5,1},{9,13},{13,9},{2,6},{6,2},{1... | collective-permute-start | bytes 6152 | tf_op jit(solution)/shard_map/ppermute | solution.py:29

commit v8 on v7

--- a/solution.py
+++ b/solution.py
@@ -48,7 +48,7 @@
 def contract(n_centers, where, plist, pcount, *refs):
     v_refs, m_refs, f_refs, occ_ref = refs[0:4], refs[4:8], refs[8:16], refs[16]
     c_refs = refs[17 : 17 + n_centers]
-    out_ref, prod, acc, listed, place = refs[17 + n_centers :]
+    out_ref, prod, acc, listed, place, queue = refs[17 + n_centers :]
     own, parity, plane, aux_at = where[0], where[1], where[2], where[3]
     n_q = acc.shape[1]
     rows = v_refs[0].shape[1]
@@ -140,10 +140,13 @@
 
     lax.fori_loop(0, (count + 1) >> 1, one_group, 0)
 
-    def tile(at, span, k):
+    def tile(at, b, k, weight=None):
+        span = pl.ds(pl.multiple_of(b * BS, BS), BS)
         left = jnp.dot(prod[at], occ_ref[:, span], preferred_element_type=jnp.float32)
         left = left.astype(jnp.bfloat16).astype(jnp.float32)
         left = [left[s * BS : (s + 1) * BS, :].T for s in range(2)]
+        if weight is not None:
+            left = [part * weight for part in left]
 
         def add(q, center):
             center = center.astype(jnp.float32)
@@ -157,13 +160,28 @@
                 add(aux_at ^ step, c_ref[k, span, :])
 
     for i in range(blocks_here // 2):
-        tile(i, pl.ds(pl.multiple_of((2 * i + parity) * BS, BS), BS), 0)
+        tile(i, 2 * i + parity, 0)
+
+    tiles = jnp.int32(0)
     for k in range(1, KN):
         for b in range(blocks_here):
-
-            @pl.when(used(b, k))
-            def _(b=b, k=k):
-                tile(place[column(b, k)], slice(b * BS, (b + 1) * BS), k)
+            use = used(b, k)
+
+            @pl.when(use)
+            def _(b=b, k=k, tiles=tiles):
+                queue[tiles] = k * blocks_here + b
+
+            tiles = tiles + use.astype(jnp.int32)
+
+    def two_tiles(i, carry):
+        one, two = queue[2 * i], queue[jnp.minimum(2 * i + 1, tiles - 1)]
+        weight = (2 * i + 1 < tiles).astype(jnp.float32)
+        for code, scale in ((one, None), (two, weight)):
+            b, k = code % blocks_here, code // blocks_here
+            tile(place[column(b, k)], b, k, scale)
+        return carry
+
+    lax.fori_loop(0, (tiles + 1) >> 1, two_tiles, 0)
 
     for s in range(2):
         out_ref[s] = acc[s].sum(axis=1)
@@ -215,14 +233,15 @@
         early.append(rest_a)
     else:
         all_centers = [lax.all_gather(centers, "aux", axis=0)]
-    pair_x, pair_y = pair(after(far_x, far_y)), pair(far_y)
+    pair_x, pair_y = pair(far_x), pair(far_y)
 
     far_x_core = core(after(far_x, far_y, *early))
     far_y_core = core(after(far_y, far_x_core))
-    centers_core = core(after(centers, far_y_core))
+    pair_x_core, pair_y_core = core(pair_x), core(pair_y)
+    centers_core = core(after(centers, far_y_core, pair_x_core))
     other_core = core(other)
     m_parts = [centers, centers_core, other, other_core, far_x, far_y, far_x_core, far_y_core]
-    m_parts += [pair_x, pair_y, core(pair_x), core(pair_y)]
+    m_parts += [pair_x, pair_y, pair_x_core, pair_y_core]
     v_parts = [mine, core(mine), v_across]
     v_parts.append(core(after(v_across, *m_parts[1:], all_centers[-1])))
     sums = pl.pallas_call(
@@ -235,6 +254,7 @@
             pltpu.VMEM((2, aux, 8, BS), jnp.float32),
             pltpu.SMEM((n_blocks,), jnp.int32),
             pltpu.SMEM((n_blocks,), jnp.int32),
+            pltpu.SMEM((rows // BS * KN,), jnp.int32),
         ],
         compiler_params=pltpu.CompilerParams(vmem_limit_bytes=(24 if aux == 4 else 48) * MIB),
     )(where, partner_list.T, partner_count, *v_parts, *m_parts, occ_density, *all_centers)

time: 59.4 us -> 62.3 us (1.049)
  starting transfers between devices: 19.1 us -> 22.2 us
  Pallas kernels: 9 us -> 6.03 us
  waiting for transfers between devices: 25.6 us -> 28.4 us
    ppermute x20, starting transfers between devices: 19.1 us -> 22.2 us  [swap(): return lax.ppermute(x, axes, perm)]
    pallas_call x1, Pallas kernels: 7.36 us -> 4.39 us  [on_device(): pl.pallas_call(functools.partial(contract, len(all_centers)), out_shape=j...]
    ppermute x20, waiting for transfers between devices: 25.6 us -> 28.4 us  [swap(): return lax.ppermute(x, axes, perm)]
  transfers between devices with their start and end apart: 20 -> 20, of which waited for: 13 -> 11; matrix products, arithmetic and copies ran while one was open for 0% -> 0% of each run, Pallas kernels for 3% -> 3%
where the time goes in v8:
time: 62.3 us; the launch traced here: 61.2 us
  waiting for transfers between devices  28.4 us (46%)
  starting transfers between devices  22.2 us (36%)
  Pallas kernels  6.03 us (10%)
  local copies, waits for them, and re-layouts  2.62 us (4%)
  between operations  1.24 us (2%)
  other arithmetic  0.69 us (1%)
    ppermute x20, waiting for transfers between devices, swap(): return lax.ppermute(x, axes, perm)  28.4 us
    ppermute x20, starting transfers between devices, swap(): return lax.ppermute(x, axes, perm)  22.2 us
    pallas_call x1, Pallas kernels, on_device(): pl.pallas_call(functools.partial(contract, len(all_centers)), out_shape=j...  4.39 us
    pallas_call x1, Pallas kernels, on_device(): pl.pallas_call(functools.partial(select, n_blocks), out_shape=jax.ShapeDt...  1.64 us
    unnamed x10, local copies, waits for them, and re-layouts  1.61 us
  transfers between devices with their start and end apart: 20, of which 11 were waited for; matrix products, arithmetic and copies ran while one was open for 0% of the time, Pallas kernels for 3%

profile of v8, /device:TPU:0, one launch (start us, length us, event | category | flops | bytes accessed | tf_op | source)
XLA Modules:
  0.0 61.2 jit_solution(12839671201465832856)
XLA Ops:
  0.0 1.0 %dynamic-slice_bitcast_fusion = bf16[3,256,128]{2,1,0:T(8,128)(2,1)S(1)} fusion(bf16[512,1,3,128]{3,0,2,1:T(8,128)(2,1)} %param.5, s32[]{:T(128)S(6)} %select_n.6), kind=kLoop, calls=%fused_computation | loop fusion | bytes 393220 | tf_op jit(solution)/shard_map/dynamic_slice | solution.py:212
  1.0 3.0 %collective-permute-start.2 = (bf16[3,256,128]{2,1,0:T(8,128)(2,1)S(1)}, bf16[3,256,128]{2,1,0:T(8,128)(2,1)S(1)}, u32[]{:S(2)}, u32[]{:S(2)}) collective-permute-start(bf16[3,256,128]{2,1,0:T(8,128)(2,1)S(1)} %dynamic-slice_bitcast_fusion), channel_id=1, source_target_pairs={{0,2},{1,3},{2,0},{3,1},{4,6},{5,7},{6,4},{7,5},{8,10},{9,11},{10,... | collective-permute-start | bytes 589832 | tf_op jit(solution)/shard_map/ppermute | solution.py:29
  4.0 2.6 %collective-permute-start.5 = (bf16[3,512,128]{2,1,0:T(8,128)(2,1)}, bf16[3,512,128]{2,1,0:T(8,128)(2,1)S(1)}, u32[]{:S(2)}, u32[]{:S(2)}) collective-permute-start(bf16[3,512,128]{2,1,0:T(8,128)(2,1)} %bitcast.19), channel_id=1, source_target_pairs={{0,8},{4,12},{8,0},{12,4},{16,28},{20,24},{24,20},{28,16},{1,9},{5... | collective-permute-start | bytes 1179656 | tf_op jit(solution)/shard_map/ppermute | solution.py:29
  6.6 1.6 %collective-permute-start.4 = (bf16[3,512,128]{2,1,0:T(8,128)(2,1)}, bf16[3,512,128]{2,1,0:T(8,128)(2,1)S(1)}, u32[]{:S(2)}, u32[]{:S(2)}) collective-permute-start(bf16[3,512,128]{2,1,0:T(8,128)(2,1)} %bitcast.20), channel_id=1, source_target_pairs={{0,4},{4,0},{8,12},{12,8},{1,5},{5,1},{9,13},{13,9},{2,6},{6,2},{1... | collective-permute-start | bytes 1179656 | tf_op jit(solution)/shard_map/ppermute | solution.py:29
  8.2 0.1 pad_add_fusion.where
  8.3 1.6 %copy-done.1 = bf16[512,2048]{1,0:T(8,128)(2,1)S(1)} copy-done((bf16[512,2048]{1,0:T(8,128)(2,1)S(1)}, bf16[512,2048]{1,0:T(8,128)(2,1)}, u32[]{:S(2)}) %copy-start.1) | copy-done | bytes 2097176
  9.9 1.6 %shard_map.55.refs_0_ = bf16[1024,512]{1,0:T(8,128)(2,1)S(1)} custom-call(s32[4]{0:T(128)S(1)} %pad_add_fusion.where, bf16[512,2048]{1,0:T(8,128)(2,1)S(1)} %copy-done.1), custom_call_target="tpu_custom_call" | custom-call | tf_op jit(solution)/shard_map/pallas_call | solution.py:215
  11.5 0.6 collective-permute-start.1
  12.1 0.0 collective-permute-done.2.refs_8_
  12.1 1.0 %collective-permute-start.3 = (bf16[3,256,128]{2,1,0:T(8,128)(2,1)S(1)}, bf16[3,256,128]{2,1,0:T(8,128)(2,1)S(1)}, u32[]{:S(2)}, u32[]{:S(2)}) collective-permute-start(bf16[3,256,128]{2,1,0:T(8,128)(2,1)S(1)} %collective-permute-done.2.refs_8_), channel_id=1, source_target_pairs={{0,16},{16,0},{1,17},{17,1},{2,18},{18,2},{3,19},{19,3},{4,20},{20... | collective-permute-start | bytes 589832 | tf_op jit(solution)/shard_map/ppermute | solution.py:29
  13.1 2.0 %collective-permute-start.8 = (bf16[3,256,128]{2,1,0:T(8,128)(2,1)S(1)}, bf16[3,256,128]{2,1,0:T(8,128)(2,1)S(1)}, u32[]{:S(2)}, u32[]{:S(2)}) collective-permute-start(bf16[3,256,128]{2,1,0:T(8,128)(2,1)S(1)} %collective-permute-done.2.refs_8_), channel_id=1, source_target_pairs={{0,4},{4,0},{8,12},{12,8},{1,5},{5,1},{9,13},{13,9},{2,6},{6,2},{1... | collective-permute-start | bytes 589832 | tf_op jit(solution)/shard_map/ppermute | solution.py:29
  15.1 2.7 %collective-permute-done.3.refs_9_ = bf16[3,256,128]{2,1,0:T(8,128)(2,1)S(1)} collective-permute-done((bf16[3,256,128]{2,1,0:T(8,128)(2,1)S(1)}, bf16[3,256,128]{2,1,0:T(8,128)(2,1)S(1)}, u32[]{:S(2)}, u32[]{:S(2)}) %collective-permute-start.3) | collective-permute-done | bytes 196640 | tf_op jit(solution)/shard_map/ppermute | solution.py:29
  17.8 6.5 %collective-permute-done.5.refs_19_ = bf16[3,512,128]{2,1,0:T(8,128)(2,1)S(1)} collective-permute-done((bf16[3,512,128]{2,1,0:T(8,128)(2,1)}, bf16[3,512,128]{2,1,0:T(8,128)(2,1)S(1)}, u32[]{:S(2)}, u32[]{:S(2)}) %collective-permute-start.5) | collective-permute-done | bytes 393248 | tf_op jit(solution)/shard_map/ppermute | solution.py:29
  24.2 2.0 %collective-permute-done.4.refs_6_.refs_18_ = bf16[3,512,128]{2,1,0:T(8,128)(2,1)S(1)} collective-permute-done((bf16[3,512,128]{2,1,0:T(8,128)(2,1)}, bf16[3,512,128]{2,1,0:T(8,128)(2,1)S(1)}, u32[]{:S(2)}, u32[]{:S(2)}) %collective-permute-start.4) | collective-permute-done | bytes 393248 | tf_op jit(solution)/shard_map/ppermute | solution.py:29
  26.2 0.0 collective-permute-start.6
  26.2 2.4 %collective-permute-done.8.refs_12_ = bf16[3,256,128]{2,1,0:T(8,128)(2,1)S(1)} collective-permute-done((bf16[3,256,128]{2,1,0:T(8,128)(2,1)S(1)}, bf16[3,256,128]{2,1,0:T(8,128)(2,1)S(1)}, u32[]{:S(2)}, u32[]{:S(2)}) %collective-permute-start.8) | collective-permute-done | bytes 196640 | tf_op jit(solution)/shard_map/ppermute | solution.py:29
  28.6 0.0 collective-permute-start.9
  28.6 0.0 collective-permute-done.6.refs_10_
  28.6 0.5 collective-permute-start.7
  29.2 1.4 %collective-permute-start.12 = (bf16[3,256,128]{2,1,0:T(8,128)(2,1)S(1)}, bf16[3,256,128]{2,1,0:T(8,128)(2,1)S(1)}, u32[]{:S(2)}, u32[]{:S(2)}) collective-permute-start(bf16[3,256,128]{2,1,0:T(8,128)(2,1)S(1)} %collective-permute-done.3.refs_9_), channel_id=1, source_target_pairs={{0,4},{4,0},{8,12},{12,8},{1,5},{5,1},{9,13},{13,9},{2,6},{6,2},{1... | collective-permute-start | bytes 589832 | tf_op jit(solution)/shard_map/ppermute | solution.py:29
  30.6 2.5 %collective-permute-start.14 = (bf16[3,512,128]{2,1,0:T(8,128)(2,1)S(1)}, bf16[3,512,128]{2,1,0:T(8,128)(2,1)S(1)}, u32[]{:S(2)}, u32[]{:S(2)}) collective-permute-start(bf16[3,512,128]{2,1,0:T(8,128)(2,1)S(1)} %collective-permute-done.5.refs_19_), channel_id=1, source_target_pairs={{0,16},{16,0},{1,17},{17,1},{2,18},{18,2},{3,19},{19,3},{4,20},{20... | collective-permute-start | bytes 1179656 | tf_op jit(solution)/shard_map/ppermute | solution.py:29
  33.1 0.0 collective-permute-done.9.refs_14_
  33.1 0.0 collective-permute-start.11
  33.1 0.0 collective-permute-done.7.refs_11_
  33.1 0.0 copy-done
  33.2 0.5 collective-permute-start.10
  33.7 2.3 %collective-permute-done.12.refs_13_ = bf16[3,256,128]{2,1,0:T(8,128)(2,1)S(1)} collective-permute-done((bf16[3,256,128]{2,1,0:T(8,128)(2,1)S(1)}, bf16[3,256,128]{2,1,0:T(8,128)(2,1)S(1)}, u32[]{:S(2)}, u32[]{:S(2)}) %collective-permute-start.12) | collective-permute-done | bytes 196640 | tf_op jit(solution)/shard_map/ppermute | solution.py:29
  36.0 0.0 collective-permute-start.13
  36.0 1.4 %collective-permute-done.13.refs_15_ = bf16[3,256,128]{2,1,0:T(8,128)(2,1)S(1)} collective-permute-done((bf16[3,256,128]{2,1,0:T(8,128)(2,1)S(1)}, bf16[3,256,128]{2,1,0:T(8,128)(2,1)S(1)}, u32[]{:S(2)}, u32[]{:S(2)}) %collective-permute-start.13) | collective-permute-done | bytes 196640 | tf_op jit(solution)/shard_map/ppermute | solution.py:29
  37.4 0.1 collective-permute-start
  37.6 4.6 %collective-permute-done.14.refs_20_ = bf16[3,512,128]{2,1,0:T(8,128)(2,1)S(1)} collective-permute-done((bf16[3,512,128]{2,1,0:T(8,128)(2,1)S(1)}, bf16[3,512,128]{2,1,0:T(8,128)(2,1)S(1)}, u32[]{:S(2)}, u32[]{:S(2)}) %collective-permute-start.14) | collective-permute-done | bytes 393248 | tf_op jit(solution)/shard_map/ppermute | solution.py:29
  42.1 0.0 collective-permute-done.11.refs_7_
  42.1 0.0 collective-permute-done.1.refs_2_
  42.1 0.0 collective-permute-done.10.refs_5_
  42.1 0.1 collective-permute-start.15
  42.2 0.0 collective-permute-done.refs_1_
  42.2 2.6 %collective-permute-done.15.refs_3_ = bf16[1024,512]{1,0:T(8,128)(2,1)S(1)} collective-permute-done((bf16[1024,512]{1,0:T(8,128)(2,1)S(1)}, bf16[1024,512]{1,0:T(8,128)(2,1)S(1)}, u32[]{:S(2)}, u32[]{:S(2)}) %collective-permute-start.15) | collective-permute-done | bytes 1048608 | tf_op jit(solution)/shard_map/ppermute | solution.py:29
  44.9 0.0 copy-done.4
  44.9 4.4 %shard_map.56 = f32[2,4,128]{2,1,0:T(4,128)S(1)} custom-call(s32[4]{0:T(128)S(1)} %pad_add_fusion.where, s32[3,16]{1,0:T(4,128)S(1)} %bitcast.24, s32[16]{0:T(128)S(1)} %copy-done.4, bf16[1024,512]{1,0:T(8,128)(2,1)S(1)} %shard_map.55.refs_0_, bf16[1024,512]{1,0:T(8,128)(2,1)S(1)} %collective-permute-done.refs_1_, ...), custom_call_target="tpu_custom_call" | custom-call | tf_op jit(solution)/shard_map/pallas_call | solution.py:247
  49.3 2.3 %collective-permute-start.16 = (f32[2,4,128]{2,1,0:T(4,128)S(1)}, f32[2,4,128]{2,1,0:T(4,128)S(1)}, u32[]{:S(2)}, u32[]{:S(2)}) collective-permute-start(f32[2,4,128]{2,1,0:T(4,128)S(1)} %shard_map.56), channel_id=1, source_target_pairs={{0,1},{1,0},{2,3},{3,2},{4,5},{5,4},{6,7},{7,6},{8,9},{9,8},{10,11... | collective-permute-start | bytes 12296 | tf_op jit(solution)/shard_map/ppermute | solution.py:29
  51.5 0.8 %collective-permute-done.16 = f32[2,4,128]{2,1,0:T(4,128)S(1)} collective-permute-done((f32[2,4,128]{2,1,0:T(4,128)S(1)}, f32[2,4,128]{2,1,0:T(4,128)S(1)}, u32[]{:S(2)}, u32[]{:S(2)}) %collective-permute-start.16) | collective-permute-done | bytes 4128 | tf_op jit(solution)/shard_map/ppermute | solution.py:29
  52.4 0.8 %collective-permute-start.17 = (f32[4,128]{1,0:T(4,128)S(1)}, f32[4,128]{1,0:T(4,128)S(1)}, u32[]{:S(2)}, u32[]{:S(2)}) collective-permute-start(f32[4,128]{1,0:T(4,128)S(1)} %get-tuple-element.15), channel_id=1, source_target_pairs={{0,2},{1,3},{2,0},{3,1},{4,6},{5,7},{6,4},{7,5},{8,10},{9,11},{10,... | collective-permute-start | bytes 6152 | tf_op jit(solution)/shard_map/ppermute | solution.py:29
  53.1 2.8 %collective-permute-start.19 = (f32[4,128]{1,0:T(4,128)S(1)}, f32[4,128]{1,0:T(4,128)S(1)}, u32[]{:S(2)}, u32[]{:S(2)}) collective-permute-start(f32[4,128]{1,0:T(4,128)S(1)} %get-tuple-element.16), channel_id=1, source_target_pairs={{0,6},{1,7},{2,4},{3,5},{4,2},{5,3},{6,0},{7,1},{8,14},{9,15},{10,... | collective-permute-start | bytes 6152 | tf_op jit(solution)/shard_map/ppermute | solution.py:29
  55.9 0.5 collective-permute-start.18
  56.4 0.0 collective-permute-done.17
  56.4 1.2 %collective-permute-done.19 = f32[4,128]{1,0:T(4,128)S(1)} collective-permute-done((f32[4,128]{1,0:T(4,128)S(1)}, f32[4,128]{1,0:T(4,128)S(1)}, u32[]{:S(2)}, u32[]{:S(2)}) %collective-permute-start.19) | collective-permute-done | bytes 2080 | tf_op jit(solution)/shard_map/ppermute | solution.py:29
  57.6 1.9 %collective-permute-done.18 = f32[4,128]{1,0:T(4,128)S(1)} collective-permute-done((f32[4,128]{1,0:T(4,128)S(1)}, f32[4,128]{1,0:T(4,128)S(1)}, u32[]{:S(2)}, u32[]{:S(2)}) %collective-permute-start.18) | collective-permute-done | bytes 2080 | tf_op jit(solution)/shard_map/ppermute | solution.py:29
  59.5 0.6 dynamic-slice_reduce_fusion
  (10 shorter events, 0.0 us)
Async XLA Ops:
  0.0 33.1 %copy-start = (bf16[512,1,3,128]{3,0,2,1:T(8,128)(2,1)S(1)}, bf16[512,1,3,128]{3,0,2,1:T(8,128)(2,1)}, u32[]{:S(2)}) copy-start(bf16[512,1,3,128]{3,0,2,1:T(8,128)(2,1)} %param.5) | copy-start | bytes 1179652
  0.0 44.9 %copy-start.4 = (s32[16]{0:T(128)S(1)}, s32[16]{0:T(128)}, u32[]{:S(2)}) copy-start(s32[16]{0:T(128)} %pcount.1) | copy-start | bytes 196
  0.0 44.9 %copy-start.3 = (s32[16,3]{0,1:T(4,128)S(1)}, s32[16,3]{0,1:T(4,128)}, u32[]{:S(2)}) copy-start(s32[16,3]{0,1:T(4,128)} %param.8) | copy-start | bytes 580
  1.0 11.1 %collective-permute-start.2 = (bf16[3,256,128]{2,1,0:T(8,128)(2,1)S(1)}, bf16[3,256,128]{2,1,0:T(8,128)(2,1)S(1)}, u32[]{:S(2)}, u32[]{:S(2)}) collective-permute-start(bf16[3,256,128]{2,1,0:T(8,128)(2,1)S(1)} %dynamic-slice_bitcast_fusion), channel_id=1, source_target_pairs={{0,2},{1,3},{2,0},{3,1},{4,6},{5,7},{6,4},{7,5},{8,10},{9,11},{10,... | collective-permute-start | bytes 589832 | tf_op jit(solution)/shard_map/ppermute | solution.py:29
  4.0 20.2 %collective-permute-start.5 = (bf16[3,512,128]{2,1,0:T(8,128)(2,1)}, bf16[3,512,128]{2,1,0:T(8,128)(2,1)S(1)}, u32[]{:S(2)}, u32[]{:S(2)}) collective-permute-start(bf16[3,512,128]{2,1,0:T(8,128)(2,1)} %bitcast.19), channel_id=1, source_target_pairs={{0,8},{4,12},{8,0},{12,4},{16,28},{20,24},{24,20},{28,16},{1,9},{5... | collective-permute-start | bytes 1179656 | tf_op jit(solution)/shard_map/ppermute | solution.py:29
  6.6 19.6 %collective-permute-start.4 = (bf16[3,512,128]{2,1,0:T(8,128)(2,1)}, bf16[3,512,128]{2,1,0:T(8,128)(2,1)S(1)}, u32[]{:S(2)}, u32[]{:S(2)}) collective-permute-start(bf16[3,512,128]{2,1,0:T(8,128)(2,1)} %bitcast.20), channel_id=1, source_target_pairs={{0,4},{4,0},{8,12},{12,8},{1,5},{5,1},{9,13},{13,9},{2,6},{6,2},{1... | collective-permute-start | bytes 1179656 | tf_op jit(solution)/shard_map/ppermute | solution.py:29
  8.3 1.6 %copy-start.1 = (bf16[512,2048]{1,0:T(8,128)(2,1)S(1)}, bf16[512,2048]{1,0:T(8,128)(2,1)}, u32[]{:S(2)}) copy-start(bf16[512,2048]{1,0:T(8,128)(2,1)} %virt_ref) | copy-start | bytes 6291460
  9.9 35.0 %copy-start.2 = (bf16[2048,512]{1,0:T(8,128)(2,1)S(1)}, bf16[2048,512]{1,0:T(8,128)(2,1)}, u32[]{:S(2)}) copy-start(bf16[2048,512]{1,0:T(8,128)(2,1)} %refs_16_.1) | copy-start | bytes 6291460
  11.5 30.6 %collective-permute-start.1 = (bf16[1024,512]{1,0:T(8,128)(2,1)S(1)}, bf16[1024,512]{1,0:T(8,128)(2,1)S(1)}, u32[]{:S(2)}, u32[]{:S(2)}) collective-permute-start(bf16[1024,512]{1,0:T(8,128)(2,1)S(1)} %shard_map.55.refs_0_), channel_id=1, source_target_pairs={{0,2},{1,3},{2,0},{3,1},{4,6},{5,7},{6,4},{7,5},{8,10},{9,11},{10,... | collective-permute-start | bytes 3145736 | tf_op jit(solution)/shard_map/ppermute | solution.py:29
  12.1 5.7 %collective-permute-start.3 = (bf16[3,256,128]{2,1,0:T(8,128)(2,1)S(1)}, bf16[3,256,128]{2,1,0:T(8,128)(2,1)S(1)}, u32[]{:S(2)}, u32[]{:S(2)}) collective-permute-start(bf16[3,256,128]{2,1,0:T(8,128)(2,1)S(1)} %collective-permute-done.2.refs_8_), channel_id=1, source_target_pairs={{0,16},{16,0},{1,17},{17,1},{2,18},{18,2},{3,19},{19,3},{4,20},{20... | collective-permute-start | bytes 589832 | tf_op jit(solution)/shard_map/ppermute | solution.py:29
  13.1 15.6 %collective-permute-start.8 = (bf16[3,256,128]{2,1,0:T(8,128)(2,1)S(1)}, bf16[3,256,128]{2,1,0:T(8,128)(2,1)S(1)}, u32[]{:S(2)}, u32[]{:S(2)}) collective-permute-start(bf16[3,256,128]{2,1,0:T(8,128)(2,1)S(1)} %collective-permute-done.2.refs_8_), channel_id=1, source_target_pairs={{0,4},{4,0},{8,12},{12,8},{1,5},{5,1},{9,13},{13,9},{2,6},{6,2},{1... | collective-permute-start | bytes 589832 | tf_op jit(solution)/shard_map/ppermute | solution.py:29
  26.2 2.5 %collective-permute-start.6 = (bf16[3,256,128]{2,1,0:T(8,128)(2,1)S(1)}, bf16[3,256,128]{2,1,0:T(8,128)(2,1)S(1)}, u32[]{:S(2)}, u32[]{:S(2)}) collective-permute-start(bf16[3,256,128]{2,1,0:T(8,128)(2,1)S(1)} %collective-permute-done.2.refs_8_), channel_id=1, source_target_pairs={{0,1},{1,0},{2,3},{3,2},{4,5},{5,4},{6,7},{7,6},{8,9},{9,8},{10,11... | collective-permute-start | bytes 589832 | tf_op jit(solution)/shard_map/ppermute | solution.py:29
  28.6 4.5 %collective-permute-start.9 = (bf16[3,256,128]{2,1,0:T(8,128)(2,1)S(1)}, bf16[3,256,128]{2,1,0:T(8,128)(2,1)S(1)}, u32[]{:S(2)}, u32[]{:S(2)}) collective-permute-start(bf16[3,256,128]{2,1,0:T(8,128)(2,1)S(1)} %collective-permute-done.8.refs_12_), channel_id=1, source_target_pairs={{0,1},{1,0},{2,3},{3,2},{4,5},{5,4},{6,7},{7,6},{8,9},{9,8},{10,11... | collective-permute-start | bytes 589832 | tf_op jit(solution)/shard_map/ppermute | solution.py:29
  28.6 4.5 %collective-permute-start.7 = (bf16[3,256,128]{2,1,0:T(8,128)(2,1)S(1)}, bf16[3,256,128]{2,1,0:T(8,128)(2,1)S(1)}, u32[]{:S(2)}, u32[]{:S(2)}) collective-permute-start(bf16[3,256,128]{2,1,0:T(8,128)(2,1)S(1)} %collective-permute-done.3.refs_9_), channel_id=1, source_target_pairs={{0,1},{1,0},{2,3},{3,2},{4,5},{5,4},{6,7},{7,6},{8,9},{9,8},{10,11... | collective-permute-start | bytes 589832 | tf_op jit(solution)/shard_map/ppermute | solution.py:29
  29.2 6.8 %collective-permute-start.12 = (bf16[3,256,128]{2,1,0:T(8,128)(2,1)S(1)}, bf16[3,256,128]{2,1,0:T(8,128)(2,1)S(1)}, u32[]{:S(2)}, u32[]{:S(2)}) collective-permute-start(bf16[3,256,128]{2,1,0:T(8,128)(2,1)S(1)} %collective-permute-done.3.refs_9_), channel_id=1, source_target_pairs={{0,4},{4,0},{8,12},{12,8},{1,5},{5,1},{9,13},{13,9},{2,6},{6,2},{1... | collective-permute-start | bytes 589832 | tf_op jit(solution)/shard_map/ppermute | solution.py:29
  30.6 11.5 %collective-permute-start.14 = (bf16[3,512,128]{2,1,0:T(8,128)(2,1)S(1)}, bf16[3,512,128]{2,1,0:T(8,128)(2,1)S(1)}, u32[]{:S(2)}, u32[]{:S(2)}) collective-permute-start(bf16[3,512,128]{2,1,0:T(8,128)(2,1)S(1)} %collective-permute-done.5.refs_19_), channel_id=1, source_target_pairs={{0,16},{16,0},{1,17},{17,1},{2,18},{18,2},{3,19},{19,3},{4,20},{20... | collective-permute-start | bytes 1179656 | tf_op jit(solution)/shard_map/ppermute | solution.py:29
  33.1 9.0 %collective-permute-start.11 = (bf16[3,512,128]{2,1,0:T(8,128)(2,1)S(1)}, bf16[3,512,128]{2,1,0:T(8,128)(2,1)S(1)}, u32[]{:S(2)}, u32[]{:S(2)}) collective-permute-start(bf16[3,512,128]{2,1,0:T(8,128)(2,1)S(1)} %collective-permute-done.4.refs_6_.refs_18_), channel_id=1, source_target_pairs={{0,1},{1,0},{2,3},{3,2},{4,5},{5,4},{6,7},{7,6},{8,9},{9,8},{10,11... | collective-permute-start | bytes 1179656 | tf_op jit(solution)/shard_map/ppermute | solution.py:29
  33.2 9.0 %collective-permute-start.10 = (bf16[3,512,128]{2,1,0:T(8,128)(2,1)S(1)}, bf16[3,512,128]{2,1,0:T(8,128)(2,1)S(1)}, u32[]{:S(2)}, u32[]{:S(2)}) collective-permute-start(bf16[3,512,128]{2,1,0:T(8,128)(2,1)S(1)} %bitcast.21), channel_id=1, source_target_pairs={{0,1},{1,0},{2,3},{3,2},{4,5},{5,4},{6,7},{7,6},{8,9},{9,8},{10,11... | collective-permute-start | bytes 1179656 | tf_op jit(solution)/shard_map/ppermute | solution.py:29
  36.0 1.4 %collective-permute-start.13 = (bf16[3,256,128]{2,1,0:T(8,128)(2,1)S(1)}, bf16[3,256,128]{2,1,0:T(8,128)(2,1)S(1)}, u32[]{:S(2)}, u32[]{:S(2)}) collective-permute-start(bf16[3,256,128]{2,1,0:T(8,128)(2,1)S(1)} %collective-permute-done.12.refs_13_), channel_id=1, source_target_pairs={{0,1},{1,0},{2,3},{3,2},{4,5},{5,4},{6,7},{7,6},{8,9},{9,8},{10,11... | collective-permute-start | bytes 589832 | tf_op jit(solution)/shard_map/ppermute | solution.py:29
  37.4 4.8 %collective-permute-start = (bf16[1024,512]{1,0:T(8,128)(2,1)S(1)}, bf16[1024,512]{1,0:T(8,128)(2,1)S(1)}, u32[]{:S(2)}, u32[]{:S(2)}) collective-permute-start(bf16[1024,512]{1,0:T(8,128)(2,1)S(1)} %shard_map.55.refs_0_), channel_id=1, source_target_pairs={{0,1},{1,0},{2,3},{3,2},{4,5},{5,4},{6,7},{7,6},{8,9},{9,8},{10,11... | collective-permute-start | bytes 3145736 | tf_op jit(solution)/shard_map/ppermute | solution.py:29
  42.1 2.7 %collective-permute-start.15 = (bf16[1024,512]{1,0:T(8,128)(2,1)S(1)}, bf16[1024,512]{1,0:T(8,128)(2,1)S(1)}, u32[]{:S(2)}, u32[]{:S(2)}) collective-permute-start(bf16[1024,512]{1,0:T(8,128)(2,1)S(1)} %collective-permute-done.1.refs_2_), channel_id=1, source_target_pairs={{0,1},{1,0},{2,3},{3,2},{4,5},{5,4},{6,7},{7,6},{8,9},{9,8},{10,11... | collective-permute-start | bytes 3145736 | tf_op jit(solution)/shard_map/ppermute | solution.py:29
  49.3 3.1 %collective-permute-start.16 = (f32[2,4,128]{2,1,0:T(4,128)S(1)}, f32[2,4,128]{2,1,0:T(4,128)S(1)}, u32[]{:S(2)}, u32[]{:S(2)}) collective-permute-start(f32[2,4,128]{2,1,0:T(4,128)S(1)} %shard_map.56), channel_id=1, source_target_pairs={{0,1},{1,0},{2,3},{3,2},{4,5},{5,4},{6,7},{7,6},{8,9},{9,8},{10,11... | collective-permute-start | bytes 12296 | tf_op jit(solution)/shard_map/ppermute | solution.py:29
  52.4 4.0 %collective-permute-start.17 = (f32[4,128]{1,0:T(4,128)S(1)}, f32[4,128]{1,0:T(4,128)S(1)}, u32[]{:S(2)}, u32[]{:S(2)}) collective-permute-start(f32[4,128]{1,0:T(4,128)S(1)} %get-tuple-element.15), channel_id=1, source_target_pairs={{0,2},{1,3},{2,0},{3,1},{4,6},{5,7},{6,4},{7,5},{8,10},{9,11},{10,... | collective-permute-start | bytes 6152 | tf_op jit(solution)/shard_map/ppermute | solution.py:29
  53.1 4.5 %collective-permute-start.19 = (f32[4,128]{1,0:T(4,128)S(1)}, f32[4,128]{1,0:T(4,128)S(1)}, u32[]{:S(2)}, u32[]{:S(2)}) collective-permute-start(f32[4,128]{1,0:T(4,128)S(1)} %get-tuple-element.16), channel_id=1, source_target_pairs={{0,6},{1,7},{2,4},{3,5},{4,2},{5,3},{6,0},{7,1},{8,14},{9,15},{10,... | collective-permute-start | bytes 6152 | tf_op jit(solution)/shard_map/ppermute | solution.py:29
  55.9 3.6 %collective-permute-start.18 = (f32[4,128]{1,0:T(4,128)S(1)}, f32[4,128]{1,0:T(4,128)S(1)}, u32[]{:S(2)}, u32[]{:S(2)}) collective-permute-start(f32[4,128]{1,0:T(4,128)S(1)} %get-tuple-element.16), channel_id=1, source_target_pairs={{0,4},{4,0},{8,12},{12,8},{1,5},{5,1},{9,13},{13,9},{2,6},{6,2},{1... | collective-permute-start | bytes 6152 | tf_op jit(solution)/shard_map/ppermute | solution.py:29
